TPU v7x, 32 devices: a whole 2x2x4 slice. The times are simulated.
32 devices in a mesh: dp: 2 (over x), context: 4 (over y, core), expert: 4 (over z).
Axes of the slice: x: 2, y: 2, z: 4, core: 2. Of those that a mesh axis runs over, the one named last changes fastest.
Arguments:
- tokens: bfloat16 [8, 1024, 1536], P(('dp', 'expert'), 'context'), may hold values from -6 to 6
- lengths: int32 [8], P(('dp', 'expert')), may hold values from 769 to 1024, as said below
- routes: int32 [8, 1024, 8], P(('dp', 'expert'), 'context'), may hold values from 0 to 31, all different within a row; in each aligned block of 256 rows (0 to 255, 256 to 511, ..., all dimensions but the last counted through in order) at most 96 rows name the same one
- gain_attn: bfloat16 [1536], P(('dp', 'context', 'expert')), may hold values from 0.5 to 1.5
- w_query: bfloat16 [1536, 1536], P(('dp', 'context', 'expert')), may hold values from -0.15625 to 0.15625
- key_weight: bfloat16 [1536, 512], P(('dp', 'context', 'expert')), may hold values from -0.15625 to 0.15625
- value_weight: bfloat16 [1536, 512], P(('dp', 'context', 'expert')), may hold values from -0.15625 to 0.15625
- w_out: bfloat16 [1536, 1536], P(('dp', 'context', 'expert')), may hold values from -1.25 to 1.25
- gain_ffn: bfloat16 [1536], P(('dp', 'context', 'expert')), may hold values from 0.5 to 1.5
- w_router: bfloat16 [1536, 32], P(('dp', 'context', 'expert')), may hold values from -0.078125 to 0.078125
- w_gate: bfloat16 [32, 1536, 512], P(('context', 'expert')), may hold values from -0.15625 to 0.15625
- w_up: bfloat16 [32, 1536, 512], P(('context', 'expert')), may hold values from -0.15625 to 0.15625
- w_down: bfloat16 [32, 512, 1536], P(('context', 'expert')), may hold values from -0.75 to 0.75
- cotangent: bfloat16 [8, 1024, 1536], P(('dp', 'expert'), 'context'), may hold values from -6 to 6
Outputs:
- block_out: bfloat16 [8, 1024, 1536], P(('dp', 'expert'), 'context')
- grad_tokens: float32 [8, 1024, 1536], P(('dp', 'expert'), 'context')
- grad_gain_attn: float32 [1536], P(('dp', 'context', 'expert'))
- grad_w_query: float32 [1536, 1536], P(('dp', 'context', 'expert'))
- grad_w_key: float32 [1536, 512], P(('dp', 'context', 'expert'))
- grad_w_value: float32 [1536, 512], P(('dp', 'context', 'expert'))
- grad_w_out: float32 [1536, 1536], P(('dp', 'context', 'expert'))
- grad_gain_ffn: float32 [1536], P(('dp', 'context', 'expert'))
- grad_w_router: float32 [1536, 32], P(('dp', 'context', 'expert'))
- grad_w_gate: float32 [32, 1536, 512], P(('context', 'expert'), 'dp')
- grad_w_up: float32 [32, 1536, 512], P(('context', 'expert'), 'dp')
- grad_w_down: float32 [32, 512, 1536], P(('context', 'expert'), 'dp')
Inputs may be any that keep to these rules, and one draw needn't show every extreme that they name: Within each aligned block of 256 positions of one slot, no expert is named by more than 96 of the block's routes. `lengths`: among the 1 consecutive slots that one index of dp and expert holds, one slot, drawn from the seed, is longer than 768; among the slots of one index of dp, one of these, drawn from the seed, has the full length 1024.
All inputs are finite; a program needn't handle non-finite values.
Results may differ from a plain program's by a relative error of at most 0.018.
Values may be sent and summed in bfloat16 or wider, within the bound.
A program may use at most 256 MiB of HBM per device.

v0:
```python
import math

import jax
import jax.numpy as jnp
from jax import lax
from jax.sharding import PartitionSpec as P

MODEL_WIDTH = 1536
QUERY_HEADS = 24
KEY_VALUE_HEADS = 8
HEAD_SIZE = 64
TOP = 8


epsilon = 1e-05
floor_score = -1e30


def rotation_tables(positions):
    half_size = HEAD_SIZE // 2
    exponent = jnp.arange(half_size, dtype=jnp.int32).astype(jnp.float32) * (2.0 / HEAD_SIZE)
    frequency = jnp.exp(-math.log(10000.0) * exponent)
    angles = positions.astype(jnp.float32)[:, None] * frequency[None, :]
    return (jnp.cos(angles)[:, None, :], jnp.sin(angles)[:, None, :])


def apply_rotation(values, cosine_table, sine_table):
    half_size = values.shape[-1] // 2
    first = values[..., :half_size]
    second = values[..., half_size:]
    return jnp.concatenate(
        [first * cosine_table - second * sine_table, second * cosine_table + first * sine_table],
        axis=-1,
    )


def inverse_rotation(gradient, cosine_table, sine_table):
    half_size = gradient.shape[-1] // 2
    first = gradient[..., :half_size]
    second = gradient[..., half_size:]
    return jnp.concatenate(
        [first * cosine_table + second * sine_table, second * cosine_table - first * sine_table],
        axis=-1,
    )


def norm_back(gradient, normed, inverse):
    return inverse * (gradient - normed * jnp.mean(gradient * normed, axis=-1, keepdims=True))


GROUP = ("context", "expert")
EVERY = ("dp", "context", "expert")


def experts_on_owner(hidden_all, final_all, routes_all, router_w, w_gate, w_up, w_down, capacity):
    single = jnp.float32
    bfloat = jnp.bfloat16
    local_exp = w_gate.shape[0]
    experts = router_w.shape[1]
    tokens_block = hidden_all.shape[1]
    first = (lax.axis_index("context") * lax.axis_size("expert") + lax.axis_index("expert")) * local_exp
    expert_ids = jnp.arange(experts, dtype=jnp.int32)
    routed = jnp.any(routes_all[..., None] == expert_ids, axis=2)
    logits = jnp.einsum("btd,de->bte", hidden_all, router_w, preferred_element_type=single)
    peak = jnp.max(jnp.where(routed, logits, floor_score), axis=-1, keepdims=True)
    raised = jnp.where(routed, jnp.exp(logits - peak), 0.0)
    gates = raised / jnp.sum(raised, axis=-1, keepdims=True)
    own_gates = lax.dynamic_slice_in_dim(gates, first, local_exp, axis=2)
    own_mask = lax.dynamic_slice_in_dim(routed.astype(single), first, local_exp, axis=2)
    token_ids = jnp.arange(tokens_block, dtype=jnp.int32)
    before = (token_ids[:, None] < token_ids[None, :]).astype(bfloat)
    rank = jnp.einsum("btj,ts->bjs", own_mask.astype(bfloat), before, preferred_element_type=single)
    slots = jnp.arange(capacity, dtype=jnp.int32).astype(single)
    own_mask = own_mask.swapaxes(1, 2)
    own_gates = own_gates.swapaxes(1, 2)
    picks = (rank[:, :, None, :] == slots[:, None]) & (own_mask[:, :, None, :] > 0.5)
    pick = picks.astype(bfloat)
    row_gates = jnp.sum(jnp.where(picks, own_gates[:, :, None, :], 0.0), axis=-1)
    received = jnp.einsum("bemt,btd->bemd", pick, hidden_all, preferred_element_type=single).astype(bfloat)
    row_final = jnp.einsum("bemt,btd->bemd", pick, final_all, preferred_element_type=single)
    gate_pre = jnp.einsum("bemd,edf->bemf", received, w_gate, preferred_element_type=single)
    up_pre = jnp.einsum("bemd,edf->bemf", received, w_up, preferred_element_type=single)
    sigmoid_gate = jax.nn.sigmoid(gate_pre)
    silu_gate = gate_pre * sigmoid_gate
    hidden_e = (silu_gate * up_pre).astype(bfloat)
    expert_out = jnp.einsum("bemf,efd->bemd", hidden_e, w_down, preferred_element_type=single).astype(bfloat)
    weighted = (pick.astype(single) * row_gates[..., None]).astype(bfloat)
    combined = jnp.einsum("bemt,bemd->btd", weighted, expert_out, preferred_element_type=single)
    row_score = jnp.sum(row_final * expert_out.astype(single), axis=-1)
    scores = jnp.sum(jnp.where(picks, row_score[..., None], 0.0), axis=2)
    grad_route = (row_gates[..., None] * row_final).astype(bfloat)
    grad_w_down = jnp.einsum("bemf,bemd->efd", hidden_e, grad_route, preferred_element_type=single)
    grad_hidden_e = (
        jnp.einsum("bemd,efd->bemf", grad_route, w_down, preferred_element_type=single)
        .astype(bfloat)
        .astype(single)
    )
    grad_gate_pre = (
        grad_hidden_e * up_pre * sigmoid_gate * (1.0 + gate_pre * (1.0 - sigmoid_gate))
    ).astype(bfloat)
    grad_up_pre = (grad_hidden_e * silu_gate).astype(bfloat)
    grad_w_gate = jnp.einsum("bemd,bemf->edf", received, grad_gate_pre, preferred_element_type=single)
    grad_w_up = jnp.einsum("bemd,bemf->edf", received, grad_up_pre, preferred_element_type=single)
    grad_rows = jnp.einsum("bemf,edf->bemd", grad_gate_pre, w_gate, preferred_element_type=single)
    grad_rows = (
        grad_rows + jnp.einsum("bemf,edf->bemd", grad_up_pre, w_up, preferred_element_type=single)
    ).astype(bfloat)
    grad_hidden = jnp.einsum("bemt,bemd->btd", pick, grad_rows, preferred_element_type=single)
    return combined, grad_hidden, scores, grad_w_gate, grad_w_up, grad_w_down


def on_device(
    tokens,
    lengths,
    routes,
    gain_attn,
    w_query,
    key_weight,
    value_weight,
    w_out,
    gain_ffn,
    w_router,
    w_gate,
    w_up,
    w_down,
    cotangent,
):
    query_groups = tokens.shape[0]
    sequence_per_device = tokens.shape[1]
    ctx_count = lax.axis_size("context")
    exp_count = lax.axis_size("expert")
    local_exp = w_gate.shape[0]
    experts = local_exp * ctx_count * exp_count
    capacity = sequence_per_device * TOP * 3 // (2 * experts)
    sequence_total = sequence_per_device * ctx_count
    group_ratio = QUERY_HEADS // KEY_VALUE_HEADS
    scale = HEAD_SIZE ** (-0.5)
    bfloat = jnp.bfloat16
    single = jnp.float32
    small = jnp.concatenate([w_router, gain_attn[:, None], gain_ffn[:, None]], axis=1)
    early = jnp.concatenate([w_query, key_weight, value_weight, small], axis=1)
    early = lax.all_gather(early, EVERY, axis=0, tiled=True)
    out_w = lax.all_gather(w_out, EVERY, axis=0, tiled=True)
    query_w = early[:, : w_query.shape[1]]
    key_w = early[:, w_query.shape[1] : w_query.shape[1] + key_weight.shape[1]]
    value_w = early[:, w_query.shape[1] + key_weight.shape[1] : -small.shape[1]]
    router_w = early[:, -small.shape[1] : -2]
    gain_one = early[:, -2]
    gain_two = early[:, -1]
    gain_one = gain_one.astype(single)
    gain_two = gain_two.astype(single)
    positions = lax.axis_index("context") * sequence_per_device + jnp.arange(
        sequence_per_device, dtype=jnp.int32
    )
    key_pos = jnp.arange(sequence_total, dtype=jnp.int32)
    valid = (positions[None, :] < lengths[:, None]).astype(single)[..., None]
    cosine_table, sine_table = rotation_tables(positions)
    inputs = tokens.astype(single)
    inverse_one = lax.rsqrt(jnp.mean(inputs * inputs, axis=-1, keepdims=True) + epsilon)
    normed_one = inputs * inverse_one
    hidden_one = (normed_one * gain_one).astype(bfloat)
    query_lin = jnp.einsum("gsd,de->gse", hidden_one, query_w, preferred_element_type=single)
    key_linear = jnp.einsum("gsd,de->gse", hidden_one, key_w, preferred_element_type=single)
    value_lower = jnp.einsum(
        "gsd,de->gse", hidden_one, value_w, preferred_element_type=single
    ).astype(bfloat)
    query_rotated = (
        apply_rotation(
            query_lin.reshape(query_groups, sequence_per_device, QUERY_HEADS, HEAD_SIZE),
            cosine_table,
            sine_table,
        )
        .astype(bfloat)
        .reshape(query_groups, sequence_per_device, QUERY_HEADS * HEAD_SIZE)
    )
    key_rotated = (
        apply_rotation(
            key_linear.reshape(query_groups, sequence_per_device, KEY_VALUE_HEADS, HEAD_SIZE),
            cosine_table,
            sine_table,
        )
        .astype(bfloat)
        .reshape(query_groups, sequence_per_device, KEY_VALUE_HEADS * HEAD_SIZE)
    )
    gathered_keys, gathered_values = (
        lax.all_gather(key_rotated, "context", axis=1, tiled=True),
        lax.all_gather(value_lower, "context", axis=1, tiled=True),
    )

    def attn_scores(slot_index):
        query_per_head = query_rotated[slot_index].reshape(
            sequence_per_device, KEY_VALUE_HEADS, group_ratio, HEAD_SIZE
        )
        key_per_head = gathered_keys[slot_index].reshape(sequence_total, KEY_VALUE_HEADS, HEAD_SIZE)
        scores = scale * jnp.einsum(
            "skrd,tkd->krst", query_per_head, key_per_head, preferred_element_type=single
        )
        allowed = (key_pos[None, :] <= positions[:, None]) & (
            key_pos[None, :] < lengths[slot_index]
        )
        return (jnp.where(allowed, scores, floor_score), allowed, query_per_head, key_per_head)

    slot_index = 0
    scores, allowed, query_per_head, key_per_head = attn_scores(slot_index)
    peak = jnp.max(scores, axis=-1, keepdims=True)
    raised = jnp.exp(scores - peak)
    total = jnp.sum(raised, axis=-1, keepdims=True)
    probs = raised / total
    value_per_head = gathered_values[slot_index].reshape(sequence_total, KEY_VALUE_HEADS, HEAD_SIZE)
    mixed_g = jnp.einsum(
        "krst,tkd->skrd", probs.astype(bfloat), value_per_head, preferred_element_type=single
    )
    mixed_list = [mixed_g.reshape(sequence_per_device, QUERY_HEADS * HEAD_SIZE)]
    lse_list = [peak + jnp.log(total)]
    mixed_low = jnp.stack(mixed_list).astype(bfloat)
    resid = inputs + jnp.einsum("gse,ed->gsd", mixed_low, out_w, preferred_element_type=single)
    inverse_two = lax.rsqrt(jnp.mean(resid * resid, axis=-1, keepdims=True) + epsilon)
    normed_two = resid * inverse_two
    hidden_two = (normed_two * gain_two).astype(bfloat)
    logits = jnp.einsum("gsd,de->gse", hidden_two, router_w, preferred_element_type=single)
    matches = routes[..., None] == jnp.arange(experts, dtype=jnp.int32)
    chosen = jnp.sum(jnp.where(matches, logits[:, :, None, :], 0.0), axis=-1)
    gates = jax.nn.softmax(chosen, axis=-1)
    final_low = (cotangent.astype(single) * valid).astype(bfloat)
    final_all = lax.all_gather(final_low[0], GROUP, axis=0, tiled=False)
    routes_all = lax.all_gather(routes[0], GROUP, axis=0, tiled=False)
    hidden_all = lax.all_gather(hidden_two[0], GROUP, axis=0, tiled=False)
    combined, grad_hidden, scores, grad_w_gate, grad_w_up, grad_w_down = experts_on_owner(
        hidden_all, final_all, routes_all, router_w, w_gate, w_up, w_down, capacity
    )
    combined = lax.psum_scatter(combined.astype(bfloat), GROUP, scatter_dimension=0, tiled=False)
    grad_hidden = lax.psum_scatter(grad_hidden.astype(bfloat), GROUP, scatter_dimension=0, tiled=False)
    scores = lax.all_to_all(scores, GROUP, split_axis=0, concat_axis=0, tiled=True)
    scores = scores.reshape(experts, sequence_per_device)
    block_out = (valid * (resid + combined.astype(single)[None])).astype(bfloat)
    grad_final = cotangent.astype(single) * valid
    grad_gates = jnp.sum(jnp.where(matches, scores.T[None, :, None, :], 0.0), axis=-1)
    gate_mean = jnp.sum(gates * grad_gates, axis=-1, keepdims=True)
    grad_chosen = gates * (grad_gates - gate_mean)
    grad_logits = jnp.sum(jnp.where(matches, grad_chosen[..., None], 0.0), axis=2).astype(bfloat)
    grad_w_router = jnp.einsum(
        "gsd,gse->de", hidden_two, grad_logits, preferred_element_type=single
    )
    grad_hidden_two = grad_hidden.astype(single)[None]
    grad_hidden_two = grad_hidden_two + jnp.einsum(
        "gse,de->gsd", grad_logits, router_w, preferred_element_type=single
    )
    grad_gain_ffn = jnp.sum(grad_hidden_two * normed_two, axis=(0, 1))
    grad_resid = norm_back(grad_hidden_two * gain_two, normed_two, inverse_two) + grad_final
    grad_attn = grad_resid.astype(bfloat)
    grad_w_out = jnp.einsum("gse,gsd->ed", mixed_low, grad_attn, preferred_element_type=single)
    mixed_gradient = jnp.einsum(
        "gsd,ed->gse", grad_attn, out_w, preferred_element_type=single
    ).astype(bfloat)
    slot_index = 0
    scores, allowed, query_per_head, key_per_head = attn_scores(slot_index)
    probs = jnp.where(allowed, jnp.exp(scores - lse_list[slot_index]), 0.0)
    value_per_head = gathered_values[slot_index].reshape(sequence_total, KEY_VALUE_HEADS, HEAD_SIZE)
    head_gradient = mixed_gradient[slot_index].reshape(
        sequence_per_device, KEY_VALUE_HEADS, group_ratio, HEAD_SIZE
    )
    grad_probs = jnp.einsum(
        "skrd,tkd->krst", head_gradient, value_per_head, preferred_element_type=single
    )
    row_delta = jnp.sum(probs * grad_probs, axis=-1, keepdims=True)
    grad_scores = (probs * (grad_probs - row_delta)).astype(bfloat)
    grad_queries = [
        (
            scale
            * jnp.einsum("krst,tkd->skrd", grad_scores, key_per_head, preferred_element_type=single)
        ).reshape(sequence_per_device, QUERY_HEADS, HEAD_SIZE)
    ]
    grad_keys = [
        (
            scale
            * jnp.einsum(
                "krst,skrd->tkd", grad_scores, query_per_head, preferred_element_type=single
            )
        ).reshape(sequence_total, KEY_VALUE_HEADS * HEAD_SIZE)
    ]
    grad_values = [
        jnp.einsum(
            "krst,skrd->tkd", probs.astype(bfloat), head_gradient, preferred_element_type=single
        ).reshape(sequence_total, KEY_VALUE_HEADS * HEAD_SIZE)
    ]
    key_gradient_rows, value_grad = (
        lax.psum_scatter(
            jnp.stack(grad_keys).astype(jnp.bfloat16), "context", scatter_dimension=1, tiled=True
        ).astype(jnp.float32),
        lax.psum_scatter(
            jnp.stack(grad_values).astype(jnp.bfloat16), "context", scatter_dimension=1, tiled=True
        ).astype(jnp.float32),
    )
    grad_query_lin = (
        inverse_rotation(jnp.stack(grad_queries), cosine_table, sine_table)
        .astype(bfloat)
        .reshape(query_groups, sequence_per_device, QUERY_HEADS * HEAD_SIZE)
    )
    grad_key_lin = (
        inverse_rotation(
            key_gradient_rows.reshape(
                query_groups, sequence_per_device, KEY_VALUE_HEADS, HEAD_SIZE
            ),
            cosine_table,
            sine_table,
        )
        .astype(bfloat)
        .reshape(query_groups, sequence_per_device, KEY_VALUE_HEADS * HEAD_SIZE)
    )
    grad_value_low = value_grad.astype(bfloat)
    grad_w_query = jnp.einsum(
        "gsd,gse->de", hidden_one, grad_query_lin, preferred_element_type=single
    )
    grad_w_key = jnp.einsum("gsd,gse->de", hidden_one, grad_key_lin, preferred_element_type=single)
    grad_w_value = jnp.einsum(
        "gsd,gse->de", hidden_one, grad_value_low, preferred_element_type=single
    )
    grad_hidden_one = jnp.einsum(
        "gse,de->gsd", grad_query_lin, query_w, preferred_element_type=single
    )
    grad_hidden_one = grad_hidden_one + jnp.einsum(
        "gse,de->gsd", grad_key_lin, key_w, preferred_element_type=single
    )
    grad_hidden_one = grad_hidden_one + jnp.einsum(
        "gse,de->gsd", grad_value_low, value_w, preferred_element_type=single
    )
    grad_gain_attn = jnp.sum(grad_hidden_one * normed_one, axis=(0, 1))
    grad_tokens = norm_back(grad_hidden_one * gain_one, normed_one, inverse_one) + grad_resid
    late = jnp.concatenate(
        [
            grad_w_query,
            grad_w_key,
            grad_w_value,
            grad_w_router,
            grad_gain_attn[:, None],
            grad_gain_ffn[:, None],
        ],
        axis=1,
    ).astype(bfloat)
    late = lax.psum_scatter(late, EVERY, scatter_dimension=0, tiled=True).astype(single)
    out_grad = lax.psum_scatter(
        grad_w_out.astype(bfloat), EVERY, scatter_dimension=0, tiled=True
    ).astype(single)
    width = grad_w_query.shape[1]
    narrow = grad_w_key.shape[1]
    shard_grads = (
        late[:, -2],
        late[:, :width],
        late[:, width : width + narrow],
        late[:, width + narrow : width + 2 * narrow],
        out_grad,
        late[:, -1],
        late[:, width + 2 * narrow : -2],
    )
    expert_sums = (
        lax.psum_scatter(
            grad_w_gate.astype(jnp.bfloat16), "dp", scatter_dimension=1, tiled=True
        ).astype(jnp.float32),
        lax.psum_scatter(
            grad_w_up.astype(jnp.bfloat16), "dp", scatter_dimension=1, tiled=True
        ).astype(jnp.float32),
        lax.psum_scatter(
            grad_w_down.astype(jnp.bfloat16), "dp", scatter_dimension=1, tiled=True
        ).astype(jnp.float32),
    )
    return (
        block_out,
        grad_tokens,
        shard_grads[0],
        shard_grads[1],
        shard_grads[2],
        shard_grads[3],
        shard_grads[4],
        shard_grads[5],
        shard_grads[6],
        expert_sums[0],
        expert_sums[1],
        expert_sums[2],
    )


def solution(mesh):
    in_specs = (
        P(("dp", "expert"), "context", None),
        P(("dp", "expert")),
        P(("dp", "expert"), "context", None),
        P(("dp", "context", "expert")),
        P(("dp", "context", "expert"), None),
        P(("dp", "context", "expert"), None),
        P(("dp", "context", "expert"), None),
        P(("dp", "context", "expert"), None),
        P(("dp", "context", "expert")),
        P(("dp", "context", "expert"), None),
        P(("context", "expert"), None, None),
        P(("context", "expert"), None, None),
        P(("context", "expert"), None, None),
        P(("dp", "expert"), "context", None),
    )
    out_specs = (
        P(("dp", "expert"), "context", None),
        P(("dp", "expert"), "context", None),
        P(("dp", "context", "expert")),
        P(("dp", "context", "expert"), None),
        P(("dp", "context", "expert"), None),
        P(("dp", "context", "expert"), None),
        P(("dp", "context", "expert"), None),
        P(("dp", "context", "expert")),
        P(("dp", "context", "expert"), None),
        P(("context", "expert"), "dp", None),
        P(("context", "expert"), "dp", None),
        P(("context", "expert"), "dp", None),
    )
    return jax.shard_map(
        on_device, mesh=mesh, in_specs=in_specs, out_specs=out_specs, check_vma=False
    )
```

profile of v0, /device:TPU:0, one launch (start us, length us, event | category | flops | bytes accessed | tf_op | source)
XLA Modules:
  0.0 1292.5 jit_solution(16110616695014916000)
XLA Ops:
  12.9 78.2 %all-gather.8.cloned.1.call-done = bf16[1536,2594]{1,0:T(8,128)(2,1)} async-done(((bf16[48,2594]{1,0:T(8,128)(2,1)}), bf16[1536,2594]{1,0:T(8,128)(2,1)}) %all-gather.8.cloned.1.call-update) | async-done | bytes 7968784 | tf_op jit(solution)/shard_map/all_gather | solution.py:142
  108.8 4.9 slice_bitcast_fusion
  113.6 6.6 copy.160
  120.3 4.3 convolution_bitcast_fusion.1
  130.4 13.5 %fusion.15 = (f32[8,3,256]{2,1,0:T(4,128)S(1)}, f32[8,1024,256,3]{2,1,3,0:T(8,128)}) fusion(pred[256,1024]{0,1:T(8,128)(4,1)S(1)} %fusion.109, bf16[1024,8,64,1]{0,2,3,1:T(8,128)(2,1)} %bitcast.281, bf16[256,8,3,32]{0,3,2,1:T(8,128)(2,1)} %bitcast.290, bf16[256,8,3,32]{0,3,2,1:T(8,128)(2,1)} %bitcast.288), kind=kOutput, calls=%fused_computation.25 | convolution fusion | flops 825747456 | bytes 27287552 | tf_op jit(solution)/shard_map/skrd,tkd->krst/dot_general | solution.py:195
  143.9 11.1 fusion.4
  155.0 12.6 fusion.98
  167.6 29.2 %all-gather.12.cloned.1.call-done = bf16[1536,1536]{1,0:T(8,128)(2,1)} async-done(((bf16[48,1536]{1,0:T(8,128)(2,1)}), bf16[1536,1536]{1,0:T(8,128)(2,1)}) %all-gather.12.cloned.1.call-update) | async-done | bytes 4718608 | tf_op jit(solution)/shard_map/all_gather | solution.py:143
  196.7 4.3 multiply_reduce_fusion
  203.3 34.9 %all_gather.25 = s32[16,256,8]{1,2,0:T(8,128)S(1)} all-gather(s32[1,256,8]{1,2,0:T(8,128)S(1)} %copy-done.26), channel_id=1, replica_groups=mesh['dp'=2,'context'=4,'expert'=4] {'context','expert'}, dimensions={0}, use_global_device_ids=true | all-gather | bytes 139264 | tf_op jit(solution)/shard_map/all_gather | solution.py:226
  240.2 61.2 %all-gather.16.cloned.1.call-done = bf16[16,256,1536]{2,1,0:T(8,128)(2,1)} async-done(((bf16[1,256,1536]{2,1,0:T(8,128)(2,1)}), bf16[16,256,1536]{2,1,0:T(8,128)(2,1)}) %all-gather.16.cloned.1.call-update) | async-done | bytes 12582928 | tf_op jit(solution)/shard_map/all_gather | solution.py:225
  301.4 14.1 %fusion.7 = f32[16,2,96,1536]{3,2,1,0:T(8,128)} fusion(bf16[16,256,1536]{2,1,0:T(8,128)(2,1)} %all-gather.16.cloned.1.call-done, f32[16,2,256]{2,1,0:T(2,128)S(1)} %copy.163, f32[96]{0:T(128)S(1)} %iota_convert_fusion, pred[16,2,256]{2,1,0:T(4,128)(4,1)S(1)} %copy.164), kind=kOutput, calls=%fused_computation.18 | convolution fusion | flops 2417491968 | bytes 31498624 | tf_op jit(solution)/shard_map/bemt,btd->bemd/dot_general | solution.py:80
  315.4 87.1 %all-gather.14.cloned.1.call-done = bf16[16,256,1536]{2,1,0:T(8,128)(2,1)} async-done(((bf16[1,256,1536]{2,1,0:T(8,128)(2,1)}), bf16[16,256,1536]{2,1,0:T(8,128)(2,1)}) %all-gather.14.cloned.1.call-update) | async-done | bytes 12582928 | tf_op jit(solution)/shard_map/all_gather | solution.py:227
  402.5 8.3 fusion.123
  411.8 11.0 fusion.27
  422.8 11.2 fusion.25
  434.0 10.4 fusion.34
  444.4 12.3 fusion.5
  460.3 16.1 %fusion.33 = (bf16[16,2,96,512]{3,2,0,1:T(8,128)(2,1)}, bf16[16,2,96,512]{3,2,0,1:T(8,128)(2,1)}) fusion(f32[2,16,96,512]{3,2,1,0:T(8,128)} %fusion.25, f32[2,16,96,512]{3,2,1,0:T(8,128)} %get-tuple-element.105, bf16[2,512,1536]{2,1,0:T(8,128)(2,1)} %param.26, f32[16,2,96,1536]{3,2,1,0:T(8,128)} %fusion.7, f32[16,2,96]{2,1,0:T(2,128)S(1)} %get-tuple-element.79), kind=kOutput, calls=%fused_computation.48 | convolution fusion | flops 4864868352 | bytes 40906752 | tf_op jit(solution)/shard_map/bemd,efd->bemf/dot_general | solution.py:94
  476.4 11.8 fusion.52
  488.1 15.9 %bitcast_convert_fusion = bf16[16,256,1536]{2,1,0:T(8,128)(2,1)} fusion(f32[2,16,96,1536]{3,2,0,1:T(8,128)} %fusion.52, bf16[2,1536,512]{2,1,0:T(8,128)(2,1)S(1)} %copy-done, bf16[16,2,96,512]{3,2,0,1:T(8,128)(2,1)} %get-tuple-element.82, f32[16,2,256]{2,1,0:T(2,128)S(1)} %copy.163, f32[96]{0:T(128)S(1)} %iota_convert_fusion, pred[16,2,256]{2,1,0:T(4,128)(4,1)S(1)} %copy.164), kind=kOutput, calls=%fused_computation.6 | convolution fusion | flops 7265058816 | bytes 37790080 | tf_op jit(solution)/shard_map/bemt,bemd->btd/dot_general | solution.py:108
  504.1 10.0 bitcast_convert_fusion.1
  516.7 3.5 all-to-all-start
  520.3 6.4 all-to-all-done
  527.0 110.2 %reduce-scatter.14.cloned.1.call-done = bf16[1,256,1536]{2,1,0:T(8,128)(2,1)} async-done(((bf16[16,256,1536]{2,1,0:T(8,128)(2,1)}), bf16[1,256,1536]{2,1,0:T(8,128)(2,1)}) %reduce-scatter.14.cloned.1.call-update) | async-done | bytes 786448 | tf_op jit(solution)/shard_map/reduce_scatter | solution.py:232
  640.2 135.0 %reduce-scatter.12.cloned.1.call-done = bf16[1,256,1536]{2,1,0:T(8,128)(2,1)} async-done(((bf16[16,256,1536]{2,1,0:T(8,128)(2,1)}), bf16[1,256,1536]{2,1,0:T(8,128)(2,1)}) %reduce-scatter.12.cloned.1.call-update) | async-done | bytes 786448 | tf_op jit(solution)/shard_map/reduce_scatter | solution.py:231
  775.1 3.4 fusion.83
  778.5 4.7 convolution_convert_fusion.4
  785.5 17.0 %fusion.1 = (f32[8,3,256]{2,1,0:T(4,128)S(1)}, f32[8,1024,256,3]{2,1,3,0:T(8,128)}) fusion(f32[8,3,256]{2,1,0:T(4,128)S(1)} %log_add_fusion, pred[256,1024]{0,1:T(8,128)(4,1)S(1)} %fusion.109, f32[8,1024,256,3]{2,1,3,0:T(8,128)} %get-tuple-element.101, bf16[1024,8,64,1]{0,2,3,1:T(8,128)(2,1)S(1)} %bitcast.296, bf16[256,8,3,64]{0,3,2,1:T(8,128)(2,1)} %bitcast.299), kind=kOutput, calls=%fused_computation.3 | convolution fusion | flops 843048960 | bytes 52477952 | tf_op jit(solution)/shard_map/skrd,tkd->krst/dot_general | solution.py:262
  802.6 21.7 %fusion.3 = bf16[8,3,256,1024]{2,3,1,0:T(8,128)(2,1)} fusion(f32[8,1024,256,3]{2,1,3,0:T(8,128)} %get-tuple-element.112, f32[8,3,256]{2,1,0:T(4,128)S(1)} %get-tuple-element.111, f32[8,3,256]{2,1,0:T(4,128)S(1)} %log_add_fusion, pred[256,1024]{0,1:T(8,128)(4,1)S(1)} %fusion.109, f32[8,1024,256,3]{2,1,3,0:T(8,128)} %get-tuple-element.101), kind=kLoop, calls=%fused_computation.5 | loop fusion | flops 44040192 | bytes 63225856 | tf_op jit(solution)/shard_map/convert_element_type | solution.py:266
  824.3 9.5 fusion.70
  833.9 13.0 %bitcast_convert_fusion.5 = bf16[8,64,1024]{2,1,0:T(8,128)(2,1)} fusion(bf16[256,8,3,64]{0,3,2,1:T(8,128)(2,1)S(1)} %bitcast.300, f32[8,3,256]{2,1,0:T(4,128)S(1)} %log_add_fusion, pred[256,1024]{0,1:T(8,128)(4,1)S(1)} %fusion.109, f32[8,1024,256,3]{2,1,3,0:T(8,128)} %get-tuple-element.101), kind=kOutput, calls=%fused_computation.96 | convolution fusion | flops 837287936 | bytes 27287552 | tf_op jit(solution)/shard_map/krst,skrd->tkd/dot_general | solution.py:282
  847.4 14.6 %bitcast_convert_fusion.2 = bf16[2,512,1536]{2,1,0:T(8,128)(2,1)} fusion(bf16[16,2,96,512]{3,2,0,1:T(8,128)(2,1)} %get-tuple-element.104, f32[16,2,96,1536]{3,2,1,0:T(8,128)} %fusion.7, f32[16,2,96]{2,1,0:T(2,128)S(1)} %get-tuple-element.79), kind=kOutput, calls=%fused_computation.40 | convolution fusion | flops 4842848256 | bytes 25178112 | tf_op jit(solution)/shard_map/bemf,bemd->efd/dot_general | solution.py:92
  862.1 13.0 %bitcast_convert_fusion.3 = bf16[2,1536,512]{2,1,0:T(8,128)(2,1)} fusion(bf16[16,2,96,1536]{3,2,1,0:T(8,128)(2,1)} %fusion.27, bf16[16,2,96,512]{3,2,0,1:T(8,128)(2,1)} %get-tuple-element.82), kind=kOutput, calls=%fused_computation.41 | convolution fusion | flops 4833411072 | bytes 15728640 | tf_op jit(solution)/shard_map/bemd,bemf->edf/dot_general | solution.py:103
  875.2 13.1 %bitcast_convert_fusion.4 = bf16[2,1536,512]{2,1,0:T(8,128)(2,1)} fusion(bf16[16,2,96,1536]{3,2,1,0:T(8,128)(2,1)} %fusion.27, bf16[16,2,96,512]{3,2,0,1:T(8,128)(2,1)} %get-tuple-element.83), kind=kOutput, calls=%fused_computation.42 | convolution fusion | flops 4833411072 | bytes 15728640 | tf_op jit(solution)/shard_map/bemd,bemf->edf/dot_general | solution.py:102
  889.4 3.5 convolution_convert_fusion.1
  894.5 7.3 convolution_multiply_fusion
  902.9 3.7 convolution_convert_fusion
  906.6 4.9 fusion.42
  916.3 4.1 fusion.78
  924.0 36.4 %concatenate.53 = bf16[1536,2594]{0,1:T(8,128)(2,1)} concatenate(bf16[1536,1536]{0,1:T(8,128)(2,1)} %convolution_convert_fusion, bf16[1536,512]{0,1:T(8,128)(2,1)} %convolution_convert_fusion.3, bf16[1536,512]{0,1:T(8,128)(2,1)} %convolution_convert_fusion.2, bf16[1536,32]{0,1:T(8,128)(2,1)S(1)} %convolution_convert_fusion.5, bf16[1536,1]{0,1:T(2,128)(2,1)S(1)} %broadcast_in_dim.143, ...), dimensions={1} | concatenate | bytes 15937536 | tf_op jit(solution)/shard_map/concatenate | solution.py:329
  960.4 11.3 copy.200
  971.7 3.5 convert_element_type.386
  976.7 3.5 convert_element_type.384
  980.2 42.1 %reduce-scatter.22.cloned.1.call-done = bf16[2,768,512]{2,1,0:T(8,128)(2,1)} async-done(((bf16[2,1536,512]{2,1,0:T(8,128)(2,1)}), bf16[2,768,512]{2,1,0:T(8,128)(2,1)}) %reduce-scatter.22.cloned.1.call-update) | async-done | bytes 1572880 | tf_op jit(solution)/shard_map/reduce_scatter | solution.py:356
  1022.3 3.6 convert_element_type.382
  1027.5 108.1 %reduce-scatter.20.cloned.1.call-done = bf16[48,1536]{1,0:T(8,128)(2,1)} async-done(((bf16[1536,1536]{1,0:T(8,128)(2,1)}), bf16[48,1536]{1,0:T(8,128)(2,1)}) %reduce-scatter.20.cloned.1.call-update) | async-done | bytes 147472 | tf_op jit(solution)/shard_map/reduce_scatter | solution.py:341
  1137.2 133.3 %reduce-scatter.28.cloned.1.call-done = bf16[48,2594]{1,0:T(8,128)(2,1)} async-done(((bf16[1536,2594]{1,0:T(8,128)(2,1)}), bf16[48,2594]{1,0:T(8,128)(2,1)}) %reduce-scatter.28.cloned.1.call-update) | async-done | bytes 249040
  (173 shorter events, 78.3 us)
Async XLA Ops:
  7.2 426.9 %copy-start = (bf16[2,1536,512]{2,1,0:T(8,128)(2,1)S(1)}, bf16[2,1536,512]{2,1,0:T(8,128)(2,1)}, u32[]{:S(2)}) copy-start(bf16[2,1536,512]{2,1,0:T(8,128)(2,1)} %param.25) | copy-start | bytes 9437188
  7.2 83.9 %all-gather.8.cloned.1.call-start = ((), (), s32[]{:S(2)}) async-start(), calls=%async_computation.10 | async-start | bytes 8515584 | tf_op jit(solution)/shard_map/all_gather | solution.py:142
  11.4 114.3 %all-gather.18.cloned.1.call-start = ((), (), s32[]{:S(2)}) async-start(), calls=%async_computation.23 | async-start | bytes 1310720 | tf_op jit(solution)/shard_map/all_gather | solution.py:187
  12.9 107.4 %copy-start.28 = (f32[256]{0:T(256)}, f32[256]{0:T(256)S(1)}, u32[]{:S(2)}) copy-start(f32[256]{0:T(256)S(1)} %add_rsqrt_fusion.1) | copy-start | bytes 3076
  92.8 27.4 %copy-start.22 = (f32[1536]{0:T(1024)}, f32[1536]{0:T(1024)S(1)}, u32[]{:S(2)}) copy-start(f32[1536]{0:T(1024)S(1)} %get-tuple-element.73) | copy-start | bytes 18436
  95.9 34.5 %all-gather.10.cloned.1.call-start = ((), (), s32[]{:S(2)}) async-start(), calls=%async_computation.11 | async-start | bytes 1310720 | tf_op jit(solution)/shard_map/all_gather | solution.py:186
  96.1 28.4 %copy-start.16 = (f32[256,32]{0,1:T(8,128)}, f32[256,32]{0,1:T(8,128)S(1)}, u32[]{:S(2)}) copy-start(f32[256,32]{0,1:T(8,128)S(1)} %get-tuple-element.98) | copy-start | bytes 98308
  96.1 28.4 %copy-start.18 = (f32[256,32]{0,1:T(8,128)}, f32[256,32]{0,1:T(8,128)S(1)}, u32[]{:S(2)}) copy-start(f32[256,32]{0,1:T(8,128)S(1)} %get-tuple-element.99) | copy-start | bytes 98308
  104.7 92.0 %all-gather.12.cloned.1.call-start = ((), (), s32[]{:S(2)}) async-start(), calls=%async_computation.12 | async-start | bytes 4866048 | tf_op jit(solution)/shard_map/all_gather | solution.py:143
  105.3 196.0 %all-gather.16.cloned.1.call-start = ((), (), s32[]{:S(2)}) async-start(), calls=%async_computation.15 | async-start | bytes 13369344 | tf_op jit(solution)/shard_map/all_gather | solution.py:225
  106.0 7.6 copy-start.30
  108.3 294.2 %all-gather.14.cloned.1.call-start = ((), (), s32[]{:S(2)}) async-start(), calls=%async_computation.13 | async-start | bytes 13369344 | tf_op jit(solution)/shard_map/all_gather | solution.py:227
  143.9 11.1 copy-start.14
  201.0 1.1 copy-start.3
  201.0 2.3 copy-start.26
  203.3 433.9 %reduce-scatter.14.cloned.1.call-start = ((), (), s32[]{:S(2)}) async-start(), calls=%async_computation.16 | async-start | bytes 13369344 | tf_op jit(solution)/shard_map/reduce_scatter | solution.py:232
  402.5 8.3 copy-start.25
  411.8 11.0 copy-start.32
  422.8 11.2 copy-start.5
  434.0 10.4 copy-start.11
  504.0 271.1 %reduce-scatter.12.cloned.1.call-start = ((), (), s32[]{:S(2)}) async-start(), calls=%async_computation.14 | async-start | bytes 13369344 | tf_op jit(solution)/shard_map/reduce_scatter | solution.py:231
  514.1 1.2 copy-start.6
  514.1 12.6 copy-start.27
  514.1 123.0 %copy-start.4 = (f32[1,256,1536]{2,1,0:T(8,128)S(1)}, f32[1,256,1536]{2,1,0:T(8,128)}, u32[]{:S(2)}) copy-start(f32[1,256,1536]{2,1,0:T(8,128)} %copy-done.3) | copy-start | bytes 4718596
  515.3 259.8 %copy-start.31 = (f32[256]{0:T(256)S(1)}, f32[256]{0:T(256)}, u32[]{:S(2)}) copy-start(f32[256]{0:T(256)} %copy-done.30) | copy-start | bytes 3076
  516.7 10.0 all-to-all-start
  520.3 391.3 %reduce-scatter.16.cloned.1.call-start = ((), (), s32[]{:S(2)}) async-start(), calls=%async_computation.17 | async-start | bytes 1310720 | tf_op jit(solution)/shard_map/reduce_scatter | solution.py:287
  778.5 7.0 copy-start.15
  802.6 21.7 %copy-start.9 = (bf16[1,256,24,32]{1,3,2,0:T(8,128)(2,1)S(1)}, bf16[1,256,24,32]{1,3,2,0:T(8,128)(2,1)}, u32[]{:S(2)}) copy-start(bf16[1,256,24,32]{1,3,2,0:T(8,128)(2,1)} %get-tuple-element.86) | copy-start | bytes 1179652
  802.6 21.7 %copy-start.10 = (bf16[1,256,24,32]{1,3,2,0:T(8,128)(2,1)S(1)}, bf16[1,256,24,32]{1,3,2,0:T(8,128)(2,1)}, u32[]{:S(2)}) copy-start(bf16[1,256,24,32]{1,3,2,0:T(8,128)(2,1)} %get-tuple-element.87) | copy-start | bytes 1179652
  824.3 9.6 copy-start.20
  833.8 82.4 %reduce-scatter.18.cloned.1.call-start = ((), (), s32[]{:S(2)}) async-start(), calls=%async_computation.18 | async-start | bytes 1310720 | tf_op jit(solution)/shard_map/reduce_scatter | solution.py:290
  847.0 124.7 %reduce-scatter.26.cloned.1.call-start = ((), (), s32[]{:S(2)}) async-start(), calls=%async_computation.22 | async-start | bytes 4718592 | tf_op jit(solution)/shard_map/reduce_scatter | solution.py:362
  862.0 114.6 %reduce-scatter.24.cloned.1.call-start = ((), (), s32[]{:S(2)}) async-start(), calls=%async_computation.21 | async-start | bytes 4718592 | tf_op jit(solution)/shard_map/reduce_scatter | solution.py:359
  875.1 147.2 %reduce-scatter.22.cloned.1.call-start = ((), (), s32[]{:S(2)}) async-start(), calls=%async_computation.20 | async-start | bytes 4718592 | tf_op jit(solution)/shard_map/reduce_scatter | solution.py:356
  888.2 1.1 copy-start.8
  888.3 247.3 %reduce-scatter.20.cloned.1.call-start = ((), (), s32[]{:S(2)}) async-start(), calls=%async_computation.19 | async-start | bytes 4866048 | tf_op jit(solution)/shard_map/reduce_scatter | solution.py:341
  892.9 1.4 copy-start.7
  892.9 377.6 %reduce-scatter.28.cloned.1.call-start = ((), (), s32[]{:S(2)}) async-start(), calls=%async_computation.24 | async-start | bytes 8515584
  894.5 7.3 copy-start.17
  894.5 7.3 copy-start.19
  901.8 1.1 copy-start.2
  901.8 1.1 copy-start.23
  901.8 1.1 copy-start.29
  911.6 1.5 copy-start.12
  916.3 5.9 copy-start.21
  1022.3 3.6 copy-start.13
  1272.6 13.2 %copy-start.1 = (bf16[2,1536,512]{2,1,0:T(8,128)(2,1)S(1)}, bf16[2,1536,512]{2,1,0:T(8,128)(2,1)}, u32[]{:S(2)}) copy-start(bf16[2,1536,512]{2,1,0:T(8,128)(2,1)} %param.25) | copy-start | bytes 9437188
  (1 other events, 0.7 us)
Sparse Core Ops, SparseCore 0:
  11.6 79.4 all-gather.7
  96.0 15.3 all-gather.17
  113.5 16.8 all-gather.9
  133.1 63.5 all-gather.11
  199.5 101.8 all-gather.15
  303.5 98.9 all-gather.13
  504.2 132.9 reduce-scatter.13
  641.2 133.9 reduce-scatter.11
  834.0 24.0 reduce-scatter.15
  860.5 24.8 reduce-scatter.17
  887.7 43.3 reduce-scatter.25
  933.3 43.3 reduce-scatter.23
  978.9 43.3 reduce-scatter.21
  1028.5 107.0 reduce-scatter.19
  1141.3 129.1 reduce-scatter.27
where the time goes:
time: 1300 us; the launch traced here: 1290 us
  waiting for transfers between devices  795 us (61%)
  matrix products  281 us (22%)
  local copies, waits for them, and re-layouts  92.4 us (7%)
  other arithmetic  68.6 us (5%)
  blocking collectives  34.9 us (3%)
  between operations  15.3 us (1%)
    reduce_scatter x1, waiting for transfers between devices, on_device(): lax.psum_scatter(combined.astype(bfloat), GROUP, scatter_dimension=0, til...  135 us
    unnamed x16, waiting for transfers between devices  134 us
    reduce_scatter x1, waiting for transfers between devices, on_device(): lax.psum_scatter(grad_hidden.astype(bfloat), GROUP, scatter_dimension=0,...  110 us
    reduce_scatter x1, waiting for transfers between devices, on_device(): lax.psum_scatter(grad_w_out.astype(bfloat), EVERY, scatter_dimension=0, t...  108 us
    all_gather x1, waiting for transfers between devices, on_device(): hidden_all = lax.all_gather(hidden_two[0], GROUP, axis=0, tiled=False)  87.1 us
    all_gather x1, waiting for transfers between devices, on_device(): early = lax.all_gather(early, EVERY, axis=0, tiled=True)  78.2 us
    all_gather x1, waiting for transfers between devices, on_device(): final_all = lax.all_gather(final_low[0], GROUP, axis=0, tiled=False)  61.2 us
    reduce_scatter x1, waiting for transfers between devices, on_device(): lax.psum_scatter(grad_w_gate.astype(jnp.bfloat16), 'dp', scatter_dimensio...  42.1 us
  transfers between devices with their start and end apart: 16, of which 12 were waited for; matrix products, arithmetic and copies ran while one was open for 19% of the time, Pallas kernels for 0%

commit v1 on v0

--- a/solution.py
+++ b/solution.py
@@ -3,6 +3,8 @@
 import jax
 import jax.numpy as jnp
 from jax import lax
+from jax.experimental import pallas as pl
+from jax.experimental.pallas import tpu as pltpu
 from jax.sharding import PartitionSpec as P
 
 MODEL_WIDTH = 1536
@@ -52,61 +54,570 @@
 EVERY = ("dp", "context", "expert")
 
 
-def experts_on_owner(hidden_all, final_all, routes_all, router_w, w_gate, w_up, w_down, capacity):
+MESH_ID = pl.DeviceIdType.MESH
+CHUNK = 512
+HALF = 256
+
+
+def contract_rows(left, right):
+    return lax.dot_general(left, right, (((0,), (0,)), ((), ())), preferred_element_type=jnp.float32)
+
+
+def contract_last(left, right):
+    return lax.dot_general(left, right, (((1,), (1,)), ((), ())), preferred_element_type=jnp.float32)
+
+
+def matmul(left, right):
+    return jnp.dot(left, right, preferred_element_type=jnp.float32)
+
+
+def line_order(z, step):
+    half = z // 2
+    inner = z + half * (3 - 2 * z)
+    base = step + inner * (1 - 2 * step) * (1 - step // 2)
+    return base + half * (3 - 2 * base)
+
+
+def experts_kernel(
+    hidden_ref,
+    final_ref,
+    routes_ref,
+    router_ref,
+    gate_hbm,
+    up_hbm,
+    down_hbm,
+    back_ref,
+    part_ref,
+    score_ref,
+    grad_gate_ref,
+    grad_up_ref,
+    grad_down_ref,
+    held,
+    w_gate,
+    w_up,
+    w_down,
+    rows_in,
+    rows_grad,
+    slope_gate,
+    slope_up,
+    hidden_e,
+    picks,
+    row_gates,
+    work,
+    pool,
+    before,
+    gather_send,
+    gather_recv,
+    local_sem,
+    load_sem,
+    part_sem,
+    sum_send,
+    core_recv,
+    y_recv,
+    z_recv,
+    ready,
+):
     single = jnp.float32
     bfloat = jnp.bfloat16
+    tokens_block = hidden_ref.shape[0]
+    width = hidden_ref.shape[1]
+    experts = router_ref.shape[0]
     local_exp = w_gate.shape[0]
-    experts = router_w.shape[1]
-    tokens_block = hidden_all.shape[1]
-    first = (lax.axis_index("context") * lax.axis_size("expert") + lax.axis_index("expert")) * local_exp
-    expert_ids = jnp.arange(experts, dtype=jnp.int32)
-    routed = jnp.any(routes_all[..., None] == expert_ids, axis=2)
-    logits = jnp.einsum("btd,de->bte", hidden_all, router_w, preferred_element_type=single)
-    peak = jnp.max(jnp.where(routed, logits, floor_score), axis=-1, keepdims=True)
-    raised = jnp.where(routed, jnp.exp(logits - peak), 0.0)
-    gates = raised / jnp.sum(raised, axis=-1, keepdims=True)
-    own_gates = lax.dynamic_slice_in_dim(gates, first, local_exp, axis=2)
-    own_mask = lax.dynamic_slice_in_dim(routed.astype(single), first, local_exp, axis=2)
-    token_ids = jnp.arange(tokens_block, dtype=jnp.int32)
-    before = (token_ids[:, None] < token_ids[None, :]).astype(bfloat)
-    rank = jnp.einsum("btj,ts->bjs", own_mask.astype(bfloat), before, preferred_element_type=single)
-    slots = jnp.arange(capacity, dtype=jnp.int32).astype(single)
-    own_mask = own_mask.swapaxes(1, 2)
-    own_gates = own_gates.swapaxes(1, 2)
-    picks = (rank[:, :, None, :] == slots[:, None]) & (own_mask[:, :, None, :] > 0.5)
-    pick = picks.astype(bfloat)
-    row_gates = jnp.sum(jnp.where(picks, own_gates[:, :, None, :], 0.0), axis=-1)
-    received = jnp.einsum("bemt,btd->bemd", pick, hidden_all, preferred_element_type=single).astype(bfloat)
-    row_final = jnp.einsum("bemt,btd->bemd", pick, final_all, preferred_element_type=single)
-    gate_pre = jnp.einsum("bemd,edf->bemf", received, w_gate, preferred_element_type=single)
-    up_pre = jnp.einsum("bemd,edf->bemf", received, w_up, preferred_element_type=single)
-    sigmoid_gate = jax.nn.sigmoid(gate_pre)
-    silu_gate = gate_pre * sigmoid_gate
-    hidden_e = (silu_gate * up_pre).astype(bfloat)
-    expert_out = jnp.einsum("bemf,efd->bemd", hidden_e, w_down, preferred_element_type=single).astype(bfloat)
-    weighted = (pick.astype(single) * row_gates[..., None]).astype(bfloat)
-    combined = jnp.einsum("bemt,bemd->btd", weighted, expert_out, preferred_element_type=single)
-    row_score = jnp.sum(row_final * expert_out.astype(single), axis=-1)
-    scores = jnp.sum(jnp.where(picks, row_score[..., None], 0.0), axis=2)
-    grad_route = (row_gates[..., None] * row_final).astype(bfloat)
-    grad_w_down = jnp.einsum("bemf,bemd->efd", hidden_e, grad_route, preferred_element_type=single)
-    grad_hidden_e = (
-        jnp.einsum("bemd,efd->bemf", grad_route, w_down, preferred_element_type=single)
-        .astype(bfloat)
-        .astype(single)
-    )
-    grad_gate_pre = (
-        grad_hidden_e * up_pre * sigmoid_gate * (1.0 + gate_pre * (1.0 - sigmoid_gate))
-    ).astype(bfloat)
-    grad_up_pre = (grad_hidden_e * silu_gate).astype(bfloat)
-    grad_w_gate = jnp.einsum("bemd,bemf->edf", received, grad_gate_pre, preferred_element_type=single)
-    grad_w_up = jnp.einsum("bemd,bemf->edf", received, grad_up_pre, preferred_element_type=single)
-    grad_rows = jnp.einsum("bemf,edf->bemd", grad_gate_pre, w_gate, preferred_element_type=single)
-    grad_rows = (
-        grad_rows + jnp.einsum("bemf,edf->bemd", grad_up_pre, w_up, preferred_element_type=single)
-    ).astype(bfloat)
-    grad_hidden = jnp.einsum("bemt,bemd->btd", pick, grad_rows, preferred_element_type=single)
-    return combined, grad_hidden, scores, grad_w_gate, grad_w_up, grad_w_down
+    hidden_units = w_gate.shape[2]
+    capacity = picks.shape[1] // local_exp
+    group_rows = 4 * capacity
+    ctx = lax.axis_index("context")
+    z = lax.axis_index("expert")
+    y = ctx // 2
+    c = ctx % 2
+    inner = z + (z // 2) * (3 - 2 * z)
+    UP, DOWN, ACROSS, CORE = 0, 1, 2, 3
+
+    def device(kind):
+        if kind == UP:
+            return {"context": ctx, "expert": z + 1}
+        if kind == DOWN:
+            return {"context": ctx, "expert": z - 1}
+        if kind == ACROSS:
+            return {"context": (1 - y) * 2 + c, "expert": z}
+        return {"context": y * 2 + 1 - c, "expert": z}
+
+    def block_id(yy, cc, zz):
+        return (yy * 2 + cc) * 4 + zz
+
+    def per_side(action):
+        @pl.when(z < 3)
+        def _():
+            action(UP)
+
+        @pl.when(z > 0)
+        def _():
+            action(DOWN)
+
+        action(ACROSS)
+        action(CORE)
+
+    weights = (
+        pltpu.make_async_copy(gate_hbm, w_gate, load_sem.at[0]),
+        pltpu.make_async_copy(up_hbm, w_up, load_sem.at[1]),
+        pltpu.make_async_copy(down_hbm, w_down, load_sem.at[2]),
+    )
+    mine = block_id(y, c, z)
+    own = pltpu.make_async_copy(hidden_ref, held.at[mine], local_sem)
+    own.start()
+    for copy in weights:
+        copy.start()
+
+    barrier = pltpu.get_barrier_semaphore()
+    per_side(
+        lambda kind: pl.semaphore_signal(
+            barrier, inc=1, device_id=device(kind), device_id_type=MESH_ID
+        )
+    )
+    pl.semaphore_wait(barrier, 3 + inner)
+    own.wait()
+
+    def spread(kind, block):
+        return pltpu.make_async_remote_copy(
+            src_ref=held.at[block],
+            dst_ref=held.at[block],
+            send_sem=gather_send.at[kind, block],
+            recv_sem=gather_recv.at[block],
+            device_id=device(kind),
+            device_id_type=MESH_ID,
+        )
+
+    def along(kind, zz):
+        if kind == UP:
+            return jnp.logical_and(z < 3, zz <= z)
+        return jnp.logical_and(z > 0, zz >= z)
+
+    def send_on(zz):
+        block = block_id(y, c, zz)
+        for kind in (UP, DOWN):
+
+            @pl.when(along(kind, zz))
+            def _():
+                spread(kind, block).start()
+
+        spread(ACROSS, block).start()
+        spread(CORE, block).start()
+
+    def forward(step):
+        zz = line_order(z, step)
+        spread(ACROSS, block_id(y, c, zz)).wait_recv()
+        send_on(zz)
+
+    send_on(z)
+    row = lax.broadcasted_iota(jnp.int32, (tokens_block, tokens_block), 0)
+    column = lax.broadcasted_iota(jnp.int32, (tokens_block, tokens_block), 1)
+    before[...] = jnp.where(row < column, 1.0, 0.0).astype(bfloat)
+    for copy in weights:
+        copy.wait()
+    first = (ctx * 4 + z) * local_exp
+
+    def member(zz, p):
+        yy = y + (p // 2) * (1 - 2 * y)
+        cc = c + (p % 2) * (1 - 2 * c)
+        return block_id(yy, cc, zz)
+
+    def load_final(zz, p):
+        return pltpu.make_async_copy(final_ref.at[member(zz, p)], pool.at[p], load_sem.at[p])
+
+    def store_part(zz, p):
+        return pltpu.make_async_copy(pool.at[4 + p], part_ref.at[member(zz, p)], part_sem.at[p])
+
+    def forward_group(step, carry):
+        zz = line_order(z, step)
+        after = step + 1 + inner * jnp.minimum(step, 1)
+
+        @pl.when(after < 4)
+        def _():
+            forward(after)
+
+        @pl.when(jnp.logical_and(step == 0, inner == 1))
+        def _():
+            forward(2)
+
+        @pl.loop(0, 4)
+        def _(p):
+            load_final(zz, p).start()
+
+        spread(CORE, block_id(y, 1 - c, zz)).wait_recv()
+        spread(CORE, block_id(1 - y, c, zz)).wait_recv()
+        spread(CORE, block_id(1 - y, c, zz)).start()
+        spread(CORE, block_id(1 - y, 1 - c, zz)).wait_recv()
+
+        @pl.loop(0, 4)
+        def _(p):
+            block = member(zz, p)
+            tokens_in = held[block]
+            logits = contract_last(router_ref[...], tokens_in)
+            expert_row = lax.broadcasted_iota(jnp.int32, (experts, tokens_block), 0)
+            routed = jnp.zeros((experts, tokens_block), single)
+            for k in range(routes_ref.shape[1]):
+                routed = routed + jnp.where(routes_ref[block, k : k + 1, :] == expert_row, 1.0, 0.0)
+            named = routed > 0.5
+            peak = jnp.max(jnp.where(named, logits, floor_score), axis=0, keepdims=True)
+            raised = jnp.where(named, jnp.exp(jnp.minimum(logits - peak, 0.0)), 0.0)
+            gates = raised / jnp.sum(raised, axis=0, keepdims=True)
+            eight = lax.broadcasted_iota(jnp.int32, (8, tokens_block), 0)
+            masks = jnp.zeros((8, tokens_block), single)
+            own_mask = []
+            own_gate = []
+            for j in range(local_exp):
+                here = expert_row == first + j
+                own_mask.append(jnp.sum(jnp.where(here, routed, 0.0), axis=0, keepdims=True))
+                own_gate.append(jnp.sum(jnp.where(here, gates, 0.0), axis=0, keepdims=True))
+                masks = masks + jnp.where(eight == j, own_mask[j], 0.0)
+            rank = matmul(masks.astype(bfloat), before[...])
+            slot = lax.broadcasted_iota(jnp.int32, (capacity, tokens_block), 0).astype(single)
+            for j in range(local_exp):
+                hit = jnp.logical_and(slot == rank[j : j + 1, :], own_mask[j] > 0.5)
+                pick = jnp.where(hit, 1.0, 0.0)
+                picks[step * 4 + p, pl.ds(j * capacity, capacity), :] = pick.astype(bfloat)
+                gate_column = jnp.sum(pick * own_gate[j], axis=1, keepdims=True)
+                row_gates[p, pl.ds(j * capacity, capacity), :] = jnp.broadcast_to(
+                    gate_column, (capacity, 128)
+                )
+            at = pl.multiple_of(step * group_rows + p * capacity, 32)
+            for n in range(width // CHUNK):
+                part = pl.ds(n * CHUNK, CHUNK)
+                got = matmul(picks[step * 4 + p], held[block, :, part]).astype(bfloat)
+                for j in range(local_exp):
+                    rows_in[j, pl.ds(at, capacity), part] = got[j * capacity : (j + 1) * capacity]
+
+        base = pl.multiple_of(step * group_rows, 128)
+        for j in range(local_exp):
+            given = rows_in[j, pl.ds(base, group_rows), :]
+            for n in range(hidden_units // HALF):
+                part = pl.ds(n * HALF, HALF)
+                gate_pre = matmul(given, w_gate[j, :, part])
+                up_pre = matmul(given, w_up[j, :, part])
+                sigmoid = 1.0 / (1.0 + jnp.exp(-gate_pre))
+                silu = gate_pre * sigmoid
+                hidden_e[j, pl.ds(base, group_rows), part] = (silu * up_pre).astype(bfloat)
+                slope_gate[j, pl.ds(base, group_rows), part] = (
+                    up_pre * sigmoid * (1.0 + gate_pre * (1.0 - sigmoid))
+                ).astype(bfloat)
+                slope_up[j, pl.ds(base, group_rows), part] = silu.astype(bfloat)
+            for n in range(width // CHUNK):
+                part = pl.ds(n * CHUNK, CHUNK)
+                work[j, :, part] = matmul(
+                    hidden_e[j, pl.ds(base, group_rows), :], w_down[j, :, part]
+                ).astype(bfloat)
+
+        @pl.loop(0, 4)
+        def _(p):
+            block = member(zz, p)
+            at = pl.multiple_of(step * group_rows + p * capacity, 32)
+            local = pl.multiple_of(p * capacity, 32)
+            pick = picks[step * 4 + p]
+            weight = row_gates[p][:, 0:1]
+            weighted = (pick.astype(single) * weight).astype(bfloat)
+            load_final(zz, p).wait()
+
+            @pl.when(step > 0)
+            def _():
+                store_part(zz, p).wait()
+
+            row_score = jnp.zeros((local_exp * capacity, 1), single)
+            for n in range(width // CHUNK):
+                part = pl.ds(n * CHUNK, CHUNK)
+                out = jnp.concatenate(
+                    [work[j, pl.ds(local, capacity), part] for j in range(local_exp)], axis=0
+                )
+                pool[4 + p, :, part] = contract_rows(weighted, out).astype(bfloat)
+                final = matmul(pick, pool[p, :, part])
+                row_score = row_score + jnp.sum(final * out.astype(single), axis=1, keepdims=True)
+                graded = (final * weight).astype(bfloat)
+                for j in range(local_exp):
+                    rows_grad[j, pl.ds(at, capacity), part] = graded[j * capacity : (j + 1) * capacity]
+            store_part(zz, p).start()
+            spread_score = pick.astype(single) * row_score
+            eight = lax.broadcasted_iota(jnp.int32, (8, tokens_block), 0)
+            scores = jnp.zeros((8, tokens_block), single)
+            for j in range(local_exp):
+                total = jnp.sum(spread_score[j * capacity : (j + 1) * capacity], axis=0, keepdims=True)
+                scores = scores + jnp.where(eight == j, total, 0.0)
+            score_ref[block] = scores
+
+        return carry
+
+    lax.fori_loop(0, 4, forward_group, 0)
+
+    @pl.loop(0, 4)
+    def _(p):
+        store_part(line_order(z, 3), p).wait()
+
+    @pl.loop(0, 4)
+    def _(zz):
+        block = block_id(y, c, zz)
+        for kind in (UP, DOWN):
+
+            @pl.when(along(kind, zz))
+            def _():
+                spread(kind, block).wait_send()
+
+        spread(ACROSS, block).wait_send()
+        spread(CORE, block).wait_send()
+        spread(CORE, block_id(1 - y, c, zz)).wait_send()
+
+    opposite = {UP: DOWN, DOWN: UP, ACROSS: ACROSS, CORE: CORE}
+    per_side(
+        lambda kind: pl.semaphore_signal(
+            ready.at[opposite[kind]], inc=1, device_id=device(kind), device_id_type=MESH_ID
+        )
+    )
+    per_side(lambda kind: pl.semaphore_wait(ready.at[kind], 1))
+
+    def to_core(p, zz):
+        yy = y + p * (1 - 2 * y)
+        return pltpu.make_async_remote_copy(
+            src_ref=pool.at[p],
+            dst_ref=held.at[yy * 4 + zz],
+            send_sem=sum_send.at[p],
+            recv_sem=core_recv.at[yy * 4 + zz],
+            device_id=device(CORE),
+            device_id_type=MESH_ID,
+        )
+
+    def from_core(slot):
+        return pltpu.make_async_remote_copy(
+            src_ref=pool.at[0],
+            dst_ref=held.at[slot],
+            send_sem=sum_send.at[0],
+            recv_sem=core_recv.at[slot],
+            device_id=device(CORE),
+            device_id_type=MESH_ID,
+        )
+
+    def to_across(turn, zz):
+        return pltpu.make_async_remote_copy(
+            src_ref=pool.at[2 + turn],
+            dst_ref=held.at[8 + zz],
+            send_sem=sum_send.at[2 + turn],
+            recv_sem=y_recv.at[zz],
+            device_id=device(ACROSS),
+            device_id_type=MESH_ID,
+        )
+
+    def to_line(kind, turn, zz, last):
+        return pltpu.make_async_remote_copy(
+            src_ref=pool.at[4 + turn],
+            dst_ref=pool.at[7] if last else held.at[12 + zz],
+            send_sem=sum_send.at[4 + turn],
+            recv_sem=z_recv.at[4 if last else zz],
+            device_id=device(kind),
+            device_id_type=MESH_ID,
+        )
+
+    def summed(*refs):
+        total = refs[0].astype(single)
+        for value in refs[1:]:
+            total = total + value.astype(single)
+        return total.astype(bfloat)
+
+    def back_block(step, p, target):
+        local = pl.multiple_of(p * capacity, 32)
+        pick = picks[step * 4 + p]
+        for n in range(width // CHUNK):
+            part = pl.ds(n * CHUNK, CHUNK)
+            grads = jnp.concatenate(
+                [work[j, pl.ds(local, capacity), part] for j in range(local_exp)], axis=0
+            )
+            pool[target, :, part] = contract_rows(pick, grads).astype(bfloat)
+
+    def line_sum(step):
+        zz = line_order(z, step)
+        turn = step % 2
+        core_slot = y * 4 + zz
+        to_across(turn, zz).wait_recv()
+        rising = zz > z
+
+        def finish(comes):
+            @pl.when(comes)
+            def _():
+                to_line(CORE, turn, zz, False).wait_recv()
+                pool[4 + turn] = summed(
+                    pool[4 + turn], held[core_slot], held[8 + zz], held[12 + zz]
+                )
+
+            @pl.when(jnp.logical_not(comes))
+            def _():
+                pool[4 + turn] = summed(pool[4 + turn], held[core_slot], held[8 + zz])
+
+        @pl.when(rising)
+        def _():
+            finish(z > 0)
+            to_line(UP, turn, zz, False).start()
+
+        @pl.when(jnp.logical_not(rising))
+        def _():
+            finish(z < 3)
+
+            @pl.when(zz == z - 1)
+            def _():
+                to_line(DOWN, turn, zz, True).start()
+
+            @pl.when(zz < z - 1)
+            def _():
+                to_line(DOWN, turn, zz, False).start()
+
+    def backward_group(turn_step, carry):
+        step = 3 - turn_step
+        zz = line_order(z, step)
+        turn = step % 2
+        base = pl.multiple_of(step * group_rows, 128)
+        for j in range(local_exp):
+            for n in range(hidden_units // HALF):
+                part = pl.ds(n * HALF, HALF)
+                grad_hidden = (
+                    contract_last(rows_grad[j, pl.ds(base, group_rows), :], w_down[j, part, :])
+                    .astype(bfloat)
+                    .astype(single)
+                )
+                slope_gate[j, pl.ds(base, group_rows), part] = (
+                    grad_hidden * slope_gate[j, pl.ds(base, group_rows), part].astype(single)
+                ).astype(bfloat)
+                slope_up[j, pl.ds(base, group_rows), part] = (
+                    grad_hidden * slope_up[j, pl.ds(base, group_rows), part].astype(single)
+                ).astype(bfloat)
+            for n in range(width // CHUNK):
+                part = pl.ds(n * CHUNK, CHUNK)
+                work[j, :, part] = (
+                    contract_last(slope_gate[j, pl.ds(base, group_rows), :], w_gate[j, part, :])
+                    + contract_last(slope_up[j, pl.ds(base, group_rows), :], w_up[j, part, :])
+                ).astype(bfloat)
+        for p, member_p in ((0, 1), (1, 3)):
+
+            @pl.when(turn_step > 0)
+            def _():
+                to_core(p, zz).wait_send()
+
+            back_block(step, member_p, p)
+            to_core(p, zz).start()
+
+        @pl.when(turn_step > 1)
+        def _():
+            to_across(turn, zz).wait_send()
+            to_line(CORE, turn, zz, False).wait_send()
+
+        back_block(step, 2, 2 + turn)
+        other = (1 - y) * 4 + zz
+        from_core(other).wait_recv()
+        pool[2 + turn] = summed(pool[2 + turn], held[other])
+        to_across(turn, zz).start()
+        back_block(step, 0, 4 + turn)
+        from_core(y * 4 + zz).wait_recv()
+
+        @pl.when(jnp.logical_and(turn_step > 0, turn_step < 3))
+        def _():
+            line_sum(step + 1)
+
+        return carry
+
+    lax.fori_loop(0, 4, backward_group, 0)
+
+    def stores(j):
+        return (
+            pltpu.make_async_copy(w_gate.at[j], grad_gate_ref.at[j], load_sem.at[3 * j]),
+            pltpu.make_async_copy(w_up.at[j], grad_up_ref.at[j], load_sem.at[3 * j + 1]),
+            pltpu.make_async_copy(w_down.at[j], grad_down_ref.at[j], load_sem.at[3 * j + 2]),
+        )
+
+    def weight_grads(j):
+        @pl.loop(0, width // CHUNK)
+        def _(n):
+            part = pl.ds(pl.multiple_of(n * CHUNK, CHUNK), CHUNK)
+            w_gate[j, part, :] = contract_rows(rows_in[j, :, part], slope_gate[j]).astype(bfloat)
+            w_up[j, part, :] = contract_rows(rows_in[j, :, part], slope_up[j]).astype(bfloat)
+            w_down[j, :, part] = contract_rows(hidden_e[j], rows_grad[j, :, part]).astype(bfloat)
+
+        for copy in stores(j):
+            copy.start()
+
+    weight_grads(0)
+    line_sum(1)
+    weight_grads(1)
+    to_across(0, z).wait_recv()
+    pool[4] = summed(pool[4], held[y * 4 + z], held[8 + z])
+
+    @pl.when(z > 0)
+    def _():
+        to_line(CORE, 0, z, False).wait_recv()
+        pool[4] = summed(pool[4], held[12 + z])
+
+    @pl.when(z < 3)
+    def _():
+        to_line(CORE, 0, z, True).wait_recv()
+        pool[4] = summed(pool[4], pool[7])
+
+    result = pltpu.make_async_copy(pool.at[4], back_ref, local_sem)
+    result.start()
+    for j in range(local_exp):
+        for copy in stores(j):
+            copy.wait()
+    for p in range(2):
+        to_core(p, z).wait_send()
+        to_across(p, z).wait_send()
+    to_line(CORE, 1, z, False).wait_send()
+    result.wait()
+
+
+def experts_on_owner(hidden, final_all, routes_all, router_rows, w_gate, w_up, w_down, capacity):
+    blocks = final_all.shape[0]
+    tokens_block, width = hidden.shape
+    local_exp, _, units = w_gate.shape
+    bfloat = jnp.bfloat16
+    single = jnp.float32
+    rows = blocks * capacity
+    anywhere = pl.BlockSpec(memory_space=pl.ANY)
+    vmem = pl.BlockSpec(memory_space=pltpu.VMEM)
+    dma = pltpu.SemaphoreType.DMA
+    return pl.pallas_call(
+        experts_kernel,
+        out_shape=(
+            jax.ShapeDtypeStruct((tokens_block, width), bfloat),
+            jax.ShapeDtypeStruct((blocks, tokens_block, width), bfloat),
+            jax.ShapeDtypeStruct((blocks, 8, tokens_block), single),
+            jax.ShapeDtypeStruct(w_gate.shape, bfloat),
+            jax.ShapeDtypeStruct(w_up.shape, bfloat),
+            jax.ShapeDtypeStruct(w_down.shape, bfloat),
+        ),
+        in_specs=[anywhere, anywhere, vmem, vmem, anywhere, anywhere, anywhere],
+        out_specs=(anywhere, anywhere, vmem, anywhere, anywhere, anywhere),
+        scratch_shapes=[
+            pltpu.VMEM((blocks, tokens_block, width), bfloat),
+            pltpu.VMEM(w_gate.shape, bfloat),
+            pltpu.VMEM(w_up.shape, bfloat),
+            pltpu.VMEM(w_down.shape, bfloat),
+            pltpu.VMEM((local_exp, rows, width), bfloat),
+            pltpu.VMEM((local_exp, rows, width), bfloat),
+            pltpu.VMEM((local_exp, rows, units), bfloat),
+            pltpu.VMEM((local_exp, rows, units), bfloat),
+            pltpu.VMEM((local_exp, rows, units), bfloat),
+            pltpu.VMEM((blocks, local_exp * capacity, tokens_block), bfloat),
+            pltpu.VMEM((4, local_exp * capacity, 128), single),
+            pltpu.VMEM((local_exp, 4 * capacity, width), bfloat),
+            pltpu.VMEM((8, tokens_block, width), bfloat),
+            pltpu.VMEM((tokens_block, tokens_block), bfloat),
+            dma((4, blocks)),
+            dma((blocks,)),
+            dma,
+            dma((6,)),
+            dma((4,)),
+            dma((6,)),
+            dma((8,)),
+            dma((4,)),
+            dma((5,)),
+            pltpu.SemaphoreType.REGULAR((4,)),
+        ],
+        compiler_params=pltpu.CompilerParams(
+            collective_id=1, has_side_effects=True, vmem_limit_bytes=63 * 2**20
+        ),
+        name="experts",
+    )(hidden, final_all, routes_all, router_rows, w_gate, w_up, w_down)
 
 
 def on_device(
@@ -223,13 +734,12 @@
     gates = jax.nn.softmax(chosen, axis=-1)
     final_low = (cotangent.astype(single) * valid).astype(bfloat)
     final_all = lax.all_gather(final_low[0], GROUP, axis=0, tiled=False)
-    routes_all = lax.all_gather(routes[0], GROUP, axis=0, tiled=False)
-    hidden_all = lax.all_gather(hidden_two[0], GROUP, axis=0, tiled=False)
-    combined, grad_hidden, scores, grad_w_gate, grad_w_up, grad_w_down = experts_on_owner(
-        hidden_all, final_all, routes_all, router_w, w_gate, w_up, w_down, capacity
-    )
-    combined = lax.psum_scatter(combined.astype(bfloat), GROUP, scatter_dimension=0, tiled=False)
-    grad_hidden = lax.psum_scatter(grad_hidden.astype(bfloat), GROUP, scatter_dimension=0, tiled=False)
+    routes_all = lax.all_gather(routes[0].T, GROUP, axis=0, tiled=False)
+    grad_hidden, combined, scores, grad_w_gate, grad_w_up, grad_w_down = experts_on_owner(
+        hidden_two[0], final_all, routes_all, router_w.T, w_gate, w_up, w_down, capacity
+    )
+    combined = lax.psum_scatter(combined, GROUP, scatter_dimension=0, tiled=False)
+    scores = scores[:, :local_exp]
     scores = lax.all_to_all(scores, GROUP, split_axis=0, concat_axis=0, tiled=True)
     scores = scores.reshape(experts, sequence_per_device)
     block_out = (valid * (resid + combined.astype(single)[None])).astype(bfloat)

time: 1300 us -> 1140 us (0.88)
  Pallas kernels: 0 us -> 197 us
  waiting for transfers between devices: 795 us -> 627 us
  matrix products: 281 us -> 118 us
  other arithmetic: 68.6 us -> 54.2 us
    pallas_call x0 -> x1, Pallas kernels: none -> 197 us  [experts_on_owner(): pl.pallas_call(experts_kernel, out_shape=(jax.ShapeDtypeStruct((tokens_bl...]
    dot_general x14 -> x0, matrix products: 162 us -> none  [the longest x1 16.1 us: experts_on_owner(): jnp.einsum('bemd,efd->bemf', grad_route, w_down, preferred_element_type=s...]
    reduce_scatter x2 -> x1, waiting for transfers between devices: 245 us -> 116 us  [on_device(): lax.psum_scatter(combined, GROUP, scatter_dimension=0, tiled=False)]
    all_gather x1 -> x0, waiting for transfers between devices: 87.1 us -> none  [on_device(): hidden_all = lax.all_gather(hidden_two[0], GROUP, axis=0, tiled=False)]
    all_gather x1, waiting for transfers between devices: 61.2 us -> 96.3 us  [on_device(): final_all = lax.all_gather(final_low[0], GROUP, axis=0, tiled=False)]
    reduce_scatter x1, waiting for transfers between devices: 1.49 us -> 32.3 us  [on_device(): lax.psum_scatter(grad_w_up.astype(jnp.bfloat16), 'dp', scatter_dimension=...]
    all_gather x1, waiting for transfers between devices: 29.2 us -> 3.31 us  [on_device(): out_w = lax.all_gather(w_out, EVERY, axis=0, tiled=True)]
    unnamed x16 -> x14, waiting for transfers between devices: 134 us -> 136 us
  transfers between devices with their start and end apart: 16 -> 14, of which waited for: 12 -> 10; matrix products, arithmetic and copies ran while one was open for 19% -> 16% of each run, Pallas kernels for 0% -> 0%
where the time goes in v1:
time: 1140 us
  waiting for transfers between devices  627 us (55%)
  Pallas kernels  197 us (17%)
  matrix products  118 us (10%)
  local copies, waits for them, and re-layouts  84.4 us (7%)
  other arithmetic  54.2 us (5%)
  blocking collectives  35 us (3%)
  between operations  15.4 us (1%)
    pallas_call x1, Pallas kernels, experts_on_owner(): pl.pallas_call(experts_kernel, out_shape=(jax.ShapeDtypeStruct((tokens_bl...  197 us
    unnamed x14, waiting for transfers between devices  136 us
    reduce_scatter x1, waiting for transfers between devices, on_device(): lax.psum_scatter(combined, GROUP, scatter_dimension=0, tiled=False)  116 us
    reduce_scatter x1, waiting for transfers between devices, on_device(): lax.psum_scatter(grad_w_out.astype(bfloat), EVERY, scatter_dimension=0, t...  108 us
    all_gather x1, waiting for transfers between devices, on_device(): final_all = lax.all_gather(final_low[0], GROUP, axis=0, tiled=False)  96.3 us
    all_gather x1, waiting for transfers between devices, on_device(): early = lax.all_gather(early, EVERY, axis=0, tiled=True)  78.2 us
    reduce_scatter x1, waiting for transfers between devices, on_device(): lax.psum_scatter(grad_w_gate.astype(jnp.bfloat16), 'dp', scatter_dimensio...  42.1 us
    concatenate x1, local copies, waits for them, and re-layouts, on_device(): jnp.concatenate([grad_w_query, grad_w_key, grad_w_value, grad_w_router, g...  36.3 us
  transfers between devices with their start and end apart: 14, of which 10 were waited for; matrix products, arithmetic and copies ran while one was open for 16% of the time, Pallas kernels for 0%

profile of v1, /device:TPU:0, one launch (start us, length us, event | category | flops | bytes accessed | tf_op | source)
XLA Modules:
  0.0 1135.7 jit_solution(3373474299476171575)
XLA Ops:
  9.6 1.7 concatenate.46
  12.8 78.2 %all-gather.8.cloned.1.call-done = bf16[1536,2594]{1,0:T(8,128)(2,1)} async-done(((bf16[48,2594]{1,0:T(8,128)(2,1)}), bf16[1536,2594]{1,0:T(8,128)(2,1)}) %all-gather.8.cloned.1.call-update) | async-done | bytes 7968784 | tf_op jit(solution)/shard_map/all_gather | solution.py:653
  91.0 1.7 convert_reduce_fusion
  92.7 2.7 fusion.37
  97.3 1.6 copy.98
  98.9 2.1 convolution_bitcast_fusion.2
  104.3 35.0 %all-gather.1 = s32[128,256]{1,0:T(8,128)} all-gather(s32[8,256]{1,0:T(8,128)S(1)} %bitcast.191), channel_id=3, replica_groups=mesh['dp'=2,'context'=4,'expert'=4] {'context','expert'}, dimensions={0}, use_global_device_ids=true | all-gather | bytes 139264 | tf_op jit(solution)/shard_map/all_gather | solution.py:737
  140.4 4.9 slice_bitcast_fusion
  145.3 6.7 copy.99
  152.0 3.9 convolution_bitcast_fusion.1
  156.2 2.5 copy.97
  158.7 11.5 %fusion.9 = (f32[8,3,256]{2,1,0:T(4,128)S(1)}, f32[8,1024,256,3]{2,1,3,0:T(8,128)}) fusion(pred[256,1024]{0,1:T(8,128)(4,1)S(1)} %fusion.40, bf16[1024,8,64,1]{0,2,3,1:T(8,128)(2,1)} %bitcast.167, bf16[256,8,3,32]{0,3,2,1:T(8,128)(2,1)S(1)} %bitcast.176, bf16[256,8,3,32]{0,3,2,1:T(8,128)(2,1)S(1)} %bitcast.174), kind=kOutput, calls=%fused_computation.14 | convolution fusion | flops 825747456 | bytes 27287552 | tf_op jit(solution)/shard_map/skrd,tkd->krst/dot_general | solution.py:706
  170.2 11.1 fusion.3
  181.4 11.7 %fusion.32 = bf16[8,64,3,256]{3,1,2,0:T(8,128)(2,1)S(1)} fusion(bf16[1024,8,64,1]{0,2,3,1:T(8,128)(2,1)S(1)} %bitcast.181, f32[8,3,256]{2,1,0:T(4,128)S(1)} %fusion.3, f32[8,3,256]{2,1,0:T(4,128)S(1)} %get-tuple-element.108, f32[8,1024,256,3]{2,1,3,0:T(8,128)} %get-tuple-element.109, pred[256,1024]{0,1:T(8,128)(4,1)S(1)} %fusion.40), kind=kOutput, calls=%fused_computation.60 | convolution fusion | flops 837156864 | bytes 27312128 | tf_op jit(solution)/shard_map/krst,tkd->skrd/dot_general | solution.py:721
  193.1 3.3 all-gather.12.cloned.1.call-done
  196.4 3.8 multiply_reduce_fusion
  202.5 96.3 %all-gather.14.cloned.1.call-done.final_ref = bf16[16,256,1536]{2,1,0:T(8,128)(2,1)} async-done(((bf16[1,256,1536]{2,1,0:T(8,128)(2,1)}), bf16[16,256,1536]{2,1,0:T(8,128)(2,1)}) %all-gather.14.cloned.1.call-update) | async-done | bytes 12582928 | tf_op jit(solution)/shard_map/all_gather | solution.py:736
  298.8 197.2 %experts.1 = (bf16[256,1536]{1,0:T(8,128)(2,1)}, bf16[16,256,1536]{2,1,0:T(8,128)(2,1)}, f32[16,8,256]{2,1,0:T(8,128)}, bf16[2,1536,512]{2,1,0:T(8,128)(2,1)}, b...) custom-call(bf16[256,1536]{1,0:T(8,128)(2,1)} %fusion.41.hidden_ref, ...), custom_call_target="tpu_custom_call" | custom-call | tf_op jit(solution)/shard_map/experts/pallas_call | solution.py:578
  500.2 3.6 all-to-all-start
  504.3 6.0 all-to-all-done
  510.6 3.3 fusion.27
  513.9 116.0 %reduce-scatter.11.cloned.1.call-done = bf16[1,256,1536]{2,1,0:T(8,128)(2,1)} async-done(((bf16[16,256,1536]{2,1,0:T(8,128)(2,1)}), bf16[1,256,1536]{2,1,0:T(8,128)(2,1)}) %reduce-scatter.11.cloned.1.call-update) | async-done | bytes 786448 | tf_op jit(solution)/shard_map/reduce_scatter | solution.py:741
  629.9 3.1 fusion.30
  634.1 4.6 convolution_convert_fusion.4
  640.3 21.8 %fusion = (f32[8,3,256]{2,1,0:T(4,128)S(1)}, f32[8,1024,256,3]{2,1,3,0:T(8,128)}) fusion(f32[8,3,256]{2,1,0:T(4,128)S(1)} %log_add_fusion, pred[256,1024]{0,1:T(8,128)(4,1)S(1)} %fusion.40, f32[8,1024,256,3]{2,1,3,0:T(8,128)} %get-tuple-element.109, bf16[1024,8,64,1]{0,2,3,1:T(8,128)(2,1)S(1)} %bitcast.182, bf16[256,8,3,64]{0,3,2,1:T(8,128)(2,1)S(1)} %bitcast.185), kind=kOutput, calls=%fused_computation.2 | convolution fusion | flops 843048960 | bytes 52477952 | tf_op jit(solution)/shard_map/skrd,tkd->krst/dot_general | solution.py:772
  662.1 17.4 %fusion.2 = bf16[8,3,256,1024]{2,3,1,0:T(8,128)(2,1)S(1)} fusion(f32[8,1024,256,3]{2,1,3,0:T(8,128)} %get-tuple-element.114, f32[8,3,256]{2,1,0:T(4,128)S(1)} %get-tuple-element.113, f32[8,3,256]{2,1,0:T(4,128)S(1)} %log_add_fusion, pred[256,1024]{0,1:T(8,128)(4,1)} %copy-done.12, f32[8,1024,256,3]{2,1,3,0:T(8,128)} %get-tuple-element.109), kind=kLoop, calls=%fused_computation.4 | loop fusion | flops 44040192 | bytes 63225856 | tf_op jit(solution)/shard_map/convert_element_type | solution.py:776
  679.6 6.6 fusion.17
  686.5 13.0 %bitcast_convert_fusion = bf16[8,64,1024]{2,1,0:T(8,128)(2,1)} fusion(bf16[256,8,3,64]{0,3,2,1:T(8,128)(2,1)} %bitcast.186, f32[8,3,256]{2,1,0:T(4,128)S(1)} %log_add_fusion, pred[256,1024]{0,1:T(8,128)(4,1)S(1)} %copy-done.13, f32[8,1024,256,3]{2,1,3,0:T(8,128)} %get-tuple-element.109), kind=kOutput, calls=%fused_computation.35 | convolution fusion | flops 837287936 | bytes 27287552 | tf_op jit(solution)/shard_map/krst,skrd->tkd/dot_general | solution.py:792
  702.6 3.5 convolution_convert_fusion.1
  708.2 6.8 convolution_multiply_fusion
  716.2 3.6 convolution_convert_fusion
  719.8 5.2 fusion.10
  726.5 3.2 convolution_add_fusion.2
  729.7 8.9 reduce-scatter.15.cloned.1.call-done
  738.6 4.0 fusion.25
  742.7 1.8 convolution_convert_fusion.3
  744.5 1.8 convolution_convert_fusion.2
  746.3 36.3 %concatenate.53 = bf16[1536,2594]{0,1:T(8,128)(2,1)} concatenate(bf16[1536,1536]{0,1:T(8,128)(2,1)} %convolution_convert_fusion, bf16[1536,512]{0,1:T(8,128)(2,1)} %convolution_convert_fusion.3, bf16[1536,512]{0,1:T(8,128)(2,1)} %convolution_convert_fusion.2, bf16[1536,32]{0,1:T(8,128)(2,1)S(1)} %copy-done.27, bf16[1536,1]{0,1:T(2,128)(2,1)S(1)} %broadcast_in_dim.97, ...), dimensions={1} | concatenate | bytes 15937536 | tf_op jit(solution)/shard_map/concatenate | solution.py:839
  782.6 11.4 %copy.117 = bf16[1536,2594]{1,0:T(8,128)(2,1)} copy(bf16[1536,2594]{0,1:T(8,128)(2,1)} %concatenate.53) | data formatting | bytes 15937536
  794.0 3.5 convert_element_type.280
  797.5 32.3 %reduce-scatter.21.cloned.1.call-done = bf16[2,768,512]{2,1,0:T(8,128)(2,1)} async-done(((bf16[2,1536,512]{2,1,0:T(8,128)(2,1)}), bf16[2,768,512]{2,1,0:T(8,128)(2,1)}) %reduce-scatter.21.cloned.1.call-update) | async-done | bytes 1572880 | tf_op jit(solution)/shard_map/reduce_scatter | solution.py:869
  829.8 3.5 convert_element_type.279
  833.4 42.1 %reduce-scatter.19.cloned.1.call-done = bf16[2,768,512]{2,1,0:T(8,128)(2,1)} async-done(((bf16[2,1536,512]{2,1,0:T(8,128)(2,1)}), bf16[2,768,512]{2,1,0:T(8,128)(2,1)}) %reduce-scatter.19.cloned.1.call-update) | async-done | bytes 1572880 | tf_op jit(solution)/shard_map/reduce_scatter | solution.py:866
  875.5 3.6 convert_element_type.278
  879.1 1.6 fusion.24
  880.7 108.0 %reduce-scatter.17.cloned.1.call-done = bf16[48,1536]{1,0:T(8,128)(2,1)} async-done(((bf16[1536,1536]{1,0:T(8,128)(2,1)}), bf16[48,1536]{1,0:T(8,128)(2,1)}) %reduce-scatter.17.cloned.1.call-update) | async-done | bytes 147472 | tf_op jit(solution)/shard_map/reduce_scatter | solution.py:851
  988.7 1.6 convert_element_type.277
  990.4 133.5 %reduce-scatter.25.cloned.1.call-done = bf16[48,2594]{1,0:T(8,128)(2,1)} async-done(((bf16[1536,2594]{1,0:T(8,128)(2,1)}), bf16[48,2594]{1,0:T(8,128)(2,1)}) %reduce-scatter.25.cloned.1.call-update) | async-done | bytes 249040
  (150 shorter events, 32.3 us)
Async XLA Ops:
  7.2 85.5 %copy-start.1 = (bf16[1,256,1536]{2,1,0:T(8,128)(2,1)S(1)}, bf16[1,256,1536]{2,1,0:T(8,128)(2,1)}, u32[]{:S(2)}) copy-start(bf16[1,256,1536]{2,1,0:T(8,128)(2,1)} %param.14) | copy-start | bytes 2359300
  7.2 83.8 %all-gather.8.cloned.1.call-start = ((), (), s32[]{:S(2)}) async-start(), calls=%async_computation.9 | async-start | bytes 8515584 | tf_op jit(solution)/shard_map/all_gather | solution.py:653
  11.3 144.8 %all-gather.16.cloned.1.call-start = ((), (), s32[]{:S(2)}) async-start(), calls=%async_computation.20 | async-start | bytes 1310720 | tf_op jit(solution)/shard_map/all_gather | solution.py:698
  12.8 139.2 %copy-start.32 = (f32[256]{0:T(256)}, f32[256]{0:T(256)S(1)}, u32[]{:S(2)}) copy-start(f32[256]{0:T(256)S(1)} %add_rsqrt_fusion.1) | copy-start | bytes 3076
  92.7 59.3 %copy-start.29 = (f32[1536]{0:T(1024)}, f32[1536]{0:T(1024)S(1)}, u32[]{:S(2)}) copy-start(f32[1536]{0:T(1024)S(1)} %get-tuple-element.85) | copy-start | bytes 18436
  95.5 63.2 %all-gather.10.cloned.1.call-start = ((), (), s32[]{:S(2)}) async-start(), calls=%async_computation.10 | async-start | bytes 1310720 | tf_op jit(solution)/shard_map/all_gather | solution.py:697
  95.8 60.1 %copy-start.22 = (f32[256,32]{0,1:T(8,128)}, f32[256,32]{0,1:T(8,128)S(1)}, u32[]{:S(2)}) copy-start(f32[256,32]{0,1:T(8,128)S(1)} %get-tuple-element.106) | copy-start | bytes 98308
  95.8 60.1 %copy-start.24 = (f32[256,32]{0,1:T(8,128)}, f32[256,32]{0,1:T(8,128)S(1)}, u32[]{:S(2)}) copy-start(f32[256,32]{0,1:T(8,128)S(1)} %get-tuple-element.107) | copy-start | bytes 98308
  101.0 2.1 copy-start.16
  101.1 3.2 copy-start.31
  101.9 94.6 %all-gather.12.cloned.1.call-start = ((), (), s32[]{:S(2)}) async-start(), calls=%async_computation.11 | async-start | bytes 4866048 | tf_op jit(solution)/shard_map/all_gather | solution.py:654
  102.4 196.3 %all-gather.14.cloned.1.call-start = ((), (), s32[]{:S(2)}) async-start(), calls=%async_computation.12 | async-start | bytes 13369344 | tf_op jit(solution)/shard_map/all_gather | solution.py:736
  103.2 36.5 %slice-start = ((bf16[1536,2594]{1,0:T(8,128)(2,1)}), bf16[1536,32]{1,0:T(8,128)(2,1)S(1)}, s32[]{:S(2)}) async-start(bf16[1536,2594]{1,0:T(8,128)(2,1)} %all-gather.8.cloned.1.call-done), calls=%async_computation.22 | async-start | bytes 786432
  104.3 525.6 %reduce-scatter.11.cloned.1.call-start = ((), (), s32[]{:S(2)}) async-start(), calls=%async_computation.13 | async-start | bytes 13369344 | tf_op jit(solution)/shard_map/reduce_scatter | solution.py:741
  139.6 500.7 %copy-start.12 = (pred[256,1024]{0,1:T(8,128)(4,1)}, pred[256,1024]{0,1:T(8,128)(4,1)S(1)}, u32[]{:S(2)}) copy-start(pred[256,1024]{0,1:T(8,128)(4,1)S(1)} %fusion.40) | copy-start | bytes 786436
  156.1 14.1 %copy-start.14 = (bf16[1,256,24,32]{1,3,2,0:T(8,128)(2,1)}, bf16[1,256,24,32]{1,3,2,0:T(8,128)(2,1)S(1)}, u32[]{:S(2)}) copy-start(bf16[1,256,24,32]{1,3,2,0:T(8,128)(2,1)S(1)} %get-tuple-element.94) | copy-start | bytes 1179652
  156.1 14.1 %copy-start.15 = (bf16[1,256,24,32]{1,3,2,0:T(8,128)(2,1)}, bf16[1,256,24,32]{1,3,2,0:T(8,128)(2,1)S(1)}, u32[]{:S(2)}) copy-start(bf16[1,256,24,32]{1,3,2,0:T(8,128)(2,1)S(1)} %get-tuple-element.95) | copy-start | bytes 1179652
  170.2 11.2 copy-start.20
  193.1 7.1 copy-start.9
  200.3 1.1 copy-start.3
  496.0 1.1 copy-start.7
  497.2 13.4 %copy-start.4 = (f32[1,256,1536]{2,1,0:T(8,128)S(1)}, f32[1,256,1536]{2,1,0:T(8,128)}, u32[]{:S(2)}) copy-start(f32[1,256,1536]{2,1,0:T(8,128)} %copy-done.3) | copy-start | bytes 4718596
  500.2 10.1 all-to-all-start
  503.8 221.2 %reduce-scatter.13.cloned.1.call-start = ((), (), s32[]{:S(2)}) async-start(), calls=%async_computation.14 | async-start | bytes 1310720 | tf_op jit(solution)/shard_map/reduce_scatter | solution.py:797
  510.5 119.3 %copy-start.17 = (bf16[1,256,1536]{2,1,0:T(8,128)(2,1)S(1)}, bf16[1,256,1536]{2,1,0:T(8,128)(2,1)}, u32[]{:S(2)}) copy-start(bf16[1,256,1536]{2,1,0:T(8,128)(2,1)} %param.27) | copy-start | bytes 2359300
  633.0 1.1 copy-start.5
  638.8 1.5 copy-start.21
  640.3 21.9 %copy-start.26 = (bf16[256,1536]{0,1:T(8,128)(2,1)}, bf16[256,1536]{0,1:T(8,128)(2,1)S(1)}, u32[]{:S(2)}) copy-start(bf16[256,1536]{0,1:T(8,128)(2,1)S(1)} %copy.102) | copy-start | bytes 2359300
  679.6 6.6 copy-start
  679.6 6.9 copy-start.13
  686.3 52.4 %reduce-scatter.15.cloned.1.call-start = ((), (), s32[]{:S(2)}) async-start(), calls=%async_computation.15 | async-start | bytes 1310720 | tf_op jit(solution)/shard_map/reduce_scatter | solution.py:800
  699.5 94.5 %reduce-scatter.23.cloned.1.call-start = ((), (), s32[]{:S(2)}) async-start(), calls=%async_computation.19 | async-start | bytes 4718592 | tf_op jit(solution)/shard_map/reduce_scatter | solution.py:872
  700.2 129.6 %reduce-scatter.21.cloned.1.call-start = ((), (), s32[]{:S(2)}) async-start(), calls=%async_computation.18 | async-start | bytes 4718592 | tf_op jit(solution)/shard_map/reduce_scatter | solution.py:869
  700.8 174.6 %reduce-scatter.19.cloned.1.call-start = ((), (), s32[]{:S(2)}) async-start(), calls=%async_computation.17 | async-start | bytes 4718592 | tf_op jit(solution)/shard_map/reduce_scatter | solution.py:866
  700.9 1.6 copy-start.6
  700.9 1.8 copy-start.10
  701.6 287.2 %reduce-scatter.17.cloned.1.call-start = ((), (), s32[]{:S(2)}) async-start(), calls=%async_computation.16 | async-start | bytes 4866048 | tf_op jit(solution)/shard_map/reduce_scatter | solution.py:851
  706.1 1.1 copy-start.8
  706.2 2.0 copy-start.11
  706.2 417.7 %reduce-scatter.25.cloned.1.call-start = ((), (), s32[]{:S(2)}) async-start(), calls=%async_computation.21 | async-start | bytes 8515584
  708.2 6.8 copy-start.23
  708.2 6.8 copy-start.25
  715.0 1.1 copy-start.2
  715.0 1.1 copy-start.30
  725.0 1.5 copy-start.18
  742.7 1.8 copy-start.28
  744.5 1.8 copy-start.27
  875.5 3.6 copy-start.19
  (1 other events, 1.1 us)
Sparse Core Ops, SparseCore 0:
  11.5 79.4 all-gather.7
  95.6 15.3 all-gather.15
  113.1 17.0 all-gather.9
  132.9 63.5 all-gather.11
  199.2 99.5 all-gather.13
  496.2 133.6 reduce-scatter.10
  686.4 24.0 reduce-scatter.12
  713.7 24.8 reduce-scatter.14
  740.9 43.3 reduce-scatter.22
  786.5 43.3 reduce-scatter.20
  832.1 43.3 reduce-scatter.18
  881.7 106.9 reduce-scatter.16
  994.6 129.2 reduce-scatter.24

commit v2 on v1

--- a/solution.py
+++ b/solution.py
@@ -57,6 +57,7 @@
 MESH_ID = pl.DeviceIdType.MESH
 CHUNK = 512
 HALF = 256
+UP, DOWN, ACROSS, CORE, DP = 0, 1, 2, 3, 4
 
 
 def contract_rows(left, right):
@@ -76,6 +77,488 @@
     inner = z + half * (3 - 2 * z)
     base = step + inner * (1 - 2 * step) * (1 - step // 2)
     return base + half * (3 - 2 * base)
+
+
+def place():
+    ctx = lax.axis_index("context")
+    z = lax.axis_index("expert")
+    y = ctx // 2
+    c = ctx % 2
+    inner = z + (z // 2) * (3 - 2 * z)
+
+    def device(kind):
+        if kind == UP:
+            return {"context": ctx, "expert": z + 1}
+        if kind == DOWN:
+            return {"context": ctx, "expert": z - 1}
+        if kind == ACROSS:
+            return {"context": (1 - y) * 2 + c, "expert": z}
+        if kind == CORE:
+            return {"context": y * 2 + 1 - c, "expert": z}
+        return {"dp": 1 - lax.axis_index("dp")}
+
+    def per_side(action, more=()):
+        @pl.when(z < 3)
+        def _():
+            action(UP)
+
+        @pl.when(z > 0)
+        def _():
+            action(DOWN)
+
+        for kind in (ACROSS, CORE, *more):
+            action(kind)
+
+    return y, c, z, inner, device, per_side
+
+
+def block_id(yy, cc, zz):
+    return (yy * 2 + cc) * 4 + zz
+
+
+def greet(per_side, device, count, more=()):
+    barrier = pltpu.get_barrier_semaphore()
+    per_side(
+        lambda kind: pl.semaphore_signal(
+            barrier, inc=1, device_id=device(kind), device_id_type=MESH_ID
+        ),
+        more,
+    )
+    pl.semaphore_wait(barrier, count)
+
+
+def gather_kernel(
+    query_ref,
+    key_ref,
+    value_ref,
+    small_ref,
+    out_ref,
+    early_ref,
+    late_ref,
+    early,
+    late,
+    local_sem,
+    early_send,
+    early_core,
+    early_recv,
+    late_send,
+    late_dp,
+    late_recv,
+):
+    y, c, z, inner, device, per_side = place()
+    d = lax.axis_index("dp")
+    mine = d * 16 + block_id(y, c, z)
+    loads = []
+    at = 0
+    for index, ref in enumerate((query_ref, key_ref, value_ref, small_ref)):
+        size = ref.shape[1]
+        loads.append(
+            pltpu.make_async_copy(ref, early.at[mine, :, pl.ds(at, size)], local_sem.at[index])
+        )
+        at += size
+    loads.append(pltpu.make_async_copy(out_ref, late.at[mine], local_sem.at[4]))
+    for copy in loads:
+        copy.start()
+    greet(per_side, device, 4 + inner, (DP,))
+    for copy in loads:
+        copy.wait()
+
+    def early_copy(kind, slot, sem):
+        return pltpu.make_async_remote_copy(
+            src_ref=early.at[slot],
+            dst_ref=early.at[slot],
+            send_sem=sem,
+            recv_sem=early_recv.at[slot],
+            device_id=device(kind),
+            device_id_type=MESH_ID,
+        )
+
+    def early_own(kind, block):
+        return early_copy(kind, d * 16 + block, early_send.at[kind, block])
+
+    def early_other(block):
+        return early_copy(CORE, (1 - d) * 16 + block, early_core.at[block])
+
+    def late_copy(kind, slot, sem):
+        return pltpu.make_async_remote_copy(
+            src_ref=late.at[slot],
+            dst_ref=late.at[slot],
+            send_sem=sem,
+            recv_sem=late_recv.at[slot],
+            device_id=device(kind),
+            device_id_type=MESH_ID,
+        )
+
+    def late_own(kind, plane, block):
+        slot = plane * 16 + block
+        return late_copy(kind, slot, late_send.at[kind, slot])
+
+    def along(kind, zz):
+        if kind == UP:
+            return jnp.logical_and(z < 3, zz <= z)
+        return jnp.logical_and(z > 0, zz >= z)
+
+    def fan(zz, act):
+        block = block_id(y, c, zz)
+        for kind in (UP, DOWN):
+
+            @pl.when(along(kind, zz))
+            def _():
+                act(early_own(kind, block))
+                act(late_own(kind, d, block))
+
+        for kind in (ACROSS, CORE):
+            act(early_own(kind, block))
+            act(late_own(kind, d, block))
+        act(early_own(DP, block))
+
+    def fan_other(zz, act):
+        block = block_id(y, c, zz)
+        for kind in (UP, DOWN):
+
+            @pl.when(along(kind, zz))
+            def _():
+                act(late_own(kind, 1 - d, block))
+
+        for kind in (ACROSS, CORE):
+            act(late_own(kind, 1 - d, block))
+
+    def fan_across(zz, act):
+        block = block_id(1 - y, c, zz)
+        act(early_own(CORE, block))
+        act(early_own(DP, block))
+        act(late_own(CORE, d, block))
+        act(late_own(CORE, 1 - d, block))
+
+    def fan_dp(zz, act):
+        act(early_other(block_id(y, c, zz)))
+        act(early_other(block_id(1 - y, c, zz)))
+
+    start = lambda copy: copy.start()
+    over_dp = late_copy(DP, mine, late_dp)
+    over_dp.start()
+    fan(z, start)
+
+    def arrive(step, carry):
+        @pl.when(step < 4)
+        def _():
+            zz = line_order(z, step)
+            block = block_id(y, c, zz)
+
+            @pl.when(step > 0)
+            def _():
+                early_own(ACROSS, block).wait_recv()
+                late_own(ACROSS, d, block).wait_recv()
+                fan(zz, start)
+
+            late_own(ACROSS, 1 - d, block).wait_recv()
+            fan_other(zz, start)
+
+        @pl.when(jnp.logical_and(step > 0, step < 5))
+        def _():
+            zz = line_order(z, jnp.maximum(step - 1, 0))
+            block = block_id(1 - y, c, zz)
+            early_own(CORE, block).wait_recv()
+            late_own(CORE, d, block).wait_recv()
+            late_own(CORE, 1 - d, block).wait_recv()
+            fan_across(zz, start)
+
+        @pl.when(step > 1)
+        def _():
+            zz = line_order(z, jnp.maximum(step - 2, 0))
+            early_other(block_id(y, c, zz)).wait_recv()
+            early_other(block_id(1 - y, c, zz)).wait_recv()
+            fan_dp(zz, start)
+
+        return carry
+
+    lax.fori_loop(0, 6, arrive, 0)
+
+    def finish(zz, carry):
+        for yy in range(2):
+            block = block_id(yy, 1 - c, zz)
+            early_own(CORE, block).wait_recv()
+            early_other(block).wait_recv()
+            late_own(CORE, d, block).wait_recv()
+            late_own(CORE, 1 - d, block).wait_recv()
+        return carry
+
+    lax.fori_loop(0, 4, finish, 0)
+    results = (
+        pltpu.make_async_copy(early, early_ref, local_sem.at[0]),
+        pltpu.make_async_copy(late, late_ref, local_sem.at[1]),
+    )
+    for copy in results:
+        copy.start()
+    end = lambda copy: copy.wait_send()
+    over_dp.wait_send()
+
+    def ends(zz, carry):
+        fan(zz, end)
+        fan_other(zz, end)
+        fan_across(zz, end)
+        fan_dp(zz, end)
+        return carry
+
+    lax.fori_loop(0, 4, ends, 0)
+    for copy in results:
+        copy.wait()
+
+
+def gather_weights(query, key, value, small, out):
+    bfloat = jnp.bfloat16
+    dma = pltpu.SemaphoreType.DMA
+    rows = query.shape[0]
+    early_width = query.shape[1] + key.shape[1] + value.shape[1] + small.shape[1]
+    anywhere = pl.BlockSpec(memory_space=pl.ANY)
+    early = (32, rows, early_width)
+    late = (32, rows, out.shape[1])
+    return pl.pallas_call(
+        gather_kernel,
+        out_shape=(jax.ShapeDtypeStruct(early, bfloat), jax.ShapeDtypeStruct(late, bfloat)),
+        in_specs=[anywhere] * 5,
+        out_specs=(anywhere, anywhere),
+        scratch_shapes=[
+            pltpu.VMEM(early, bfloat),
+            pltpu.VMEM(late, bfloat),
+            dma((5,)),
+            dma((5, 16)),
+            dma((16,)),
+            dma((32,)),
+            dma((4, 32)),
+            dma,
+            dma((32,)),
+        ],
+        compiler_params=pltpu.CompilerParams(
+            collective_id=0, has_side_effects=True, vmem_limit_bytes=40 * 2**20
+        ),
+        name="gather_weights",
+    )(query, key, value, small, out)
+
+
+def sums_kernel(
+    proj_ref,
+    small_ref,
+    out_ref,
+    gate_ref,
+    up_ref,
+    down_ref,
+    sum_ref,
+    gate_got,
+    up_got,
+    down_got,
+    parts,
+    core_got,
+    y_got,
+    z_got,
+    dp_got,
+    load_sem,
+    swap_send,
+    swap_recv,
+    core_send,
+    core_recv,
+    y_send,
+    y_recv,
+    z_send,
+    z_recv,
+    dp_send,
+    dp_recv,
+):
+    single = jnp.float32
+    bfloat = jnp.bfloat16
+    y, c, z, inner, device, per_side = place()
+    d = lax.axis_index("dp")
+    rows = proj_ref.shape[2]
+    loads = []
+    at = 0
+    for index, ref in enumerate((proj_ref, small_ref, out_ref)):
+        size = ref.shape[3]
+        for plane in range(2):
+            loads.append(
+                pltpu.make_async_copy(
+                    ref.at[plane],
+                    parts.at[:, pl.ds(plane * rows, rows), pl.ds(at, size)],
+                    load_sem.at[index * 2 + plane],
+                )
+            )
+        at += size
+    for copy in loads:
+        copy.start()
+    greet(per_side, device, 4 + inner, (DP,))
+
+    swaps = []
+    for index, (source, target) in enumerate(
+        ((gate_ref, gate_got), (up_ref, up_got), (down_ref, down_got))
+    ):
+        half = target.shape[1]
+        for j in range(target.shape[0]):
+            swaps.append(
+                pltpu.make_async_remote_copy(
+                    src_ref=source.at[j, pl.ds(pl.multiple_of((1 - d) * half, 128), half), :],
+                    dst_ref=target.at[j],
+                    send_sem=swap_send.at[index * 2 + j],
+                    recv_sem=swap_recv.at[index * 2 + j],
+                    device_id=device(DP),
+                    device_id_type=MESH_ID,
+                )
+            )
+    for copy in swaps:
+        copy.start()
+    for copy in loads:
+        copy.wait()
+
+    def remote(kind, source, target, send_sem, recv_sem):
+        return pltpu.make_async_remote_copy(
+            src_ref=source,
+            dst_ref=target,
+            send_sem=send_sem,
+            recv_sem=recv_sem,
+            device_id=device(kind),
+            device_id_type=MESH_ID,
+        )
+
+    def to_core(yy, zz):
+        slot = yy * 4 + zz
+        return remote(
+            CORE, parts.at[block_id(yy, 1 - c, zz)], core_got.at[slot], core_send.at[slot], core_recv.at[slot]
+        )
+
+    def to_across(zz):
+        return remote(ACROSS, parts.at[block_id(1 - y, c, zz)], y_got.at[zz], y_send.at[zz], y_recv.at[zz])
+
+    def to_line(kind, zz, slot):
+        return remote(kind, parts.at[block_id(y, c, zz)], z_got.at[slot], z_send.at[zz], z_recv.at[slot])
+
+    def add(block, got):
+        parts[block] = (parts[block].astype(single) + got.astype(single)).astype(bfloat)
+
+    def core_sends(step, carry):
+        zz = line_order(z, 3 - step)
+        to_core(1 - y, zz).start()
+        to_core(y, zz).start()
+        return carry
+
+    lax.fori_loop(0, 4, core_sends, 0)
+
+    def line_sum(step):
+        zz = line_order(z, step)
+        block = block_id(y, c, zz)
+        to_across(zz).wait_recv()
+        add(block, y_got[zz])
+        rising = zz > z
+        comes = jnp.logical_or(jnp.logical_and(rising, z > 0), jnp.logical_and(zz < z, z < 3))
+
+        @pl.when(comes)
+        def _():
+            to_line(CORE, zz, zz).wait_recv()
+            add(block, z_got[zz])
+
+        @pl.when(rising)
+        def _():
+            to_line(UP, zz, zz).start()
+
+        @pl.when(zz == z - 1)
+        def _():
+            to_line(DOWN, zz, 4).start()
+
+        @pl.when(zz < z - 1)
+        def _():
+            to_line(DOWN, zz, zz).start()
+
+    def stage(turn, carry):
+        @pl.when(turn < 4)
+        def _():
+            zz = line_order(z, 3 - jnp.minimum(turn, 3))
+            to_core(1 - y, zz).wait_recv()
+            add(block_id(1 - y, c, zz), core_got[(1 - y) * 4 + zz])
+            to_across(zz).start()
+            to_core(y, zz).wait_recv()
+            add(block_id(y, c, zz), core_got[y * 4 + zz])
+
+        @pl.when(jnp.logical_and(turn > 0, turn < 4))
+        def _():
+            line_sum(4 - jnp.maximum(turn, 1))
+
+        return carry
+
+    lax.fori_loop(0, 4, stage, 0)
+    mine = block_id(y, c, z)
+    to_across(z).wait_recv()
+    add(mine, y_got[z])
+
+    @pl.when(z > 0)
+    def _():
+        to_line(CORE, z, z).wait_recv()
+        add(mine, z_got[z])
+
+    @pl.when(z < 3)
+    def _():
+        to_line(CORE, z, 4).wait_recv()
+        add(mine, z_got[4])
+
+    there = pl.ds(pl.multiple_of((1 - d) * rows, 16), rows)
+    here = pl.ds(pl.multiple_of(d * rows, 16), rows)
+    last = remote(DP, parts.at[mine, there, :], dp_got, dp_send, dp_recv)
+    last.start()
+    last.wait_recv()
+    sum_ref[...] = parts[mine, here, :].astype(single) + dp_got[...].astype(single)
+    last.wait_send()
+    for copy in swaps:
+        copy.wait()
+
+    def ends(zz, carry):
+        to_core(y, zz).wait_send()
+        to_core(1 - y, zz).wait_send()
+        to_across(zz).wait_send()
+
+        @pl.when(zz != z)
+        def _():
+            to_line(CORE, zz, zz).wait_send()
+
+        return carry
+
+    lax.fori_loop(0, 4, ends, 0)
+
+
+def sum_gradients(proj, small, out, gate, up, down):
+    bfloat = jnp.bfloat16
+    dma = pltpu.SemaphoreType.DMA
+    rows = proj.shape[0] // 32
+    parts = [x.reshape(2, 16, rows, x.shape[1]) for x in (proj, small, out)]
+    width = sum(x.shape[3] for x in parts)
+    anywhere = pl.BlockSpec(memory_space=pl.ANY)
+    halves = [(x.shape[0], x.shape[1] // 2, x.shape[2]) for x in (gate, up, down)]
+    return pl.pallas_call(
+        sums_kernel,
+        out_shape=(
+            jax.ShapeDtypeStruct((rows, width), jnp.float32),
+            *(jax.ShapeDtypeStruct(shape, bfloat) for shape in halves),
+        ),
+        in_specs=[anywhere] * 6,
+        out_specs=(pl.BlockSpec(memory_space=pltpu.VMEM), anywhere, anywhere, anywhere),
+        scratch_shapes=[
+            pltpu.VMEM((16, 2 * rows, width), bfloat),
+            pltpu.VMEM((8, 2 * rows, width), bfloat),
+            pltpu.VMEM((4, 2 * rows, width), bfloat),
+            pltpu.VMEM((5, 2 * rows, width), bfloat),
+            pltpu.VMEM((rows, width), bfloat),
+            dma((6,)),
+            dma((6,)),
+            dma((6,)),
+            dma((8,)),
+            dma((8,)),
+            dma((4,)),
+            dma((4,)),
+            dma((4,)),
+            dma((5,)),
+            dma,
+            dma,
+        ],
+        compiler_params=pltpu.CompilerParams(
+            collective_id=2, has_side_effects=True, vmem_limit_bytes=40 * 2**20
+        ),
+        name="sum_gradients",
+    )(*parts, gate, up, down)
 
 
 def experts_kernel(
@@ -131,7 +614,6 @@
     y = ctx // 2
     c = ctx % 2
     inner = z + (z // 2) * (3 - 2 * z)
-    UP, DOWN, ACROSS, CORE = 0, 1, 2, 3
 
     def device(kind):
         if kind == UP:
@@ -648,16 +1130,41 @@
     scale = HEAD_SIZE ** (-0.5)
     bfloat = jnp.bfloat16
     single = jnp.float32
-    small = jnp.concatenate([w_router, gain_attn[:, None], gain_ffn[:, None]], axis=1)
-    early = jnp.concatenate([w_query, key_weight, value_weight, small], axis=1)
-    early = lax.all_gather(early, EVERY, axis=0, tiled=True)
-    out_w = lax.all_gather(w_out, EVERY, axis=0, tiled=True)
-    query_w = early[:, : w_query.shape[1]]
-    key_w = early[:, w_query.shape[1] : w_query.shape[1] + key_weight.shape[1]]
-    value_w = early[:, w_query.shape[1] + key_weight.shape[1] : -small.shape[1]]
-    router_w = early[:, -small.shape[1] : -2]
-    gain_one = early[:, -2]
-    gain_two = early[:, -1]
+    proj_width = w_query.shape[1] + key_weight.shape[1] + value_weight.shape[1]
+    own_rows = w_query.shape[0]
+    small = jnp.concatenate(
+        [
+            w_router,
+            gain_attn[:, None],
+            gain_ffn[:, None],
+            jnp.zeros((own_rows, 64 - experts - 2), bfloat),
+        ],
+        axis=1,
+    )
+    if lax.axis_size("dp") == 2:
+        packed = routes.reshape(-1, 64).astype(bfloat)
+        packed = jnp.pad(packed, ((0, own_rows - packed.shape[0]), (0, 0)))
+        early, late = gather_weights(
+            w_query, key_weight, value_weight, jnp.concatenate([small, packed], axis=1), w_out
+        )
+        routes_all = lax.dynamic_slice(
+            early,
+            (lax.axis_index("dp") * 16, 0, proj_width + 64),
+            (16, sequence_per_device * TOP // 64, 64),
+        )
+        routes_all = routes_all.astype(jnp.int32).reshape(16, sequence_per_device, TOP)
+        routes_all = routes_all.swapaxes(1, 2)
+        early = early.reshape(-1, early.shape[2])
+        out_w = late.reshape(-1, late.shape[2])
+    else:
+        early = jnp.concatenate([w_query, key_weight, value_weight, small], axis=1)
+        early = lax.all_gather(early, EVERY, axis=0, tiled=True)
+        out_w = lax.all_gather(w_out, EVERY, axis=0, tiled=True)
+        routes_all = lax.all_gather(routes[0].T, GROUP, axis=0, tiled=False)
+    proj_w = early[:, :proj_width]
+    router_w = early[:, proj_width : proj_width + experts]
+    gain_one = early[:, proj_width + experts]
+    gain_two = early[:, proj_width + experts + 1]
     gain_one = gain_one.astype(single)
     gain_two = gain_two.astype(single)
     positions = lax.axis_index("context") * sequence_per_device + jnp.arange(
@@ -670,11 +1177,10 @@
     inverse_one = lax.rsqrt(jnp.mean(inputs * inputs, axis=-1, keepdims=True) + epsilon)
     normed_one = inputs * inverse_one
     hidden_one = (normed_one * gain_one).astype(bfloat)
-    query_lin = jnp.einsum("gsd,de->gse", hidden_one, query_w, preferred_element_type=single)
-    key_linear = jnp.einsum("gsd,de->gse", hidden_one, key_w, preferred_element_type=single)
-    value_lower = jnp.einsum(
-        "gsd,de->gse", hidden_one, value_w, preferred_element_type=single
-    ).astype(bfloat)
+    projected = jnp.einsum("gsd,de->gse", hidden_one, proj_w, preferred_element_type=single)
+    query_lin = projected[..., : w_query.shape[1]]
+    key_linear = projected[..., w_query.shape[1] : w_query.shape[1] + key_weight.shape[1]]
+    value_lower = projected[..., -value_weight.shape[1] :].astype(bfloat)
     query_rotated = (
         apply_rotation(
             query_lin.reshape(query_groups, sequence_per_device, QUERY_HEADS, HEAD_SIZE),
@@ -697,6 +1203,12 @@
         lax.all_gather(key_rotated, "context", axis=1, tiled=True),
         lax.all_gather(value_lower, "context", axis=1, tiled=True),
     )
+
+    final_low = (cotangent.astype(single) * valid).astype(bfloat)
+    final_low, gathered_keys, gathered_values = lax.optimization_barrier(
+        (final_low, gathered_keys, gathered_values)
+    )
+    final_all = lax.all_gather(final_low[0], GROUP, axis=0, tiled=False)
 
     def attn_scores(slot_index):
         query_per_head = query_rotated[slot_index].reshape(
@@ -732,9 +1244,6 @@
     matches = routes[..., None] == jnp.arange(experts, dtype=jnp.int32)
     chosen = jnp.sum(jnp.where(matches, logits[:, :, None, :], 0.0), axis=-1)
     gates = jax.nn.softmax(chosen, axis=-1)
-    final_low = (cotangent.astype(single) * valid).astype(bfloat)
-    final_all = lax.all_gather(final_low[0], GROUP, axis=0, tiled=False)
-    routes_all = lax.all_gather(routes[0].T, GROUP, axis=0, tiled=False)
     grad_hidden, combined, scores, grad_w_gate, grad_w_up, grad_w_down = experts_on_owner(
         hidden_two[0], final_all, routes_all, router_w.T, w_gate, w_up, w_down, capacity
     )
@@ -742,7 +1251,6 @@
     scores = scores[:, :local_exp]
     scores = lax.all_to_all(scores, GROUP, split_axis=0, concat_axis=0, tiled=True)
     scores = scores.reshape(experts, sequence_per_device)
-    block_out = (valid * (resid + combined.astype(single)[None])).astype(bfloat)
     grad_final = cotangent.astype(single) * valid
     grad_gates = jnp.sum(jnp.where(matches, scores.T[None, :, None, :], 0.0), axis=-1)
     gate_mean = jnp.sum(gates * grad_gates, axis=-1, keepdims=True)
@@ -818,60 +1326,58 @@
         .reshape(query_groups, sequence_per_device, KEY_VALUE_HEADS * HEAD_SIZE)
     )
     grad_value_low = value_grad.astype(bfloat)
-    grad_w_query = jnp.einsum(
-        "gsd,gse->de", hidden_one, grad_query_lin, preferred_element_type=single
-    )
-    grad_w_key = jnp.einsum("gsd,gse->de", hidden_one, grad_key_lin, preferred_element_type=single)
-    grad_w_value = jnp.einsum(
-        "gsd,gse->de", hidden_one, grad_value_low, preferred_element_type=single
-    )
-    grad_hidden_one = jnp.einsum(
-        "gse,de->gsd", grad_query_lin, query_w, preferred_element_type=single
-    )
-    grad_hidden_one = grad_hidden_one + jnp.einsum(
-        "gse,de->gsd", grad_key_lin, key_w, preferred_element_type=single
-    )
-    grad_hidden_one = grad_hidden_one + jnp.einsum(
-        "gse,de->gsd", grad_value_low, value_w, preferred_element_type=single
-    )
+    grad_proj = jnp.concatenate([grad_query_lin, grad_key_lin, grad_value_low], axis=-1)
+    grad_proj_w = jnp.einsum("gsd,gse->de", hidden_one, grad_proj, preferred_element_type=single)
+    grad_hidden_one = jnp.einsum("gse,de->gsd", grad_proj, proj_w, preferred_element_type=single)
     grad_gain_attn = jnp.sum(grad_hidden_one * normed_one, axis=(0, 1))
     grad_tokens = norm_back(grad_hidden_one * gain_one, normed_one, inverse_one) + grad_resid
-    late = jnp.concatenate(
+    grad_proj_w = grad_proj_w.astype(bfloat)
+    grad_out_w = grad_w_out.astype(bfloat)
+    combined, grad_proj_w = lax.optimization_barrier((combined, grad_proj_w))
+    block_out = (valid * (resid + combined.astype(single)[None])).astype(bfloat)
+    grad_small = jnp.concatenate(
         [
-            grad_w_query,
-            grad_w_key,
-            grad_w_value,
             grad_w_router,
             grad_gain_attn[:, None],
             grad_gain_ffn[:, None],
+            jnp.zeros((MODEL_WIDTH, 128 - experts - 2), single),
         ],
         axis=1,
     ).astype(bfloat)
-    late = lax.psum_scatter(late, EVERY, scatter_dimension=0, tiled=True).astype(single)
-    out_grad = lax.psum_scatter(
-        grad_w_out.astype(bfloat), EVERY, scatter_dimension=0, tiled=True
-    ).astype(single)
-    width = grad_w_query.shape[1]
-    narrow = grad_w_key.shape[1]
+    if lax.axis_size("dp") == 2:
+        summed, *got = sum_gradients(
+            grad_proj_w, grad_small, grad_out_w, grad_w_gate, grad_w_up, grad_w_down
+        )
+
+        def both(whole, other):
+            half = whole.shape[1] // 2
+            own = lax.dynamic_slice_in_dim(whole, lax.axis_index("dp") * half, half, axis=1)
+            return own.astype(single) + other.astype(single)
+
+        expert_sums = tuple(
+            both(whole, other)
+            for whole, other in zip((grad_w_gate, grad_w_up, grad_w_down), got)
+        )
+    else:
+        summed = lax.psum_scatter(
+            jnp.concatenate([grad_proj_w, grad_small, grad_out_w], axis=1),
+            EVERY,
+            scatter_dimension=0,
+            tiled=True,
+        ).astype(single)
+        expert_sums = tuple(
+            lax.psum_scatter(x, "dp", scatter_dimension=1, tiled=True).astype(single)
+            for x in (grad_w_gate, grad_w_up, grad_w_down)
+        )
+    ends = (w_query.shape[1], proj_width - value_weight.shape[1], proj_width)
     shard_grads = (
-        late[:, -2],
-        late[:, :width],
-        late[:, width : width + narrow],
-        late[:, width + narrow : width + 2 * narrow],
-        out_grad,
-        late[:, -1],
-        late[:, width + 2 * narrow : -2],
-    )
-    expert_sums = (
-        lax.psum_scatter(
-            grad_w_gate.astype(jnp.bfloat16), "dp", scatter_dimension=1, tiled=True
-        ).astype(jnp.float32),
-        lax.psum_scatter(
-            grad_w_up.astype(jnp.bfloat16), "dp", scatter_dimension=1, tiled=True
-        ).astype(jnp.float32),
-        lax.psum_scatter(
-            grad_w_down.astype(jnp.bfloat16), "dp", scatter_dimension=1, tiled=True
-        ).astype(jnp.float32),
+        summed[:, proj_width + experts],
+        summed[:, : ends[0]],
+        summed[:, ends[0] : ends[1]],
+        summed[:, ends[1] : ends[2]],
+        summed[:, proj_width + 128 :],
+        summed[:, proj_width + experts + 1],
+        summed[:, proj_width : proj_width + experts],
     )
     return (
         block_out,

time: 1140 us -> 826 us (0.72)
  waiting for transfers between devices: 627 us -> 236 us
  Pallas kernels: 197 us -> 374 us
  local copies, waits for them, and re-layouts: 84.4 us -> 35.4 us
  blocking collectives: 35 us -> 0 us
  matrix products: 118 us -> 104 us
    reduce_scatter x4 -> x0, waiting for transfers between devices: 182 us -> none  [the longest x1 108 us: on_device(): lax.psum_scatter(grad_w_out.astype(bfloat), EVERY, scatter_dimension=0, t...]
    pallas_call x0 -> x2, Pallas kernels: none -> 176 us  [the longest x1 114 us: sum_gradients(): pl.pallas_call(sums_kernel, out_shape=(jax.ShapeDtypeStruct((rows, width)...]
    unnamed x14 -> x6, waiting for transfers between devices: 136 us -> 0.59 us
    all_gather x2 -> x0, waiting for transfers between devices: 81.5 us -> none  [the longest x1 78.2 us: on_device(): early = lax.all_gather(early, EVERY, axis=0, tiled=True)]
    all_gather x1, waiting for transfers between devices: 96.3 us -> 54.2 us  [on_device(): final_all = lax.all_gather(final_low[0], GROUP, axis=0, tiled=False)]
    concatenate x2 -> x4, local copies, waits for them, and re-layouts: 38 us -> 2.1 us  [the longest x3 2 us: on_device(): jnp.concatenate([grad_w_router, grad_gain_attn[:, None], grad_gain_ffn[:,...]
    all_gather x1 -> x0, blocking collectives: 35 us -> none  [on_device(): routes_all = lax.all_gather(routes[0].T, GROUP, axis=0, tiled=False)]
    all_gather x1, waiting for transfers between devices: 0.02 us -> 18.9 us  [on_device(): lax.all_gather(value_lower, 'context', axis=1, tiled=True)]
  transfers between devices with their start and end apart: 14 -> 7, of which waited for: 10 -> 6; matrix products, arithmetic and copies ran while one was open for 16% -> 12% of each run, Pallas kernels for 0% -> 0%
where the time goes in v2:
time: 826 us; the launch traced here: 822 us
  Pallas kernels  374 us (45%)
  waiting for transfers between devices  236 us (29%)
  matrix products  104 us (13%)
  other arithmetic  52.1 us (6%)
  local copies, waits for them, and re-layouts  35.4 us (4%)
  between operations  15.8 us (2%)
    pallas_call x1, Pallas kernels, experts_on_owner(): pl.pallas_call(experts_kernel, out_shape=(jax.ShapeDtypeStruct((tokens_bl...  197 us
    reduce_scatter x1, waiting for transfers between devices, on_device(): lax.psum_scatter(combined, GROUP, scatter_dimension=0, tiled=False)  121 us
    pallas_call x1, Pallas kernels, sum_gradients(): pl.pallas_call(sums_kernel, out_shape=(jax.ShapeDtypeStruct((rows, width)...  114 us
    pallas_call x1, Pallas kernels, gather_weights(): pl.pallas_call(gather_kernel, out_shape=(jax.ShapeDtypeStruct(early, bflo...  62.8 us
    all_gather x1, waiting for transfers between devices, on_device(): final_all = lax.all_gather(final_low[0], GROUP, axis=0, tiled=False)  54.2 us
    dot_general x1, matrix products, on_device(): jnp.einsum('skrd,tkd->krst', head_gradient, value_per_head, preferred_ele...  21.8 us
    reduce_scatter x1, waiting for transfers between devices, on_device(): lax.psum_scatter(jnp.stack(grad_values).astype(jnp.bfloat16), 'context',...  20 us
    all_gather x1, waiting for transfers between devices, on_device(): lax.all_gather(value_lower, 'context', axis=1, tiled=True)  18.9 us
  transfers between devices with their start and end apart: 7, of which 6 were waited for; matrix products, arithmetic and copies ran while one was open for 12% of the time, Pallas kernels for 0%

profile of v2, /device:TPU:0, one launch (start us, length us, event | category | flops | bytes accessed | tf_op | source)
XLA Modules:
  0.0 822.1 jit_solution(1037689071572805347)
XLA Ops:
  14.0 62.8 %gather_weights.1 = (bf16[32,48,2688]{2,1,0:T(8,128)(2,1)S(1)}, bf16[32,48,1536]{2,1,0:T(8,128)(2,1)S(1)}) custom-call(bf16[48,1536]{1,0:T(8,128)(2,1)S(1)} %copy-done.9, bf16[48,512]{1,0:T(8,128)(2,1)S(1)} %copy-done.11, bf16[48,512]{1,0:T(8,128)(2,1)S(1)} %copy-done.12, bf16[48,128]{1,0:T(8,128)(2,1)S(1)} %concatenate.44.small_ref, ...), custom_call_target="tpu_custom_call" | custom-call | tf_op jit(solution)/shard_map/gather_weights/pallas_call | solution.py:316
  77.4 2.0 fusion.31
  79.4 3.9 fusion.14
  84.2 2.0 copy.145
  86.5 1.1 subtract_convert_fusion.3
  90.4 1.1 fusion.38
  91.5 14.5 %all-gather.4.cloned.1.call-done = bf16[1,1024,512]{1,2,0:T(8,128)(2,1)} async-done(((bf16[1,256,512]{1,2,0:T(8,128)(2,1)}), bf16[1,1024,512]{1,2,0:T(8,128)(2,1)}) %all-gather.4.cloned.1.call-update) | async-done | bytes 1048592 | tf_op jit(solution)/shard_map/all_gather | solution.py:1203
  106.0 18.9 %all-gather.6.cloned.1.call-done = bf16[1,1024,512]{2,1,0:T(8,128)(2,1)} async-done(((bf16[1,256,512]{2,1,0:T(8,128)(2,1)}), bf16[1,1024,512]{2,1,0:T(8,128)(2,1)}) %all-gather.6.cloned.1.call-update) | async-done | bytes 1048592 | tf_op jit(solution)/shard_map/all_gather | solution.py:1204
  124.9 1.3 slice.99
  127.2 1.9 copy.147
  129.1 1.0 dynamic-slice_convert_fusion
  133.6 1.6 copy.146
  135.2 11.6 %fusion.9 = (f32[8,3,256]{2,1,0:T(4,128)S(1)}, f32[8,1024,256,3]{2,1,3,0:T(8,128)}) fusion(pred[256,1024]{0,1:T(8,128)(4,1)S(1)} %fusion.40, bf16[1024,8,64,1]{0,2,3,1:T(8,128)(2,1)S(1)} %bitcast.167, bf16[256,8,3,32]{0,3,2,1:T(8,128)(2,1)} %bitcast.175, bf16[256,8,3,32]{0,3,2,1:T(8,128)(2,1)S(1)} %bitcast.173), kind=kOutput, calls=%fused_computation.15 | convolution fusion | flops 825747456 | bytes 27287552 | tf_op jit(solution)/shard_map/skrd,tkd->krst/dot_general | solution.py:1218
  146.9 11.4 %fusion.3 = f32[8,3,256]{2,1,0:T(4,128)S(1)} fusion(f32[8,3,256]{2,1,0:T(4,128)S(1)} %get-tuple-element.142, f32[8,1024,256,3]{2,1,3,0:T(8,128)} %get-tuple-element.143, pred[256,1024]{0,1:T(8,128)(4,1)S(1)} %fusion.40), kind=kLoop, calls=%fused_computation.9 | loop fusion | flops 25159680 | bytes 25477120 | tf_op jit(solution)/shard_map/reduce_sum | solution.py:1230
  158.3 11.7 %fusion.39 = bf16[8,64,3,256]{3,1,2,0:T(8,128)(2,1)S(1)} fusion(bf16[1024,8,64,1]{0,2,3,1:T(8,128)(2,1)S(1)} %bitcast.184, f32[8,3,256]{2,1,0:T(4,128)S(1)} %fusion.3, f32[8,3,256]{2,1,0:T(4,128)S(1)} %get-tuple-element.142, f32[8,1024,256,3]{2,1,3,0:T(8,128)} %get-tuple-element.143, pred[256,1024]{0,1:T(8,128)(4,1)S(1)} %fusion.40), kind=kOutput, calls=%fused_computation.60 | convolution fusion | flops 837156864 | bytes 27312128 | tf_op jit(solution)/shard_map/krst,tkd->skrd/dot_general | solution.py:1233
  170.0 1.5 multiply_reduce_fusion
  171.5 1.7 fusion.59
  173.3 1.1 fusion.85.hidden_ref
  174.4 54.2 %all-gather.8.cloned.1.call-done.final_ref = bf16[16,256,1536]{2,1,0:T(8,128)(2,1)} async-done(((bf16[1,256,1536]{2,1,0:T(8,128)(2,1)}), bf16[16,256,1536]{2,1,0:T(8,128)(2,1)}) %all-gather.8.cloned.1.call-update) | async-done | bytes 12582928 | tf_op jit(solution)/shard_map/all_gather | solution.py:1211
  228.6 197.5 %experts.1 = (bf16[256,1536]{1,0:T(8,128)(2,1)}, bf16[16,256,1536]{2,1,0:T(8,128)(2,1)}, f32[16,8,256]{2,1,0:T(8,128)}, bf16[2,1536,512]{2,1,0:T(8,128)(2,1)}, b...) custom-call(bf16[256,1536]{1,0:T(8,128)(2,1)} %fusion.85.hidden_ref, ...), custom_call_target="tpu_custom_call" | custom-call | tf_op jit(solution)/shard_map/experts/pallas_call | solution.py:1060
  426.1 1.7 slice.81
  427.8 4.4 all-to-all-start
  432.3 6.4 all-to-all-done
  438.9 2.5 fusion.34
  442.0 1.1 copy-done.21
  443.1 3.8 convolution_convert_fusion.2
  447.3 21.8 %fusion = (f32[8,3,256]{2,1,0:T(4,128)S(1)}, f32[8,1024,256,3]{2,1,3,0:T(8,128)}) fusion(f32[8,3,256]{2,1,0:T(4,128)S(1)} %log_add_fusion, pred[256,1024]{0,1:T(8,128)(4,1)S(1)} %fusion.40, f32[8,1024,256,3]{2,1,3,0:T(8,128)} %get-tuple-element.143, bf16[1024,8,64,1]{0,2,3,1:T(8,128)(2,1)S(1)} %bitcast.185, bf16[256,8,3,64]{0,3,2,1:T(8,128)(2,1)S(1)} %bitcast.187), kind=kOutput, calls=%fused_computation.2 | convolution fusion | flops 843048960 | bytes 52477952 | tf_op jit(solution)/shard_map/skrd,tkd->krst/dot_general | solution.py:1280
  469.1 17.3 %fusion.2 = bf16[8,3,256,1024]{2,3,1,0:T(8,128)(2,1)S(1)} fusion(f32[8,1024,256,3]{2,1,3,0:T(8,128)} %get-tuple-element.148, f32[8,3,256]{2,1,0:T(4,128)S(1)} %get-tuple-element.147, f32[8,3,256]{2,1,0:T(4,128)S(1)} %log_add_fusion, pred[256,1024]{0,1:T(8,128)(4,1)S(1)} %fusion.40, f32[8,1024,256,3]{2,1,3,0:T(8,128)} %get-tuple-element.143), kind=kLoop, calls=%fused_computation.4 | loop fusion | flops 44040192 | bytes 63225856 | tf_op jit(solution)/shard_map/convert_element_type | solution.py:1284
  486.4 6.6 fusion.22
  493.2 13.0 %bitcast_convert_fusion = bf16[8,64,1024]{2,1,0:T(8,128)(2,1)} fusion(bf16[256,8,3,64]{0,3,2,1:T(8,128)(2,1)} %bitcast.188, f32[8,3,256]{2,1,0:T(4,128)S(1)} %log_add_fusion, pred[256,1024]{0,1:T(8,128)(4,1)S(1)} %fusion.40, f32[8,1024,256,3]{2,1,3,0:T(8,128)} %get-tuple-element.143), kind=kOutput, calls=%fused_computation.35 | convolution fusion | flops 837287936 | bytes 27287552 | tf_op jit(solution)/shard_map/krst,skrd->tkd/dot_general | solution.py:1300
  510.4 6.9 convolution_multiply_fusion
  517.6 1.1 copy-done.22
  518.9 3.5 convolution_convert_fusion.1
  523.5 20.0 %reduce-scatter.8.cloned.1.call-done = bf16[1,256,512]{1,2,0:T(8,128)(2,1)} async-done(((bf16[1,1024,512]{1,2,0:T(8,128)(2,1)}), bf16[1,256,512]{1,2,0:T(8,128)(2,1)}) %reduce-scatter.8.cloned.1.call-update) | async-done | bytes 262160 | tf_op jit(solution)/shard_map/reduce_scatter | solution.py:1308
  543.6 7.0 fusion.30
  551.8 7.5 convolution_convert_fusion
  559.3 1.6 fusion.29
  560.9 121.4 %reduce-scatter.4.cloned.1.call-done = bf16[1,256,1536]{2,1,0:T(8,128)(2,1)} async-done(((bf16[16,256,1536]{2,1,0:T(8,128)(2,1)}), bf16[1,256,1536]{2,1,0:T(8,128)(2,1)}) %reduce-scatter.4.cloned.1.call-update) | async-done | bytes 786448 | tf_op jit(solution)/shard_map/reduce_scatter | solution.py:1250
  682.2 1.9 copy-done.2
  684.1 113.6 %sum_gradients.1 = (f32[48,4224]{1,0:T(8,128)S(1)}, bf16[2,768,512]{2,1,0:T(8,128)(2,1)S(1)}, bf16[2,768,512]{2,1,0:T(8,128)(2,1)S(1)}, bf16[2,256,1536]{2,1,0:T(8,128)(2,1)S(1)}) custom-call(bf16[2,16,48,2560]{3,2,1,0:T(8,128)(2,1)} %bitcast.163, bf16[2,16,48,128]{3,2,1,0:T(8,128)(2,1)S(1)} %maximum_maximum_fusion.small_ref, ...), custom_call_target="tpu_custom_call" | custom-call | tf_op jit(solution)/shard_map/sum_gradients/pallas_call | solution.py:531
  797.7 1.2 copy-done.3
  798.9 1.1 copy-done.5
  800.0 1.1 copy-done.7
  803.4 1.1 fusion.33
  805.2 4.2 convert_add_fusion.2
  809.4 2.1 convert_add_fusion.1
  811.5 1.3 copy-done.28
  812.9 2.1 convert_add_fusion
  (164 shorter events, 26.2 us)
Async XLA Ops:
  7.2 98.8 %all-gather.4.cloned.1.call-start = ((), (), s32[]{:S(2)}) async-start(), calls=%async_computation.4 | async-start | bytes 1310720 | tf_op jit(solution)/shard_map/all_gather | solution.py:1203
  76.9 6.5 copy-start
  76.9 6.5 copy-start.8
  77.4 6.0 copy-start.42
  79.4 4.0 copy-start.45
  83.4 7.0 copy-start.30
  86.5 46.1 %copy-start.36 = (f32[256,32]{0,1:T(8,128)}, f32[256,32]{0,1:T(8,128)S(1)}, u32[]{:S(2)}) copy-start(f32[256,32]{0,1:T(8,128)S(1)} %get-tuple-element.140) | copy-start | bytes 98308
  86.5 46.1 %copy-start.38 = (f32[256,32]{0,1:T(8,128)}, f32[256,32]{0,1:T(8,128)S(1)}, u32[]{:S(2)}) copy-start(f32[256,32]{0,1:T(8,128)S(1)} %get-tuple-element.141) | copy-start | bytes 98308
  88.4 36.5 %all-gather.6.cloned.1.call-start = ((), (), s32[]{:S(2)}) async-start(), calls=%async_computation.5 | async-start | bytes 1310720 | tf_op jit(solution)/shard_map/all_gather | solution.py:1204
  89.2 139.4 %all-gather.8.cloned.1.call-start = ((), (), s32[]{:S(2)}) async-start(), calls=%async_computation.6 | async-start | bytes 13369344 | tf_op jit(solution)/shard_map/all_gather | solution.py:1211
  131.5 3.7 copy-start.26
  133.6 13.3 %copy-start.29 = (bf16[1,256,24,32]{1,3,2,0:T(8,128)(2,1)}, bf16[1,256,24,32]{1,3,2,0:T(8,128)(2,1)S(1)}, u32[]{:S(2)}) copy-start(bf16[1,256,24,32]{1,3,2,0:T(8,128)(2,1)S(1)} %get-tuple-element.130) | copy-start | bytes 1179652
  135.2 23.1 %copy-start.34 = (bf16[1,1024,512]{1,2,0:T(8,128)(2,1)}, bf16[1,1024,512]{1,2,0:T(8,128)(2,1)S(1)}, u32[]{:S(2)}) copy-start(bf16[1,1024,512]{1,2,0:T(8,128)(2,1)S(1)} %copy.146) | copy-start | bytes 3145732
  146.8 23.1 %slice-start = ((s8[4718592]{0:T(1024)(128)(4,1)}), s8[4194304]{0:T(1024)(128)(4,1)S(1)}, s32[]{:S(2)}) async-start(s8[4718592]{0:T(1024)(128)(4,1)} %bitcast.154), calls=%async_computation.10 | async-start | bytes 8388608
  158.3 11.7 %slice-start.1 = ((s8[4718592]{0:T(1024)(128)(4,1)}), s8[524288]{0:T(1024)(128)(4,1)S(1)}, s32[]{:S(2)}) async-start(s8[4718592]{0:T(1024)(128)(4,1)} %bitcast.154), calls=%async_computation.11 | async-start | bytes 1048576
  158.3 11.7 %copy-start.18 = (bf16[1,256,1536]{2,1,0:T(8,128)(2,1)S(1)}, bf16[1,256,1536]{2,1,0:T(8,128)(2,1)}, u32[]{:S(2)}) copy-start(bf16[1,256,1536]{2,1,0:T(8,128)(2,1)} %param.14) | copy-start | bytes 2359300
  170.0 1.5 copy-start.24
  171.5 1.8 copy-start.14
  228.6 210.1 %copy-start.44 = (s32[1,256,8]{1,2,0:T(8,128)S(1)}, s32[1,256,8]{1,2,0:T(8,128)}, u32[]{:S(2)}) copy-start(s32[1,256,8]{1,2,0:T(8,128)} %param.16) | copy-start | bytes 24580
  426.1 15.3 %copy-start.15 = (f32[1,256,1536]{2,1,0:T(8,128)S(1)}, f32[1,256,1536]{2,1,0:T(8,128)}, u32[]{:S(2)}) copy-start(f32[1,256,1536]{2,1,0:T(8,128)} %copy-done.14) | copy-start | bytes 4718596
  426.1 15.3 %copy-start.31 = (bf16[1,256,1536]{2,1,0:T(8,128)(2,1)S(1)}, bf16[1,256,1536]{2,1,0:T(8,128)(2,1)}, u32[]{:S(2)}) copy-start(bf16[1,256,1536]{2,1,0:T(8,128)(2,1)} %param.27) | copy-start | bytes 2359300
  427.8 10.9 %all-to-all-start = ((f32[16,2,256]{2,1,0:T(2,128)}), f32[16,2,256]{2,1,0:T(2,128)S(1)}, u32[]{:S(2)}, u32[]{:S(2)}) async-start(f32[16,2,256]{2,1,0:T(2,128)} %slice.81), calls=%async_computation.1 | async-start | bytes 65536 | tf_op jit(solution)/shard_map/all_to_all | solution.py:1252
  432.2 90.3 %reduce-scatter.6.cloned.1.call-start = ((), (), s32[]{:S(2)}) async-start(), calls=%async_computation.8 | async-start | bytes 1310720 | tf_op jit(solution)/shard_map/reduce_scatter | solution.py:1305
  443.1 4.1 copy-start.35
  447.2 21.9 %copy-start.40 = (bf16[256,1536]{0,1:T(8,128)(2,1)}, bf16[256,1536]{0,1:T(8,128)(2,1)S(1)}, u32[]{:S(2)}) copy-start(bf16[256,1536]{0,1:T(8,128)(2,1)S(1)} %copy.152) | copy-start | bytes 2359300
  486.4 6.6 copy-start.13
  493.0 50.6 %reduce-scatter.8.cloned.1.call-start = ((), (), s32[]{:S(2)}) async-start(), calls=%async_computation.9 | async-start | bytes 1310720 | tf_op jit(solution)/shard_map/reduce_scatter | solution.py:1308
  506.2 176.1 %reduce-scatter.4.cloned.1.call-start = ((), (), s32[]{:S(2)}) async-start(), calls=%async_computation.7 | async-start | bytes 13369344 | tf_op jit(solution)/shard_map/reduce_scatter | solution.py:1250
  506.2 1.5 copy-start.16
  507.7 2.7 copy-start.27
  510.4 6.9 copy-start.37
  510.4 6.9 copy-start.39
  517.3 1.6 copy-start.25
  518.9 24.7 %copy-start.19 = (bf16[1,256,1536]{2,1,0:T(8,128)(2,1)S(1)}, bf16[1,256,1536]{2,1,0:T(8,128)(2,1)}, u32[]{:S(2)}) copy-start(bf16[1,256,1536]{2,1,0:T(8,128)(2,1)} %param.14) | copy-start | bytes 2359300
  518.9 24.7 %copy-start.43 = (f32[1536]{0:T(1024)S(1)}, f32[1536]{0:T(1024)}, u32[]{:S(2)}) copy-start(f32[1536]{0:T(1024)} %copy-done.42) | copy-start | bytes 18436
  518.9 24.7 %copy-start.46 = (f32[256]{0:T(256)S(1)}, f32[256]{0:T(256)}, u32[]{:S(2)}) copy-start(f32[256]{0:T(256)} %copy-done.45) | copy-start | bytes 3076
  543.6 7.7 copy-start.32
  543.6 7.7 copy-start.47
  551.7 7.6 copy-start.20
  551.7 7.5 copy-start.23
  551.8 7.5 copy-start.33
  559.3 123.0 %copy-start.1 = (bf16[2,1536,512]{2,1,0:T(8,128)(2,1)S(1)}, bf16[2,1536,512]{2,1,0:T(8,128)(2,1)}, u32[]{:S(2)}) copy-start(bf16[2,1536,512]{2,1,0:T(8,128)(2,1)} %get-tuple-element.40.up_ref) | copy-start | bytes 9437188
  682.2 1.9 copy-start.2
  684.1 119.3 %copy-start.41 = (bf16[1,256,1536]{2,1,0:T(8,128)(2,1)S(1)}, bf16[1,256,1536]{2,1,0:T(8,128)(2,1)}, u32[]{:S(2)}) copy-start(bf16[1,256,1536]{2,1,0:T(8,128)(2,1)} %reduce-scatter.4.cloned.1.call-done) | copy-start | bytes 2359300
  801.2 2.3 copy-start.17
  805.2 4.2 copy-start.6
  809.4 2.2 copy-start.4
  809.4 3.5 copy-start.28
  (9 other events, 9.4 us)
Sparse Core Ops, SparseCore 0:
  88.5 17.4 all-gather.3
  108.1 16.7 all-gather.5
  127.8 100.7 all-gather.7
  493.1 22.3 reduce-scatter.5
  518.6 24.9 reduce-scatter.7
  547.5 134.7 reduce-scatter.3

commit v3 on v2

--- a/solution.py
+++ b/solution.py
@@ -1,3 +1,4 @@
+import functools
 import math
 
 import jax
@@ -8,12 +9,8 @@
 from jax.sharding import PartitionSpec as P
 
 MODEL_WIDTH = 1536
-QUERY_HEADS = 24
-KEY_VALUE_HEADS = 8
 HEAD_SIZE = 64
 TOP = 8
-
-
 epsilon = 1e-05
 floor_score = -1e30
 
@@ -22,28 +19,20 @@
     half_size = HEAD_SIZE // 2
     exponent = jnp.arange(half_size, dtype=jnp.int32).astype(jnp.float32) * (2.0 / HEAD_SIZE)
     frequency = jnp.exp(-math.log(10000.0) * exponent)
-    angles = positions.astype(jnp.float32)[:, None] * frequency[None, :]
-    return (jnp.cos(angles)[:, None, :], jnp.sin(angles)[:, None, :])
-
-
-def apply_rotation(values, cosine_table, sine_table):
-    half_size = values.shape[-1] // 2
-    first = values[..., :half_size]
-    second = values[..., half_size:]
-    return jnp.concatenate(
-        [first * cosine_table - second * sine_table, second * cosine_table + first * sine_table],
-        axis=-1,
-    )
-
-
-def inverse_rotation(gradient, cosine_table, sine_table):
-    half_size = gradient.shape[-1] // 2
-    first = gradient[..., :half_size]
-    second = gradient[..., half_size:]
-    return jnp.concatenate(
-        [first * cosine_table + second * sine_table, second * cosine_table - first * sine_table],
-        axis=-1,
-    )
+    angles = frequency[:, None] * positions.astype(jnp.float32)[None, :]
+    return (jnp.cos(angles), jnp.sin(angles))
+
+
+def apply_rotation(values, cosine, sine):
+    split = values.reshape(-1, 2, HEAD_SIZE // 2, values.shape[1])
+    first = split[:, 0]
+    second = split[:, 1]
+    turned = jnp.stack([first * cosine - second * sine, second * cosine + first * sine], axis=1)
+    return turned.reshape(values.shape)
+
+
+def inverse_rotation(gradient, cosine, sine):
+    return apply_rotation(gradient, cosine, -sine)
 
 
 def norm_back(gradient, normed, inverse):
@@ -125,6 +114,24 @@
         more,
     )
     pl.semaphore_wait(barrier, count)
+
+
+def swap_copies(sources, targets, j, device, send_sem, recv_sem):
+    d = lax.axis_index("dp")
+    copies = []
+    for index, (source, target) in enumerate(zip(sources, targets)):
+        half = target.shape[0]
+        copies.append(
+            pltpu.make_async_remote_copy(
+                src_ref=source.at[j, pl.ds(pl.multiple_of((1 - d) * half, 128), half), :],
+                dst_ref=target,
+                send_sem=send_sem.at[index],
+                recv_sem=recv_sem.at[index],
+                device_id=device(DP),
+                device_id_type=MESH_ID,
+            )
+        )
+    return copies
 
 
 def gather_kernel(
@@ -386,22 +393,9 @@
         copy.start()
     greet(per_side, device, 4 + inner, (DP,))
 
-    swaps = []
-    for index, (source, target) in enumerate(
-        ((gate_ref, gate_got), (up_ref, up_got), (down_ref, down_got))
-    ):
-        half = target.shape[1]
-        for j in range(target.shape[0]):
-            swaps.append(
-                pltpu.make_async_remote_copy(
-                    src_ref=source.at[j, pl.ds(pl.multiple_of((1 - d) * half, 128), half), :],
-                    dst_ref=target.at[j],
-                    send_sem=swap_send.at[index * 2 + j],
-                    recv_sem=swap_recv.at[index * 2 + j],
-                    device_id=device(DP),
-                    device_id_type=MESH_ID,
-                )
-            )
+    swaps = swap_copies(
+        (gate_ref, up_ref, down_ref), (gate_got, up_got, down_got), 1, device, swap_send, swap_recv
+    )
     for copy in swaps:
         copy.start()
     for copy in loads:
@@ -527,7 +521,7 @@
     parts = [x.reshape(2, 16, rows, x.shape[1]) for x in (proj, small, out)]
     width = sum(x.shape[3] for x in parts)
     anywhere = pl.BlockSpec(memory_space=pl.ANY)
-    halves = [(x.shape[0], x.shape[1] // 2, x.shape[2]) for x in (gate, up, down)]
+    halves = [(x.shape[1] // 2, x.shape[2]) for x in (gate, up, down)]
     return pl.pallas_call(
         sums_kernel,
         out_shape=(
@@ -559,6 +553,284 @@
         ),
         name="sum_gradients",
     )(*parts, gate, up, down)
+
+
+def fill_bias(length_ref, bias, ctx):
+    blocks, keys, queries = bias.shape
+    row = lax.broadcasted_iota(jnp.int32, (keys, queries), 0)
+    column = lax.broadcasted_iota(jnp.int32, (keys, queries), 1) + ctx * queries
+    for j in range(blocks):
+        key = row + j * keys
+        allowed = jnp.logical_and(key <= column, key < length_ref[0])
+        bias[j] = jnp.where(allowed, 0.0, floor_score)
+
+
+def head_probs(query, keys, bias):
+    scores = [contract_rows(key, query) + bias[j] for j, key in enumerate(keys)]
+    peak = jnp.max(scores[0], axis=0, keepdims=True)
+    for score in scores[1:]:
+        peak = jnp.maximum(peak, jnp.max(score, axis=0, keepdims=True))
+    raised = [jnp.exp(score - peak) for score in scores]
+    total = jnp.sum(raised[0], axis=0, keepdims=True)
+    for value in raised[1:]:
+        total = total + jnp.sum(value, axis=0, keepdims=True)
+    inverse = 1.0 / total
+    return [value * inverse for value in raised]
+
+
+def attend_kernel(
+    query_ref, own_ref, length_ref, mixed_ref, all_ref, pairs, bias, local_sem, send_sem, recv_sem
+):
+    bfloat = jnp.bfloat16
+    y, c, _, _, device, _ = place()
+    mine = y * 2 + c
+    own = pltpu.make_async_copy(own_ref, pairs.at[mine], local_sem)
+    own.start()
+    barrier = pltpu.get_barrier_semaphore()
+    for kind in (ACROSS, CORE):
+        pl.semaphore_signal(barrier, inc=1, device_id=device(kind), device_id_type=MESH_ID)
+    pl.semaphore_wait(barrier, 2)
+    own.wait()
+
+    def send(kind, slot, index):
+        return pltpu.make_async_remote_copy(
+            src_ref=pairs.at[slot],
+            dst_ref=pairs.at[slot],
+            send_sem=send_sem.at[index],
+            recv_sem=recv_sem.at[slot],
+            device_id=device(kind),
+            device_id_type=MESH_ID,
+        )
+
+    across = send(ACROSS, mine, 0)
+    core = send(CORE, mine, 1)
+    onward = send(CORE, (1 - y) * 2 + c, 2)
+    across.start()
+    core.start()
+    fill_bias(length_ref, bias, mine)
+    send(ACROSS, (1 - y) * 2 + c, 0).wait_recv()
+    onward.start()
+    send(CORE, y * 2 + 1 - c, 1).wait_recv()
+    send(CORE, (1 - y) * 2 + 1 - c, 2).wait_recv()
+    result = pltpu.make_async_copy(pairs, all_ref, local_sem)
+    result.start()
+    blocks = pairs.shape[0]
+    half = pairs.shape[1] // 2
+    ratio = query_ref.shape[0] // half
+
+    def group(g, carry):
+        rows = pl.ds(pl.multiple_of(g * HEAD_SIZE, HEAD_SIZE), HEAD_SIZE)
+        low = pl.ds(pl.multiple_of(half + g * HEAD_SIZE, HEAD_SIZE), HEAD_SIZE)
+        keys = [pairs[j, rows, :] for j in range(blocks)]
+        values = [pairs[j, low, :] for j in range(blocks)]
+        for r in range(ratio):
+            head = pl.ds(pl.multiple_of((g * ratio + r) * HEAD_SIZE, HEAD_SIZE), HEAD_SIZE)
+            probs = head_probs(query_ref[head, :], keys, bias)
+            total = matmul(values[0], probs[0].astype(bfloat))
+            for j in range(1, blocks):
+                total = total + matmul(values[j], probs[j].astype(bfloat))
+            mixed_ref[head, :] = total.astype(bfloat)
+        return carry
+
+    lax.fori_loop(0, half // HEAD_SIZE, group, 0)
+    for copy in (across, core, onward):
+        copy.wait_send()
+    result.wait()
+
+
+def attend(query, own_pairs, lengths):
+    bfloat = jnp.bfloat16
+    dma = pltpu.SemaphoreType.DMA
+    anywhere = pl.BlockSpec(memory_space=pl.ANY)
+    vmem = pl.BlockSpec(memory_space=pltpu.VMEM)
+    pairs = (4, *own_pairs.shape)
+    keys = own_pairs.shape[1]
+    return pl.pallas_call(
+        attend_kernel,
+        out_shape=(
+            jax.ShapeDtypeStruct(query.shape, bfloat),
+            jax.ShapeDtypeStruct(pairs, bfloat),
+        ),
+        in_specs=[vmem, anywhere, pl.BlockSpec(memory_space=pltpu.SMEM)],
+        out_specs=(vmem, anywhere),
+        scratch_shapes=[
+            pltpu.VMEM(pairs, bfloat),
+            pltpu.VMEM((4, keys, query.shape[1]), jnp.float32),
+            dma,
+            dma((3,)),
+            dma((4,)),
+        ],
+        compiler_params=pltpu.CompilerParams(
+            collective_id=3, has_side_effects=True, vmem_limit_bytes=40 * 2**20
+        ),
+        name="attend",
+    )(query, own_pairs, lengths)
+
+
+def attend_back_kernel(swap, *refs):
+    query_ref, pairs_ref, grad_ref, length_ref, *refs = refs
+    sources, refs = refs[:swap], refs[swap:]
+    query_out, pairs_out, *refs = refs
+    targets, refs = refs[:swap], refs[swap:]
+    parts, core_got, y_got, bias, swap_send, swap_recv, core_send, core_recv, y_send, y_recv = refs
+    bfloat = jnp.bfloat16
+    single = jnp.float32
+    y, c, _, _, device, _ = place()
+    mine = y * 2 + c
+    kinds = (ACROSS, CORE, DP) if swap else (ACROSS, CORE)
+    barrier = pltpu.get_barrier_semaphore()
+    for kind in kinds:
+        pl.semaphore_signal(barrier, inc=1, device_id=device(kind), device_id_type=MESH_ID)
+    pl.semaphore_wait(barrier, len(kinds))
+    swaps = swap_copies(sources, targets, 0, device, swap_send, swap_recv)
+    for copy in swaps:
+        copy.start()
+    fill_bias(length_ref, bias, mine)
+    blocks = pairs_ref.shape[0]
+    half = pairs_ref.shape[1] // 2
+    ratio = query_ref.shape[0] // half
+    groups = half // HEAD_SIZE
+    turns = parts.shape[1]
+    per_turn = groups // turns
+    quarter = half // turns
+
+    def to_core(yy, turn):
+        return pltpu.make_async_remote_copy(
+            src_ref=parts.at[yy * 2 + 1 - c, turn],
+            dst_ref=core_got.at[turn, yy],
+            send_sem=core_send.at[turn, yy],
+            recv_sem=core_recv.at[turn, yy],
+            device_id=device(CORE),
+            device_id_type=MESH_ID,
+        )
+
+    def to_across(turn):
+        return pltpu.make_async_remote_copy(
+            src_ref=parts.at[(1 - y) * 2 + c, turn],
+            dst_ref=y_got.at[turn],
+            send_sem=y_send.at[turn],
+            recv_sem=y_recv.at[turn],
+            device_id=device(ACROSS),
+            device_id_type=MESH_ID,
+        )
+
+    def core_stage(turn):
+        to_core(1 - y, turn).start()
+        to_core(y, turn).start()
+
+    def across_stage(turn):
+        to_core(1 - y, turn).wait_recv()
+        slot = (1 - y) * 2 + c
+        parts[slot, turn] = (
+            parts[slot, turn].astype(single) + core_got[turn, 1 - y].astype(single)
+        ).astype(bfloat)
+        to_across(turn).start()
+
+    def last_stage(turn):
+        to_core(y, turn).wait_recv()
+        to_across(turn).wait_recv()
+        pairs_out[turn] = (
+            parts[mine, turn].astype(single)
+            + core_got[turn, y].astype(single)
+            + y_got[turn].astype(single)
+        )
+
+    def group(g, carry):
+        rows = pl.ds(pl.multiple_of(g * HEAD_SIZE, HEAD_SIZE), HEAD_SIZE)
+        low = pl.ds(pl.multiple_of(half + g * HEAD_SIZE, HEAD_SIZE), HEAD_SIZE)
+        keys = [pairs_ref[j, rows, :] for j in range(blocks)]
+        values = [pairs_ref[j, low, :] for j in range(blocks)]
+        grad_keys = [None] * blocks
+        grad_values = [None] * blocks
+        for r in range(ratio):
+            head = pl.ds(pl.multiple_of((g * ratio + r) * HEAD_SIZE, HEAD_SIZE), HEAD_SIZE)
+            query = query_ref[head, :]
+            grad = grad_ref[head, :]
+            probs = head_probs(query, keys, bias)
+            grad_probs = [contract_rows(value, grad) for value in values]
+            delta = jnp.sum(probs[0] * grad_probs[0], axis=0, keepdims=True)
+            for j in range(1, blocks):
+                delta = delta + jnp.sum(probs[j] * grad_probs[j], axis=0, keepdims=True)
+            grad_query = None
+            for j in range(blocks):
+                low_probs = probs[j].astype(bfloat)
+                grad_score = (probs[j] * (grad_probs[j] - delta)).astype(bfloat)
+                terms = (
+                    matmul(keys[j], grad_score),
+                    contract_last(query, grad_score),
+                    contract_last(grad, low_probs),
+                )
+                grad_query = terms[0] if j == 0 else grad_query + terms[0]
+                grad_keys[j] = terms[1] if r == 0 else grad_keys[j] + terms[1]
+                grad_values[j] = terms[2] if r == 0 else grad_values[j] + terms[2]
+            query_out[head, :] = grad_query * HEAD_SIZE ** (-0.5)
+        turn = g // per_turn
+        at = pl.multiple_of((g % per_turn) * HEAD_SIZE, HEAD_SIZE)
+        for j in range(blocks):
+            parts[j, turn, pl.ds(at, HEAD_SIZE), :] = grad_keys[j].astype(bfloat)
+            parts[j, turn, pl.ds(quarter + at, HEAD_SIZE), :] = grad_values[j].astype(bfloat)
+        for index in range(turns - 1):
+
+            @pl.when(g == (index + 1) * per_turn - 1)
+            def _():
+                core_stage(index)
+
+            @pl.when(g == (index + 1) * per_turn)
+            def _():
+                across_stage(index)
+
+        return carry
+
+    lax.fori_loop(0, groups, group, 0)
+    core_stage(turns - 1)
+    across_stage(turns - 1)
+    for turn in range(turns):
+        last_stage(turn)
+    for turn in range(turns):
+        to_core(y, turn).wait_send()
+        to_core(1 - y, turn).wait_send()
+        to_across(turn).wait_send()
+    for copy in swaps:
+        copy.wait()
+
+
+def attend_back(query, pairs, grad, lengths, expert_grads):
+    bfloat = jnp.bfloat16
+    single = jnp.float32
+    dma = pltpu.SemaphoreType.DMA
+    anywhere = pl.BlockSpec(memory_space=pl.ANY)
+    vmem = pl.BlockSpec(memory_space=pltpu.VMEM)
+    swap = len(expert_grads)
+    blocks, rows, keys = pairs.shape
+    turns = 2
+    part = (turns, rows // turns, keys)
+    halves = [(x.shape[1] // 2, x.shape[2]) for x in expert_grads]
+    return pl.pallas_call(
+        functools.partial(attend_back_kernel, swap),
+        out_shape=(
+            jax.ShapeDtypeStruct(query.shape, single),
+            jax.ShapeDtypeStruct(part, single),
+            *(jax.ShapeDtypeStruct(shape, bfloat) for shape in halves),
+        ),
+        in_specs=[vmem, vmem, vmem, pl.BlockSpec(memory_space=pltpu.SMEM)] + [anywhere] * swap,
+        out_specs=(vmem, vmem, *([anywhere] * swap)),
+        scratch_shapes=[
+            pltpu.VMEM((blocks, *part), bfloat),
+            pltpu.VMEM((turns, 2, *part[1:]), bfloat),
+            pltpu.VMEM(part, bfloat),
+            pltpu.VMEM((blocks, keys, query.shape[1]), single),
+            dma((3,)),
+            dma((3,)),
+            dma((turns, 2)),
+            dma((turns, 2)),
+            dma((turns,)),
+            dma((turns,)),
+        ],
+        compiler_params=pltpu.CompilerParams(
+            collective_id=4, has_side_effects=True, vmem_limit_bytes=48 * 2**20
+        ),
+        name="attend_back",
+    )(query, pairs, grad, lengths, *expert_grads)
 
 
 def experts_kernel(
@@ -1118,20 +1390,19 @@
     w_down,
     cotangent,
 ):
-    query_groups = tokens.shape[0]
-    sequence_per_device = tokens.shape[1]
+    tokens_own = tokens.shape[1]
+    exp_count = lax.axis_size("expert")
     ctx_count = lax.axis_size("context")
-    exp_count = lax.axis_size("expert")
     local_exp = w_gate.shape[0]
     experts = local_exp * ctx_count * exp_count
-    capacity = sequence_per_device * TOP * 3 // (2 * experts)
-    sequence_total = sequence_per_device * ctx_count
-    group_ratio = QUERY_HEADS // KEY_VALUE_HEADS
-    scale = HEAD_SIZE ** (-0.5)
+    capacity = tokens_own * TOP * 3 // (2 * experts)
     bfloat = jnp.bfloat16
     single = jnp.float32
-    proj_width = w_query.shape[1] + key_weight.shape[1] + value_weight.shape[1]
+    query_width = w_query.shape[1]
+    key_width = key_weight.shape[1]
+    proj_width = query_width + 2 * key_width
     own_rows = w_query.shape[0]
+    pair = lax.axis_size("dp") == 2
     small = jnp.concatenate(
         [
             w_router,
@@ -1141,7 +1412,7 @@
         ],
         axis=1,
     )
-    if lax.axis_size("dp") == 2:
+    if pair:
         packed = routes.reshape(-1, 64).astype(bfloat)
         packed = jnp.pad(packed, ((0, own_rows - packed.shape[0]), (0, 0)))
         early, late = gather_weights(
@@ -1150,9 +1421,9 @@
         routes_all = lax.dynamic_slice(
             early,
             (lax.axis_index("dp") * 16, 0, proj_width + 64),
-            (16, sequence_per_device * TOP // 64, 64),
-        )
-        routes_all = routes_all.astype(jnp.int32).reshape(16, sequence_per_device, TOP)
+            (16, tokens_own * TOP // 64, 64),
+        )
+        routes_all = routes_all.astype(jnp.int32).reshape(16, tokens_own, TOP)
         routes_all = routes_all.swapaxes(1, 2)
         early = early.reshape(-1, early.shape[2])
         out_w = late.reshape(-1, late.shape[2])
@@ -1161,180 +1432,76 @@
         early = lax.all_gather(early, EVERY, axis=0, tiled=True)
         out_w = lax.all_gather(w_out, EVERY, axis=0, tiled=True)
         routes_all = lax.all_gather(routes[0].T, GROUP, axis=0, tiled=False)
+    positions = lax.axis_index("context") * tokens_own + jnp.arange(tokens_own, dtype=jnp.int32)
+    valid = (positions < lengths[0]).astype(single)[:, None]
+    grad_final = cotangent[0].astype(single) * valid
+    final_low, early = lax.optimization_barrier((grad_final.astype(bfloat), early))
+    final_all = lax.all_gather(final_low, GROUP, axis=0, tiled=False)
     proj_w = early[:, :proj_width]
     router_w = early[:, proj_width : proj_width + experts]
-    gain_one = early[:, proj_width + experts]
-    gain_two = early[:, proj_width + experts + 1]
-    gain_one = gain_one.astype(single)
-    gain_two = gain_two.astype(single)
-    positions = lax.axis_index("context") * sequence_per_device + jnp.arange(
-        sequence_per_device, dtype=jnp.int32
-    )
-    key_pos = jnp.arange(sequence_total, dtype=jnp.int32)
-    valid = (positions[None, :] < lengths[:, None]).astype(single)[..., None]
-    cosine_table, sine_table = rotation_tables(positions)
-    inputs = tokens.astype(single)
+    gain_one = early[:, proj_width + experts].astype(single)
+    gain_two = early[:, proj_width + experts + 1].astype(single)
+    cosine, sine = rotation_tables(positions)
+
+    inputs = tokens[0].astype(single)
     inverse_one = lax.rsqrt(jnp.mean(inputs * inputs, axis=-1, keepdims=True) + epsilon)
     normed_one = inputs * inverse_one
     hidden_one = (normed_one * gain_one).astype(bfloat)
-    projected = jnp.einsum("gsd,de->gse", hidden_one, proj_w, preferred_element_type=single)
-    query_lin = projected[..., : w_query.shape[1]]
-    key_linear = projected[..., w_query.shape[1] : w_query.shape[1] + key_weight.shape[1]]
-    value_lower = projected[..., -value_weight.shape[1] :].astype(bfloat)
-    query_rotated = (
-        apply_rotation(
-            query_lin.reshape(query_groups, sequence_per_device, QUERY_HEADS, HEAD_SIZE),
-            cosine_table,
-            sine_table,
-        )
-        .astype(bfloat)
-        .reshape(query_groups, sequence_per_device, QUERY_HEADS * HEAD_SIZE)
+    projected = jnp.einsum("de,sd->es", proj_w, hidden_one, preferred_element_type=single)
+    rotated = apply_rotation(projected[: query_width + key_width], cosine, sine).astype(bfloat)
+    query = rotated[:query_width] * HEAD_SIZE ** (-0.5)
+    own_pairs = jnp.concatenate(
+        [rotated[query_width:], projected[query_width + key_width :].astype(bfloat)], axis=0
     )
-    key_rotated = (
-        apply_rotation(
-            key_linear.reshape(query_groups, sequence_per_device, KEY_VALUE_HEADS, HEAD_SIZE),
-            cosine_table,
-            sine_table,
-        )
-        .astype(bfloat)
-        .reshape(query_groups, sequence_per_device, KEY_VALUE_HEADS * HEAD_SIZE)
-    )
-    gathered_keys, gathered_values = (
-        lax.all_gather(key_rotated, "context", axis=1, tiled=True),
-        lax.all_gather(value_lower, "context", axis=1, tiled=True),
-    )
-
-    final_low = (cotangent.astype(single) * valid).astype(bfloat)
-    final_low, gathered_keys, gathered_values = lax.optimization_barrier(
-        (final_low, gathered_keys, gathered_values)
-    )
-    final_all = lax.all_gather(final_low[0], GROUP, axis=0, tiled=False)
-
-    def attn_scores(slot_index):
-        query_per_head = query_rotated[slot_index].reshape(
-            sequence_per_device, KEY_VALUE_HEADS, group_ratio, HEAD_SIZE
-        )
-        key_per_head = gathered_keys[slot_index].reshape(sequence_total, KEY_VALUE_HEADS, HEAD_SIZE)
-        scores = scale * jnp.einsum(
-            "skrd,tkd->krst", query_per_head, key_per_head, preferred_element_type=single
-        )
-        allowed = (key_pos[None, :] <= positions[:, None]) & (
-            key_pos[None, :] < lengths[slot_index]
-        )
-        return (jnp.where(allowed, scores, floor_score), allowed, query_per_head, key_per_head)
-
-    slot_index = 0
-    scores, allowed, query_per_head, key_per_head = attn_scores(slot_index)
-    peak = jnp.max(scores, axis=-1, keepdims=True)
-    raised = jnp.exp(scores - peak)
-    total = jnp.sum(raised, axis=-1, keepdims=True)
-    probs = raised / total
-    value_per_head = gathered_values[slot_index].reshape(sequence_total, KEY_VALUE_HEADS, HEAD_SIZE)
-    mixed_g = jnp.einsum(
-        "krst,tkd->skrd", probs.astype(bfloat), value_per_head, preferred_element_type=single
-    )
-    mixed_list = [mixed_g.reshape(sequence_per_device, QUERY_HEADS * HEAD_SIZE)]
-    lse_list = [peak + jnp.log(total)]
-    mixed_low = jnp.stack(mixed_list).astype(bfloat)
-    resid = inputs + jnp.einsum("gse,ed->gsd", mixed_low, out_w, preferred_element_type=single)
+    mixed, pairs = attend(query, own_pairs, lengths)
+    resid = inputs + jnp.einsum("es,ed->sd", mixed, out_w, preferred_element_type=single)
     inverse_two = lax.rsqrt(jnp.mean(resid * resid, axis=-1, keepdims=True) + epsilon)
     normed_two = resid * inverse_two
     hidden_two = (normed_two * gain_two).astype(bfloat)
-    logits = jnp.einsum("gsd,de->gse", hidden_two, router_w, preferred_element_type=single)
-    matches = routes[..., None] == jnp.arange(experts, dtype=jnp.int32)
-    chosen = jnp.sum(jnp.where(matches, logits[:, :, None, :], 0.0), axis=-1)
-    gates = jax.nn.softmax(chosen, axis=-1)
+
     grad_hidden, combined, scores, grad_w_gate, grad_w_up, grad_w_down = experts_on_owner(
-        hidden_two[0], final_all, routes_all, router_w.T, w_gate, w_up, w_down, capacity
+        hidden_two, final_all, routes_all, router_w.T, w_gate, w_up, w_down, capacity
     )
     combined = lax.psum_scatter(combined, GROUP, scatter_dimension=0, tiled=False)
-    scores = scores[:, :local_exp]
-    scores = lax.all_to_all(scores, GROUP, split_axis=0, concat_axis=0, tiled=True)
-    scores = scores.reshape(experts, sequence_per_device)
-    grad_final = cotangent.astype(single) * valid
-    grad_gates = jnp.sum(jnp.where(matches, scores.T[None, :, None, :], 0.0), axis=-1)
+    scores = lax.all_to_all(scores[:, :local_exp], GROUP, split_axis=0, concat_axis=0, tiled=True)
+    grad_gates = scores.reshape(experts, tokens_own).T
+
+    routed = jnp.any(routes[0][:, :, None] == jnp.arange(experts, dtype=jnp.int32), axis=1)
+    logits = jnp.einsum("sd,de->se", hidden_two, router_w, preferred_element_type=single)
+    gates = jax.nn.softmax(jnp.where(routed, logits, floor_score), axis=-1)
+    gates = jnp.where(routed, gates, 0.0)
     gate_mean = jnp.sum(gates * grad_gates, axis=-1, keepdims=True)
-    grad_chosen = gates * (grad_gates - gate_mean)
-    grad_logits = jnp.sum(jnp.where(matches, grad_chosen[..., None], 0.0), axis=2).astype(bfloat)
-    grad_w_router = jnp.einsum(
-        "gsd,gse->de", hidden_two, grad_logits, preferred_element_type=single
+    grad_logits = (gates * (grad_gates - gate_mean)).astype(bfloat)
+    grad_w_router = jnp.einsum("sd,se->de", hidden_two, grad_logits, preferred_element_type=single)
+    grad_hidden_two = grad_hidden.astype(single) + jnp.einsum(
+        "se,de->sd", grad_logits, router_w, preferred_element_type=single
     )
-    grad_hidden_two = grad_hidden.astype(single)[None]
-    grad_hidden_two = grad_hidden_two + jnp.einsum(
-        "gse,de->gsd", grad_logits, router_w, preferred_element_type=single
-    )
-    grad_gain_ffn = jnp.sum(grad_hidden_two * normed_two, axis=(0, 1))
+    grad_gain_ffn = jnp.sum(grad_hidden_two * normed_two, axis=0)
     grad_resid = norm_back(grad_hidden_two * gain_two, normed_two, inverse_two) + grad_final
     grad_attn = grad_resid.astype(bfloat)
-    grad_w_out = jnp.einsum("gse,gsd->ed", mixed_low, grad_attn, preferred_element_type=single)
-    mixed_gradient = jnp.einsum(
-        "gsd,ed->gse", grad_attn, out_w, preferred_element_type=single
+
+    grad_out_w = jnp.einsum("es,sd->ed", mixed, grad_attn, preferred_element_type=single)
+    grad_mixed = jnp.einsum("ed,sd->es", out_w, grad_attn, preferred_element_type=single)
+    expert_grads = (grad_w_gate, grad_w_up, grad_w_down)
+    grad_query, grad_pairs, *first_got = attend_back(
+        query, pairs, grad_mixed.astype(bfloat), lengths, expert_grads if pair else ()
+    )
+    grad_pairs = grad_pairs.reshape(2, 2, key_width // 2, tokens_own)
+    grad_key = grad_pairs[:, 0].reshape(key_width, tokens_own)
+    grad_value = grad_pairs[:, 1].reshape(key_width, tokens_own)
+    grad_proj = jnp.concatenate(
+        [
+            inverse_rotation(grad_query, cosine, sine),
+            inverse_rotation(grad_key, cosine, sine),
+            grad_value,
+        ],
+        axis=0,
     ).astype(bfloat)
-    slot_index = 0
-    scores, allowed, query_per_head, key_per_head = attn_scores(slot_index)
-    probs = jnp.where(allowed, jnp.exp(scores - lse_list[slot_index]), 0.0)
-    value_per_head = gathered_values[slot_index].reshape(sequence_total, KEY_VALUE_HEADS, HEAD_SIZE)
-    head_gradient = mixed_gradient[slot_index].reshape(
-        sequence_per_device, KEY_VALUE_HEADS, group_ratio, HEAD_SIZE
-    )
-    grad_probs = jnp.einsum(
-        "skrd,tkd->krst", head_gradient, value_per_head, preferred_element_type=single
-    )
-    row_delta = jnp.sum(probs * grad_probs, axis=-1, keepdims=True)
-    grad_scores = (probs * (grad_probs - row_delta)).astype(bfloat)
-    grad_queries = [
-        (
-            scale
-            * jnp.einsum("krst,tkd->skrd", grad_scores, key_per_head, preferred_element_type=single)
-        ).reshape(sequence_per_device, QUERY_HEADS, HEAD_SIZE)
-    ]
-    grad_keys = [
-        (
-            scale
-            * jnp.einsum(
-                "krst,skrd->tkd", grad_scores, query_per_head, preferred_element_type=single
-            )
-        ).reshape(sequence_total, KEY_VALUE_HEADS * HEAD_SIZE)
-    ]
-    grad_values = [
-        jnp.einsum(
-            "krst,skrd->tkd", probs.astype(bfloat), head_gradient, preferred_element_type=single
-        ).reshape(sequence_total, KEY_VALUE_HEADS * HEAD_SIZE)
-    ]
-    key_gradient_rows, value_grad = (
-        lax.psum_scatter(
-            jnp.stack(grad_keys).astype(jnp.bfloat16), "context", scatter_dimension=1, tiled=True
-        ).astype(jnp.float32),
-        lax.psum_scatter(
-            jnp.stack(grad_values).astype(jnp.bfloat16), "context", scatter_dimension=1, tiled=True
-        ).astype(jnp.float32),
-    )
-    grad_query_lin = (
-        inverse_rotation(jnp.stack(grad_queries), cosine_table, sine_table)
-        .astype(bfloat)
-        .reshape(query_groups, sequence_per_device, QUERY_HEADS * HEAD_SIZE)
-    )
-    grad_key_lin = (
-        inverse_rotation(
-            key_gradient_rows.reshape(
-                query_groups, sequence_per_device, KEY_VALUE_HEADS, HEAD_SIZE
-            ),
-            cosine_table,
-            sine_table,
-        )
-        .astype(bfloat)
-        .reshape(query_groups, sequence_per_device, KEY_VALUE_HEADS * HEAD_SIZE)
-    )
-    grad_value_low = value_grad.astype(bfloat)
-    grad_proj = jnp.concatenate([grad_query_lin, grad_key_lin, grad_value_low], axis=-1)
-    grad_proj_w = jnp.einsum("gsd,gse->de", hidden_one, grad_proj, preferred_element_type=single)
-    grad_hidden_one = jnp.einsum("gse,de->gsd", grad_proj, proj_w, preferred_element_type=single)
-    grad_gain_attn = jnp.sum(grad_hidden_one * normed_one, axis=(0, 1))
+    grad_proj_w = jnp.einsum("sd,es->de", hidden_one, grad_proj, preferred_element_type=single)
+    grad_hidden_one = jnp.einsum("es,de->sd", grad_proj, proj_w, preferred_element_type=single)
+    grad_gain_attn = jnp.sum(grad_hidden_one * normed_one, axis=0)
     grad_tokens = norm_back(grad_hidden_one * gain_one, normed_one, inverse_one) + grad_resid
-    grad_proj_w = grad_proj_w.astype(bfloat)
-    grad_out_w = grad_w_out.astype(bfloat)
-    combined, grad_proj_w = lax.optimization_barrier((combined, grad_proj_w))
-    block_out = (valid * (resid + combined.astype(single)[None])).astype(bfloat)
+
     grad_small = jnp.concatenate(
         [
             grad_w_router,
@@ -1344,19 +1511,18 @@
         ],
         axis=1,
     ).astype(bfloat)
-    if lax.axis_size("dp") == 2:
-        summed, *got = sum_gradients(
-            grad_proj_w, grad_small, grad_out_w, grad_w_gate, grad_w_up, grad_w_down
-        )
-
-        def both(whole, other):
+    grad_proj_w = grad_proj_w.astype(bfloat)
+    grad_out_w = grad_out_w.astype(bfloat)
+    if pair:
+        summed, *last_got = sum_gradients(grad_proj_w, grad_small, grad_out_w, *expert_grads)
+
+        def both(whole, *others):
             half = whole.shape[1] // 2
             own = lax.dynamic_slice_in_dim(whole, lax.axis_index("dp") * half, half, axis=1)
-            return own.astype(single) + other.astype(single)
+            return own.astype(single) + jnp.stack(others).astype(single)
 
         expert_sums = tuple(
-            both(whole, other)
-            for whole, other in zip((grad_w_gate, grad_w_up, grad_w_down), got)
+            both(whole, *others) for whole, *others in zip(expert_grads, first_got, last_got)
         )
     else:
         summed = lax.psum_scatter(
@@ -1367,31 +1533,21 @@
         ).astype(single)
         expert_sums = tuple(
             lax.psum_scatter(x, "dp", scatter_dimension=1, tiled=True).astype(single)
-            for x in (grad_w_gate, grad_w_up, grad_w_down)
-        )
-    ends = (w_query.shape[1], proj_width - value_weight.shape[1], proj_width)
-    shard_grads = (
+            for x in expert_grads
+        )
+    combined, summed = lax.optimization_barrier((combined, summed))
+    block_out = (valid * (resid + combined.astype(single))).astype(bfloat)
+    return (
+        block_out[None],
+        grad_tokens[None],
         summed[:, proj_width + experts],
-        summed[:, : ends[0]],
-        summed[:, ends[0] : ends[1]],
-        summed[:, ends[1] : ends[2]],
+        summed[:, :query_width],
+        summed[:, query_width : query_width + key_width],
+        summed[:, query_width + key_width : proj_width],
         summed[:, proj_width + 128 :],
         summed[:, proj_width + experts + 1],
         summed[:, proj_width : proj_width + experts],
-    )
-    return (
-        block_out,
-        grad_tokens,
-        shard_grads[0],
-        shard_grads[1],
-        shard_grads[2],
-        shard_grads[3],
-        shard_grads[4],
-        shard_grads[5],
-        shard_grads[6],
-        expert_sums[0],
-        expert_sums[1],
-        expert_sums[2],
+        *expert_sums,
     )
 
 

time: 826 us -> 612 us (0.74)
  waiting for transfers between devices: 236 us -> 45.3 us
  Pallas kernels: 374 us -> 445 us
  matrix products: 104 us -> 33.6 us
  other arithmetic: 52.1 us -> 22 us
    reduce_scatter x1, waiting for transfers between devices: 121 us -> 0.01 us  [on_device(): lax.psum_scatter(combined, GROUP, scatter_dimension=0, tiled=False)]
    pallas_call x0 -> x2, Pallas kernels: none -> 88.6 us  [the longest x1 56.8 us: attend_back(): pl.pallas_call(functools.partial(attend_back_kernel, swap), out_shape=(ja...]
    dot_general x15 -> x9, matrix products: 104 us -> 33.6 us  [the longest x1 7.3 us: on_device(): jnp.einsum('es,de->sd', grad_proj, proj_w, preferred_element_type=single)]
    all_gather x3 -> x1, waiting for transfers between devices: 87.6 us -> 38.8 us  [on_device(): final_all = lax.all_gather(final_low, GROUP, axis=0, tiled=False)]
    reduce_scatter x2 -> x0, waiting for transfers between devices: 20 us -> none  [the longest x1 20 us: on_device(): lax.psum_scatter(jnp.stack(grad_values).astype(jnp.bfloat16), 'context',...]
    pallas_call x1, Pallas kernels: 114 us -> 97 us  [sum_gradients(): pl.pallas_call(sums_kernel, out_shape=(jax.ShapeDtypeStruct((rows, width)...]
    convert_element_type x5 -> x6, other arithmetic: 20 us -> 5.07 us  [the longest x1 2.28 us: on_device(): grad_final.astype(bfloat)]
    reduce_sum x4 -> x1, other arithmetic: 11.5 us -> 0.03 us  [on_device(): gates = jax.nn.softmax(jnp.where(routed, logits, floor_score), axis=-1)]
  transfers between devices with their start and end apart: 7 -> 3, of which waited for: 6 -> 2; matrix products, arithmetic and copies ran while one was open for 12% -> 12% of each run, Pallas kernels for 0% -> 31%
where the time goes in v3:
time: 612 us; the launch traced here: 604 us
  Pallas kernels  445 us (73%)
  waiting for transfers between devices  45.3 us (7%)
  local copies, waits for them, and re-layouts  37.7 us (6%)
  matrix products  33.6 us (5%)
  other arithmetic  22 us (4%)
  between operations  15.9 us (3%)
    pallas_call x1, Pallas kernels, experts_on_owner(): pl.pallas_call(experts_kernel, out_shape=(jax.ShapeDtypeStruct((tokens_bl...  197 us
    pallas_call x1, Pallas kernels, sum_gradients(): pl.pallas_call(sums_kernel, out_shape=(jax.ShapeDtypeStruct((rows, width)...  97 us
    pallas_call x1, Pallas kernels, gather_weights(): pl.pallas_call(gather_kernel, out_shape=(jax.ShapeDtypeStruct(early, bflo...  62.9 us
    pallas_call x1, Pallas kernels, attend_back(): pl.pallas_call(functools.partial(attend_back_kernel, swap), out_shape=(ja...  56.8 us
    all_gather x1, waiting for transfers between devices, on_device(): final_all = lax.all_gather(final_low, GROUP, axis=0, tiled=False)  38.8 us
    pallas_call x1, Pallas kernels, attend(): pl.pallas_call(attend_kernel, out_shape=(jax.ShapeDtypeStruct(query.shape...  31.8 us
  transfers between devices with their start and end apart: 3, of which 2 were waited for; matrix products, arithmetic and copies ran while one was open for 12% of the time, Pallas kernels for 31%

profile of v3, /device:TPU:0, one launch (start us, length us, event | category | flops | bytes accessed | tf_op | source)
XLA Modules:
  0.0 603.9 jit_solution(7850223471860698406)
XLA Ops:
  8.0 0.8 copy.59
  8.8 0.8 copy.60
  9.6 0.8 copy.61
  10.3 0.7 convert_element_type.125
  11.3 2.3 fusion.17
  13.7 62.9 %gather_weights.1 = (bf16[32,48,2688]{2,1,0:T(8,128)(2,1)S(1)}, bf16[32,48,1536]{2,1,0:T(8,128)(2,1)S(1)}) custom-call(bf16[48,1536]{1,0:T(8,128)(2,1)S(1)} %copy-done.10, bf16[48,512]{1,0:T(8,128)(2,1)S(1)} %copy-done.12, bf16[48,512]{1,0:T(8,128)(2,1)S(1)} %copy-done.13, bf16[48,128]{1,0:T(8,128)(2,1)S(1)} %concatenate.21.small_ref, ...), custom_call_target="tpu_custom_call" | custom-call | tf_op jit(solution)/shard_map/gather_weights/pallas_call | solution.py:323
  76.6 2.1 copy-done.3
  78.7 3.2 copy-done.4
  82.0 1.7 convert_reduce_fusion
  83.9 5.7 fusion.2
  89.7 1.5 copy-done.24
  91.2 11.9 %copy.64 = bf16[1536,2688]{0,1:T(8,128)(2,1)} copy(bf16[1536,2688]{1,0:T(8,128)(2,1)} %bitcast.72) | data formatting | bytes 16515072 | tf_op jit(solution)/shard_map/optimization_barrier | solution.py:1438
  103.0 1.2 dynamic-slice_convert_fusion
  104.2 1.3 copy.62
  105.6 2.2 copy.63
  108.5 31.8 %attend.1 = (bf16[1536,256]{1,0:T(8,128)(2,1)S(1)}, bf16[4,1024,256]{2,1,0:T(8,128)(2,1)S(1)}) custom-call(bf16[1536,256]{1,0:T(8,128)(2,1)S(1)} %bitcast.74, bf16[1024,256]{1,0:T(8,128)(2,1)S(1)} %pad_maximum_fusion.4.own_ref, s32[1]{0:T(128)} %copy.69.length_ref.refs_3_), custom_call_target="tpu_custom_call" | custom-call | tf_op jit(solution)/shard_map/attend/pallas_call | solution.py:648
  140.4 1.5 multiply_reduce_fusion.2
  142.0 1.7 slice_bitcast_fusion.router_ref
  143.6 1.1 multiply_convert_fusion.1.hidden_ref
  144.7 38.8 %all-gather.3.cloned.1.call-done = bf16[4096,1536]{1,0:T(8,128)(2,1)} async-done(((bf16[256,1536]{1,0:T(8,128)(2,1)}), bf16[4096,1536]{1,0:T(8,128)(2,1)}) %all-gather.3.cloned.1.call-update) | async-done | bytes 12582928 | tf_op jit(solution)/shard_map/all_gather | solution.py:1439
  183.5 197.0 %experts.1 = (bf16[256,1536]{1,0:T(8,128)(2,1)}, bf16[16,256,1536]{2,1,0:T(8,128)(2,1)}, f32[16,8,256]{2,1,0:T(8,128)}, bf16[2,1536,512]{2,1,0:T(8,128)(2,1)}, b...) custom-call(bf16[256,1536]{1,0:T(8,128)(2,1)} %multiply_convert_fusion.1.hidden_ref, ...), custom_call_target="tpu_custom_call" | custom-call | tf_op jit(solution)/shard_map/experts/pallas_call | solution.py:1332
  380.6 0.6 copy-done.32
  381.7 1.2 fusion.38
  382.9 1.5 slice.89
  384.4 3.8 all-to-all-start
  388.3 6.5 %all-to-all-done = f32[16,2,256]{2,1,0:T(2,128)S(1)} async-done(((f32[16,2,256]{2,1,0:T(2,128)}), f32[16,2,256]{2,1,0:T(2,128)S(1)}, u32[]{:S(2)}, u32[]{:S(2)}) %all-to-all-start) | async-done | bytes 32800 | tf_op jit(solution)/shard_map/all_to_all | solution.py:1466
  394.8 2.1 multiply_reduce_fusion
  397.5 5.0 convolution_convert_fusion.2.refs_2_
  402.5 56.8 %attend_back.1 = (f32[1536,256]{1,0:T(8,128)}, f32[2,512,256]{2,1,0:T(8,128)S(1)}, bf16[768,512]{1,0:T(8,128)(2,1)S(1)}, bf16[768,512]{1,0:T(8,128)(2,1)S(1)}, bf16[256,1536]{1,0:T(8,128)(2,1)S(1)}) custom-call(bf16[1536,256]{1,0:T(8,128)(2,1)S(1)} %bitcast.75, bf16[4,1024,256]{2,1,0:T(8,128)(2,1)} %copy-done.7, ...), custom_call_target="tpu_custom_call" | custom-call | tf_op jit(solution)/shard_map/attend_back/pallas_call | solution.py:808
  459.3 0.9 copy-done.8
  460.1 0.7 slice.151
  460.9 1.5 concatenate.29
  462.5 1.7 subtract_convert_fusion.1
  464.4 7.3 %fusion.10 = (f32[256]{0:T(256)S(1)}, bf16[1536]{0:T(1024)(128)(2,1)S(1)}, f32[256,1536]{1,0:T(8,128)}) fusion(bf16[1,256,1536]{2,1,0:T(8,128)(2,1)S(1)} %copy-done.21, f32[1536]{0:T(1024)S(1)} %get-tuple-element.107, f32[256]{0:T(256)S(1)} %add_rsqrt_fusion.1, bf16[1536,2688]{1,0:T(8,128)(2,1)} %bitcast.73, bf16[512,256]{1,0:T(8,128)(2,1)S(1)} %bitcast.94, ...), kind=kOutput, calls=%fused_computation.21 | convolution fusion | flops 2019948800 | bytes 11545600 | tf_op jit(solution)/shard_map/es,de->sd/dot_general | solution.py:1501
  471.7 1.5 concatenate.28
  473.2 1.4 convolution_convert_fusion.3
  474.5 0.9 copy.65
  475.5 1.7 maximum_maximum_fusion.small_ref
  477.2 3.5 convolution_convert_fusion.1
  480.8 5.9 convolution_convert_fusion
  486.8 97.0 %sum_gradients.1 = (f32[48,4224]{1,0:T(8,128)S(1)}, bf16[768,512]{1,0:T(8,128)(2,1)S(1)}, bf16[768,512]{1,0:T(8,128)(2,1)S(1)}, bf16[256,1536]{1,0:T(8,128)(2,1)S(1)}) custom-call(bf16[2,16,48,2560]{3,2,1,0:T(8,128)(2,1)} %bitcast.84, bf16[2,16,48,128]{3,2,1,0:T(8,128)(2,1)S(1)} %maximum_maximum_fusion.small_ref, bf16[2,16,48,1536]{3,2,1,0:T(8,128)(2,1)} %bitcast.85, ...), custom_call_target="tpu_custom_call" | custom-call | tf_op jit(solution)/shard_map/sum_gradients/pallas_call | solution.py:525
  583.8 3.7 convert_add_fusion.1
  587.6 2.1 convert_add_fusion
  589.7 0.7 slice_reduce_fusion
  590.4 0.9 fusion.36
  591.2 0.7 fusion.37
  591.9 0.7 copy.68
  592.6 4.0 fusion.14
  (105 shorter events, 3.0 us)
Async XLA Ops:
  7.2 6.5 %copy-start.10 = (bf16[48,1536]{1,0:T(8,128)(2,1)S(1)}, bf16[48,1536]{1,0:T(8,128)(2,1)}, u32[]{:S(2)}) copy-start(bf16[48,1536]{1,0:T(8,128)(2,1)} %query_ref.1) | copy-start | bytes 442372
  7.2 6.5 %copy-start.12 = (bf16[48,512]{1,0:T(8,128)(2,1)S(1)}, bf16[48,512]{1,0:T(8,128)(2,1)}, u32[]{:S(2)}) copy-start(bf16[48,512]{1,0:T(8,128)(2,1)} %key_ref.1) | copy-start | bytes 147460
  7.2 6.5 %copy-start.13 = (bf16[48,512]{1,0:T(8,128)(2,1)S(1)}, bf16[48,512]{1,0:T(8,128)(2,1)}, u32[]{:S(2)}) copy-start(bf16[48,512]{1,0:T(8,128)(2,1)} %value_ref.1) | copy-start | bytes 147460
  7.2 6.5 %copy-start.11 = (bf16[48,1536]{1,0:T(8,128)(2,1)S(1)}, bf16[48,1536]{1,0:T(8,128)(2,1)}, u32[]{:S(2)}) copy-start(bf16[48,1536]{1,0:T(8,128)(2,1)} %out_ref.1) | copy-start | bytes 442372
  7.2 176.3 %all-gather.3.cloned.1.call-start = ((), (), s32[]{:S(2)}) async-start(), calls=%async_computation.3 | async-start | bytes 13369344 | tf_op jit(solution)/shard_map/all_gather | solution.py:1439
  11.3 72.4 %copy-start.19 = (bf16[1,256,1536]{2,1,0:T(8,128)(2,1)S(1)}, bf16[1,256,1536]{2,1,0:T(8,128)(2,1)}, u32[]{:S(2)}) copy-start(bf16[1,256,1536]{2,1,0:T(8,128)(2,1)} %param.14) | copy-start | bytes 2359300
  76.6 2.1 copy-start.3
  78.7 3.2 copy-start.4
  81.9 507.7 %reduce-scatter.2.cloned.1.call-start = ((), (), s32[]{:S(2)}) async-start(), calls=%async_computation.2 | async-start | bytes 13369344 | tf_op jit(solution)/shard_map/reduce_scatter | solution.py:1465
  89.6 1.5 copy-start.24
  103.0 4.9 slice-start.2
  104.2 36.2 %slice-start = ((s8[4718592]{0:T(1024)(128)(4,1)}), s8[524288]{0:T(1024)(128)(4,1)S(1)}, s32[]{:S(2)}) async-start(s8[4718592]{0:T(1024)(128)(4,1)} %bitcast.67), calls=%async_computation.4 | async-start | bytes 1048576
  108.0 32.4 %slice-start.1 = ((s8[4718592]{0:T(1024)(128)(4,1)}), s8[4194304]{0:T(1024)(128)(4,1)S(1)}, s32[]{:S(2)}) async-start(s8[4718592]{0:T(1024)(128)(4,1)} %bitcast.67), calls=%async_computation.5 | async-start | bytes 8388608
  108.4 32.0 %copy-start.20 = (bf16[1,256,1536]{2,1,0:T(8,128)(2,1)S(1)}, bf16[1,256,1536]{2,1,0:T(8,128)(2,1)}, u32[]{:S(2)}) copy-start(bf16[1,256,1536]{2,1,0:T(8,128)(2,1)} %param.14) | copy-start | bytes 2359300
  108.5 33.4 %copy-start.5 = (bf16[24,2,32,256]{3,2,1,0:T(8,128)(2,1)}, bf16[24,2,32,256]{3,2,1,0:T(8,128)(2,1)S(1)}, u32[]{:S(2)}) copy-start(bf16[24,2,32,256]{3,2,1,0:T(8,128)(2,1)S(1)} %fusion.19) | copy-start | bytes 2359300
  140.4 1.5 copy-start.7
  141.9 1.7 copy-start.14
  380.5 0.7 copy-start.32
  380.5 1.1 copy-start.23
  380.5 14.3 %copy-start.15 = (f32[256,1536]{1,0:T(8,128)S(1)}, f32[256,1536]{1,0:T(8,128)}, u32[]{:S(2)}) copy-start(f32[256,1536]{1,0:T(8,128)} %copy-done.14) | copy-start | bytes 4718596
  384.4 10.3 %all-to-all-start = ((f32[16,2,256]{2,1,0:T(2,128)}), f32[16,2,256]{2,1,0:T(2,128)S(1)}, u32[]{:S(2)}, u32[]{:S(2)}) async-start(f32[16,2,256]{2,1,0:T(2,128)} %slice.89), calls=%async_computation.1 | async-start | bytes 65536 | tf_op jit(solution)/shard_map/all_to_all | solution.py:1466
  394.8 2.1 copy-start.27
  397.5 5.0 copy-start.17
  397.5 5.0 copy-start.6
  459.3 0.9 copy-start.8
  462.5 1.9 copy-start.30
  462.5 1.9 copy-start.21
  462.5 1.9 copy-start.28
  464.3 7.3 %copy-start.25 = (bf16[24,2,32,256]{3,2,1,0:T(8,128)(2,1)}, bf16[24,2,32,256]{3,2,1,0:T(8,128)(2,1)S(1)}, u32[]{:S(2)}) copy-start(bf16[24,2,32,256]{3,2,1,0:T(8,128)(2,1)S(1)} %pad_maximum_fusion.1) | copy-start | bytes 2359300
  475.5 1.8 copy-start.18
  477.2 3.6 copy-start.26
  477.2 3.6 copy-start.29
  477.2 3.6 copy-start.31
  480.8 6.0 copy-start
  480.8 6.0 copy-start.1
  480.8 5.9 copy-start.2
  486.8 97.1 %copy-start.9 = (bf16[768,512]{1,0:T(8,128)(2,1)S(1)}, bf16[768,512]{1,0:T(8,128)(2,1)}, u32[]{:S(2)}) copy-start(bf16[768,512]{1,0:T(8,128)(2,1)} %copy-done.8) | copy-start | bytes 2359300
  587.5 5.0 copy-start.22
  589.7 2.9 copy-start.16
Sparse Core Ops, SparseCore 0:
  82.1 101.3 all-gather.2
  380.7 133.8 reduce-scatter.1

commit v4 on v3

--- a/solution.py
+++ b/solution.py
@@ -116,10 +116,10 @@
     pl.semaphore_wait(barrier, count)
 
 
-def swap_copies(sources, targets, j, device, send_sem, recv_sem):
+def swap_copies(pieces, device, send_sem, recv_sem):
     d = lax.axis_index("dp")
     copies = []
-    for index, (source, target) in enumerate(zip(sources, targets)):
+    for index, (source, j, target) in enumerate(pieces):
         half = target.shape[0]
         copies.append(
             pltpu.make_async_remote_copy(
@@ -134,272 +134,13 @@
     return copies
 
 
-def gather_kernel(
-    query_ref,
-    key_ref,
-    value_ref,
-    small_ref,
-    out_ref,
-    early_ref,
-    late_ref,
-    early,
-    late,
-    local_sem,
-    early_send,
-    early_core,
-    early_recv,
-    late_send,
-    late_dp,
-    late_recv,
-):
-    y, c, z, inner, device, per_side = place()
+def ring_sum(parts, core_got, y_got, z_got, dp_got, sems):
+    single = jnp.float32
+    core_send, core_recv, y_send, y_recv, z_send, z_recv, dp_send, dp_recv = sems
+    y, c, z, _, device, _ = place()
     d = lax.axis_index("dp")
-    mine = d * 16 + block_id(y, c, z)
-    loads = []
-    at = 0
-    for index, ref in enumerate((query_ref, key_ref, value_ref, small_ref)):
-        size = ref.shape[1]
-        loads.append(
-            pltpu.make_async_copy(ref, early.at[mine, :, pl.ds(at, size)], local_sem.at[index])
-        )
-        at += size
-    loads.append(pltpu.make_async_copy(out_ref, late.at[mine], local_sem.at[4]))
-    for copy in loads:
-        copy.start()
-    greet(per_side, device, 4 + inner, (DP,))
-    for copy in loads:
-        copy.wait()
-
-    def early_copy(kind, slot, sem):
-        return pltpu.make_async_remote_copy(
-            src_ref=early.at[slot],
-            dst_ref=early.at[slot],
-            send_sem=sem,
-            recv_sem=early_recv.at[slot],
-            device_id=device(kind),
-            device_id_type=MESH_ID,
-        )
-
-    def early_own(kind, block):
-        return early_copy(kind, d * 16 + block, early_send.at[kind, block])
-
-    def early_other(block):
-        return early_copy(CORE, (1 - d) * 16 + block, early_core.at[block])
-
-    def late_copy(kind, slot, sem):
-        return pltpu.make_async_remote_copy(
-            src_ref=late.at[slot],
-            dst_ref=late.at[slot],
-            send_sem=sem,
-            recv_sem=late_recv.at[slot],
-            device_id=device(kind),
-            device_id_type=MESH_ID,
-        )
-
-    def late_own(kind, plane, block):
-        slot = plane * 16 + block
-        return late_copy(kind, slot, late_send.at[kind, slot])
-
-    def along(kind, zz):
-        if kind == UP:
-            return jnp.logical_and(z < 3, zz <= z)
-        return jnp.logical_and(z > 0, zz >= z)
-
-    def fan(zz, act):
-        block = block_id(y, c, zz)
-        for kind in (UP, DOWN):
-
-            @pl.when(along(kind, zz))
-            def _():
-                act(early_own(kind, block))
-                act(late_own(kind, d, block))
-
-        for kind in (ACROSS, CORE):
-            act(early_own(kind, block))
-            act(late_own(kind, d, block))
-        act(early_own(DP, block))
-
-    def fan_other(zz, act):
-        block = block_id(y, c, zz)
-        for kind in (UP, DOWN):
-
-            @pl.when(along(kind, zz))
-            def _():
-                act(late_own(kind, 1 - d, block))
-
-        for kind in (ACROSS, CORE):
-            act(late_own(kind, 1 - d, block))
-
-    def fan_across(zz, act):
-        block = block_id(1 - y, c, zz)
-        act(early_own(CORE, block))
-        act(early_own(DP, block))
-        act(late_own(CORE, d, block))
-        act(late_own(CORE, 1 - d, block))
-
-    def fan_dp(zz, act):
-        act(early_other(block_id(y, c, zz)))
-        act(early_other(block_id(1 - y, c, zz)))
-
-    start = lambda copy: copy.start()
-    over_dp = late_copy(DP, mine, late_dp)
-    over_dp.start()
-    fan(z, start)
-
-    def arrive(step, carry):
-        @pl.when(step < 4)
-        def _():
-            zz = line_order(z, step)
-            block = block_id(y, c, zz)
-
-            @pl.when(step > 0)
-            def _():
-                early_own(ACROSS, block).wait_recv()
-                late_own(ACROSS, d, block).wait_recv()
-                fan(zz, start)
-
-            late_own(ACROSS, 1 - d, block).wait_recv()
-            fan_other(zz, start)
-
-        @pl.when(jnp.logical_and(step > 0, step < 5))
-        def _():
-            zz = line_order(z, jnp.maximum(step - 1, 0))
-            block = block_id(1 - y, c, zz)
-            early_own(CORE, block).wait_recv()
-            late_own(CORE, d, block).wait_recv()
-            late_own(CORE, 1 - d, block).wait_recv()
-            fan_across(zz, start)
-
-        @pl.when(step > 1)
-        def _():
-            zz = line_order(z, jnp.maximum(step - 2, 0))
-            early_other(block_id(y, c, zz)).wait_recv()
-            early_other(block_id(1 - y, c, zz)).wait_recv()
-            fan_dp(zz, start)
-
-        return carry
-
-    lax.fori_loop(0, 6, arrive, 0)
-
-    def finish(zz, carry):
-        for yy in range(2):
-            block = block_id(yy, 1 - c, zz)
-            early_own(CORE, block).wait_recv()
-            early_other(block).wait_recv()
-            late_own(CORE, d, block).wait_recv()
-            late_own(CORE, 1 - d, block).wait_recv()
-        return carry
-
-    lax.fori_loop(0, 4, finish, 0)
-    results = (
-        pltpu.make_async_copy(early, early_ref, local_sem.at[0]),
-        pltpu.make_async_copy(late, late_ref, local_sem.at[1]),
-    )
-    for copy in results:
-        copy.start()
-    end = lambda copy: copy.wait_send()
-    over_dp.wait_send()
-
-    def ends(zz, carry):
-        fan(zz, end)
-        fan_other(zz, end)
-        fan_across(zz, end)
-        fan_dp(zz, end)
-        return carry
-
-    lax.fori_loop(0, 4, ends, 0)
-    for copy in results:
-        copy.wait()
-
-
-def gather_weights(query, key, value, small, out):
-    bfloat = jnp.bfloat16
-    dma = pltpu.SemaphoreType.DMA
-    rows = query.shape[0]
-    early_width = query.shape[1] + key.shape[1] + value.shape[1] + small.shape[1]
-    anywhere = pl.BlockSpec(memory_space=pl.ANY)
-    early = (32, rows, early_width)
-    late = (32, rows, out.shape[1])
-    return pl.pallas_call(
-        gather_kernel,
-        out_shape=(jax.ShapeDtypeStruct(early, bfloat), jax.ShapeDtypeStruct(late, bfloat)),
-        in_specs=[anywhere] * 5,
-        out_specs=(anywhere, anywhere),
-        scratch_shapes=[
-            pltpu.VMEM(early, bfloat),
-            pltpu.VMEM(late, bfloat),
-            dma((5,)),
-            dma((5, 16)),
-            dma((16,)),
-            dma((32,)),
-            dma((4, 32)),
-            dma,
-            dma((32,)),
-        ],
-        compiler_params=pltpu.CompilerParams(
-            collective_id=0, has_side_effects=True, vmem_limit_bytes=40 * 2**20
-        ),
-        name="gather_weights",
-    )(query, key, value, small, out)
-
-
-def sums_kernel(
-    proj_ref,
-    small_ref,
-    out_ref,
-    gate_ref,
-    up_ref,
-    down_ref,
-    sum_ref,
-    gate_got,
-    up_got,
-    down_got,
-    parts,
-    core_got,
-    y_got,
-    z_got,
-    dp_got,
-    load_sem,
-    swap_send,
-    swap_recv,
-    core_send,
-    core_recv,
-    y_send,
-    y_recv,
-    z_send,
-    z_recv,
-    dp_send,
-    dp_recv,
-):
-    single = jnp.float32
-    bfloat = jnp.bfloat16
-    y, c, z, inner, device, per_side = place()
-    d = lax.axis_index("dp")
-    rows = proj_ref.shape[2]
-    loads = []
-    at = 0
-    for index, ref in enumerate((proj_ref, small_ref, out_ref)):
-        size = ref.shape[3]
-        for plane in range(2):
-            loads.append(
-                pltpu.make_async_copy(
-                    ref.at[plane],
-                    parts.at[:, pl.ds(plane * rows, rows), pl.ds(at, size)],
-                    load_sem.at[index * 2 + plane],
-                )
-            )
-        at += size
-    for copy in loads:
-        copy.start()
-    greet(per_side, device, 4 + inner, (DP,))
-
-    swaps = swap_copies(
-        (gate_ref, up_ref, down_ref), (gate_got, up_got, down_got), 1, device, swap_send, swap_recv
-    )
-    for copy in swaps:
-        copy.start()
-    for copy in loads:
-        copy.wait()
+    rows = parts.shape[1] // 2
+    mine = block_id(y, c, z)
 
     def remote(kind, source, target, send_sem, recv_sem):
         return pltpu.make_async_remote_copy(
@@ -424,17 +165,24 @@
         return remote(kind, parts.at[block_id(y, c, zz)], z_got.at[slot], z_send.at[zz], z_recv.at[slot])
 
     def add(block, got):
-        parts[block] = (parts[block].astype(single) + got.astype(single)).astype(bfloat)
-
-    def core_sends(step, carry):
-        zz = line_order(z, 3 - step)
-        to_core(1 - y, zz).start()
-        to_core(y, zz).start()
-        return carry
-
-    lax.fori_loop(0, 4, core_sends, 0)
-
-    def line_sum(step):
+        parts[block] = (parts[block].astype(single) + got.astype(single)).astype(parts.dtype)
+
+    def core_sends():
+        @pl.loop(0, 4)
+        def _(turn):
+            zz = line_order(z, 3 - turn)
+            to_core(1 - y, zz).start()
+            to_core(y, zz).start()
+
+    def across(step):
+        zz = line_order(z, step)
+        to_core(1 - y, zz).wait_recv()
+        add(block_id(1 - y, c, zz), core_got[(1 - y) * 4 + zz])
+        to_across(zz).start()
+        to_core(y, zz).wait_recv()
+        add(block_id(y, c, zz), core_got[y * 4 + zz])
+
+    def line(step):
         zz = line_order(z, step)
         block = block_id(y, c, zz)
         to_across(zz).wait_recv()
@@ -459,100 +207,451 @@
         def _():
             to_line(DOWN, zz, zz).start()
 
-    def stage(turn, carry):
-        @pl.when(turn < 4)
-        def _():
-            zz = line_order(z, 3 - jnp.minimum(turn, 3))
-            to_core(1 - y, zz).wait_recv()
-            add(block_id(1 - y, c, zz), core_got[(1 - y) * 4 + zz])
-            to_across(zz).start()
-            to_core(y, zz).wait_recv()
-            add(block_id(y, c, zz), core_got[y * 4 + zz])
-
-        @pl.when(jnp.logical_and(turn > 0, turn < 4))
-        def _():
-            line_sum(4 - jnp.maximum(turn, 1))
-
-        return carry
-
-    lax.fori_loop(0, 4, stage, 0)
-    mine = block_id(y, c, z)
-    to_across(z).wait_recv()
-    add(mine, y_got[z])
-
-    @pl.when(z > 0)
-    def _():
-        to_line(CORE, z, z).wait_recv()
-        add(mine, z_got[z])
-
-    @pl.when(z < 3)
-    def _():
-        to_line(CORE, z, 4).wait_recv()
-        add(mine, z_got[4])
-
     there = pl.ds(pl.multiple_of((1 - d) * rows, 16), rows)
     here = pl.ds(pl.multiple_of(d * rows, 16), rows)
     last = remote(DP, parts.at[mine, there, :], dp_got, dp_send, dp_recv)
-    last.start()
-    last.wait_recv()
-    sum_ref[...] = parts[mine, here, :].astype(single) + dp_got[...].astype(single)
-    last.wait_send()
+
+    def over_dp():
+        to_across(z).wait_recv()
+        add(mine, y_got[z])
+
+        @pl.when(z > 0)
+        def _():
+            to_line(CORE, z, z).wait_recv()
+            add(mine, z_got[z])
+
+        @pl.when(z < 3)
+        def _():
+            to_line(CORE, z, 4).wait_recv()
+            add(mine, z_got[4])
+
+        last.start()
+
+    def finish(result):
+        last.wait_recv()
+        result[...] = parts[mine, here, :].astype(single) + dp_got[...].astype(single)
+        last.wait_send()
+
+        @pl.loop(0, 4)
+        def _(zz):
+            to_core(y, zz).wait_send()
+            to_core(1 - y, zz).wait_send()
+            to_across(zz).wait_send()
+
+            @pl.when(zz != z)
+            def _():
+                to_line(CORE, zz, zz).wait_send()
+
+    return core_sends, across, line, over_dp, finish
+
+
+def ring_scratch(rows, width):
+    bfloat = jnp.bfloat16
+    dma = pltpu.SemaphoreType.DMA
+    return [
+        pltpu.VMEM((16, 2 * rows, width), bfloat),
+        pltpu.VMEM((8, 2 * rows, width), bfloat),
+        pltpu.VMEM((4, 2 * rows, width), bfloat),
+        pltpu.VMEM((5, 2 * rows, width), bfloat),
+        pltpu.VMEM((rows, width), bfloat),
+        dma((8,)),
+        dma((8,)),
+        dma((4,)),
+        dma((4,)),
+        dma((4,)),
+        dma((5,)),
+        dma,
+        dma,
+    ]
+
+
+def load_parts(refs, parts, sem):
+    loads = []
+    at = 0
+    for index, ref in enumerate(refs):
+        rows, size = ref.shape[2], ref.shape[3]
+        for plane in range(2):
+            loads.append(
+                pltpu.make_async_copy(
+                    ref.at[plane],
+                    parts.at[:, pl.ds(plane * rows, rows), pl.ds(at, size)],
+                    sem.at[index * 2 + plane],
+                )
+            )
+        at += size
+    return loads
+
+
+def gather_kernel(
+    query_ref,
+    key_ref,
+    value_ref,
+    small_ref,
+    out_ref,
+    proj_all,
+    small_all,
+    out_all,
+    whole,
+    local_sem,
+    send_sem,
+    core_sem,
+    recv_sem,
+):
+    y, c, z, inner, device, per_side = place()
+    d = lax.axis_index("dp")
+    mine = d * 16 + block_id(y, c, z)
+    loads = []
+    at = 0
+    for index, ref in enumerate((query_ref, key_ref, value_ref, small_ref, out_ref)):
+        size = ref.shape[1]
+        loads.append(
+            pltpu.make_async_copy(ref, whole.at[mine, :, pl.ds(at, size)], local_sem.at[index])
+        )
+        at += size
+    for copy in loads:
+        copy.start()
+    greet(per_side, device, 4 + inner, (DP,))
+    for copy in loads:
+        copy.wait()
+
+    def copy_of(kind, slot, sem):
+        return pltpu.make_async_remote_copy(
+            src_ref=whole.at[slot],
+            dst_ref=whole.at[slot],
+            send_sem=sem,
+            recv_sem=recv_sem.at[slot],
+            device_id=device(kind),
+            device_id_type=MESH_ID,
+        )
+
+    def own(kind, block):
+        return copy_of(kind, d * 16 + block, send_sem.at[kind, block])
+
+    def other(block):
+        return copy_of(CORE, (1 - d) * 16 + block, core_sem.at[block])
+
+    def along(kind, zz):
+        if kind == UP:
+            return jnp.logical_and(z < 3, zz <= z)
+        return jnp.logical_and(z > 0, zz >= z)
+
+    def fan(zz, act):
+        block = block_id(y, c, zz)
+        for kind in (UP, DOWN):
+
+            @pl.when(along(kind, zz))
+            def _():
+                act(own(kind, block))
+
+        for kind in (ACROSS, DP, CORE):
+            act(own(kind, block))
+
+    def fan_across(zz, act):
+        block = block_id(1 - y, c, zz)
+        act(own(DP, block))
+        act(own(CORE, block))
+
+    def fan_dp(zz, act):
+        act(other(block_id(y, c, zz)))
+        act(other(block_id(1 - y, c, zz)))
+
+    start = lambda copy: copy.start()
+    fan(z, start)
+
+    def arrive(step, carry):
+        @pl.when(jnp.logical_and(step > 0, step < 4))
+        def _():
+            zz = line_order(z, jnp.minimum(step, 3))
+            own(ACROSS, block_id(y, c, zz)).wait_recv()
+            fan(zz, start)
+
+        @pl.when(jnp.logical_and(step > 0, step < 5))
+        def _():
+            zz = line_order(z, jnp.maximum(step - 1, 0))
+            own(CORE, block_id(1 - y, c, zz)).wait_recv()
+            fan_across(zz, start)
+
+        @pl.when(step > 1)
+        def _():
+            zz = line_order(z, jnp.maximum(step - 2, 0))
+            other(block_id(y, c, zz)).wait_recv()
+            other(block_id(1 - y, c, zz)).wait_recv()
+            fan_dp(zz, start)
+
+        return carry
+
+    lax.fori_loop(0, 6, arrive, 0)
+
+    def finish(zz, carry):
+        for yy in range(2):
+            block = block_id(yy, 1 - c, zz)
+            own(CORE, block).wait_recv()
+            other(block).wait_recv()
+        return carry
+
+    lax.fori_loop(0, 4, finish, 0)
+    results = []
+    at = 0
+    for index, ref in enumerate((proj_all, small_all, out_all)):
+        size = ref.shape[2]
+        results.append(
+            pltpu.make_async_copy(whole.at[:, :, pl.ds(at, size)], ref, local_sem.at[index])
+        )
+        at += size
+    for copy in results:
+        copy.start()
+    end = lambda copy: copy.wait_send()
+
+    def ends(zz, carry):
+        fan(zz, end)
+        fan_across(zz, end)
+        fan_dp(zz, end)
+        return carry
+
+    lax.fori_loop(0, 4, ends, 0)
+    for copy in results:
+        copy.wait()
+
+
+def gather_weights(query, key, value, small, out):
+    bfloat = jnp.bfloat16
+    dma = pltpu.SemaphoreType.DMA
+    rows = query.shape[0]
+    widths = (query.shape[1] + key.shape[1] + value.shape[1], small.shape[1], out.shape[1])
+    anywhere = pl.BlockSpec(memory_space=pl.ANY)
+    return pl.pallas_call(
+        gather_kernel,
+        out_shape=tuple(jax.ShapeDtypeStruct((32, rows, width), bfloat) for width in widths),
+        in_specs=[anywhere] * 5,
+        out_specs=(anywhere, anywhere, anywhere),
+        scratch_shapes=[
+            pltpu.VMEM((32, rows, sum(widths)), bfloat),
+            dma((5,)),
+            dma((5, 16)),
+            dma((16,)),
+            dma((32,)),
+        ],
+        compiler_params=pltpu.CompilerParams(
+            collective_id=0, has_side_effects=True, vmem_limit_bytes=60 * 2**20
+        ),
+        name="gather_weights",
+    )(query, key, value, small, out)
+
+
+def ring_sum_dp_early(parts, core_got, dp_got, y_got, z_got, sems):
+    single = jnp.float32
+    core_send, core_recv, dp_send, dp_recv, y_send, y_recv, z_send, z_recv = sems
+    y, c, z, _, device, _ = place()
+    d = lax.axis_index("dp")
+    rows = parts.shape[1] // 2
+    mine = block_id(y, c, z)
+    there = pl.ds(pl.multiple_of((1 - d) * rows, 16), rows)
+    here = pl.ds(pl.multiple_of(d * rows, 16), rows)
+
+    def remote(kind, source, target, send_sem, recv_sem):
+        return pltpu.make_async_remote_copy(
+            src_ref=source,
+            dst_ref=target,
+            send_sem=send_sem,
+            recv_sem=recv_sem,
+            device_id=device(kind),
+            device_id_type=MESH_ID,
+        )
+
+    def to_core(yy, zz):
+        slot = yy * 4 + zz
+        return remote(
+            CORE, parts.at[block_id(yy, 1 - c, zz)], core_got.at[slot], core_send.at[slot], core_recv.at[slot]
+        )
+
+    def to_dp(yy, zz):
+        slot = yy * 4 + zz
+        return remote(
+            DP, parts.at[block_id(yy, c, zz), there, :], dp_got.at[slot], dp_send.at[slot], dp_recv.at[slot]
+        )
+
+    def to_across(zz):
+        return remote(
+            ACROSS, parts.at[block_id(1 - y, c, zz), here, :], y_got.at[zz], y_send.at[zz], y_recv.at[zz]
+        )
+
+    def to_line(kind, zz, slot):
+        return remote(
+            kind, parts.at[block_id(y, c, zz), here, :], z_got.at[slot], z_send.at[zz], z_recv.at[slot]
+        )
+
+    def add(block, got):
+        parts[block, here, :] = (
+            parts[block, here, :].astype(single) + got.astype(single)
+        ).astype(parts.dtype)
+
+    def core_sends():
+        @pl.loop(0, 4)
+        def _(turn):
+            zz = line_order(z, 3 - turn)
+            to_core(1 - y, zz).start()
+            to_core(y, zz).start()
+
+    def meet(step):
+        zz = line_order(z, step)
+        for yy in (1 - y, y):
+            block = block_id(yy, c, zz)
+            to_core(yy, zz).wait_recv()
+            parts[block] = (
+                parts[block].astype(single) + core_got[yy * 4 + zz].astype(single)
+            ).astype(parts.dtype)
+            to_dp(yy, zz).start()
+
+    def across(step):
+        zz = line_order(z, step)
+        for yy in (1 - y, y):
+            to_dp(yy, zz).wait_recv()
+            add(block_id(yy, c, zz), dp_got[yy * 4 + zz])
+        to_across(zz).start()
+
+    def line(step):
+        zz = line_order(z, step)
+        block = block_id(y, c, zz)
+        to_across(zz).wait_recv()
+        add(block, y_got[zz])
+        rising = zz > z
+        comes = jnp.logical_or(jnp.logical_and(rising, z > 0), jnp.logical_and(zz < z, z < 3))
+
+        @pl.when(comes)
+        def _():
+            to_line(CORE, zz, zz).wait_recv()
+            add(block, z_got[zz])
+
+        @pl.when(rising)
+        def _():
+            to_line(UP, zz, zz).start()
+
+        @pl.when(zz == z - 1)
+        def _():
+            to_line(DOWN, zz, 4).start()
+
+        @pl.when(zz < z - 1)
+        def _():
+            to_line(DOWN, zz, zz).start()
+
+    def finish(result):
+        to_across(z).wait_recv()
+        result[...] = parts[mine, here, :].astype(single) + y_got[z].astype(single)
+
+        @pl.when(z > 0)
+        def _():
+            to_line(CORE, z, z).wait_recv()
+            result[...] += z_got[z].astype(single)
+
+        @pl.when(z < 3)
+        def _():
+            to_line(CORE, z, 4).wait_recv()
+            result[...] += z_got[4].astype(single)
+
+        @pl.loop(0, 4)
+        def _(zz):
+            for yy in (y, 1 - y):
+                to_core(yy, zz).wait_send()
+                to_dp(yy, zz).wait_send()
+            to_across(zz).wait_send()
+
+            @pl.when(zz != z)
+            def _():
+                to_line(CORE, zz, zz).wait_send()
+
+    return core_sends, meet, across, line, finish
+
+
+def ring_scratch_dp_early(rows, width):
+    bfloat = jnp.bfloat16
+    dma = pltpu.SemaphoreType.DMA
+    return [
+        pltpu.VMEM((16, 2 * rows, width), bfloat),
+        pltpu.VMEM((8, 2 * rows, width), bfloat),
+        pltpu.VMEM((8, rows, width), bfloat),
+        pltpu.VMEM((4, rows, width), bfloat),
+        pltpu.VMEM((5, rows, width), bfloat),
+        *[dma((n,)) for n in (8, 8, 8, 8, 4, 4, 4, 5)],
+    ]
+
+
+def sums_kernel(
+    proj_ref, small_ref, out_ref, down_ref, sum_ref, out_sum, down_got, load_sem, swap_send, swap_recv, *rings
+):
+    _, _, _, inner, device, per_side = place()
+    ring, out_ring = rings[:13], rings[13:]
+    loads = load_parts((proj_ref, small_ref), ring[0], load_sem) + load_parts(
+        (out_ref,), out_ring[0], load_sem.at[pl.ds(4, 2)]
+    )
+    for copy in loads:
+        copy.start()
+    greet(per_side, device, 4 + inner, (DP,))
+    for copy in loads:
+        copy.wait()
+    core_sends, meet, across, line, finish = ring_sum_dp_early(*ring[:5], ring[5:])
+    out_core, out_across, out_line, out_dp, out_finish = ring_sum(*out_ring[:5], out_ring[5:])
+    core_sends()
+    out_core()
+
+    @pl.loop(0, 4)
+    def _(turn):
+        meet(3 - turn)
+        out_across(3 - turn)
+
+    swaps = swap_copies(((down_ref, 1, down_got),), device, swap_send, swap_recv)
+    for copy in swaps:
+        copy.start()
+
+    @pl.loop(0, 4)
+    def _(turn):
+        across(3 - turn)
+
+        @pl.when(turn < 3)
+        def _():
+            out_line(3 - jnp.minimum(turn, 2))
+
+        @pl.when(turn > 0)
+        def _():
+            line(4 - jnp.maximum(turn, 1))
+
+    out_dp()
+    finish(sum_ref)
+    out_finish(out_sum)
     for copy in swaps:
         copy.wait()
 
-    def ends(zz, carry):
-        to_core(y, zz).wait_send()
-        to_core(1 - y, zz).wait_send()
-        to_across(zz).wait_send()
-
-        @pl.when(zz != z)
-        def _():
-            to_line(CORE, zz, zz).wait_send()
-
-        return carry
-
-    lax.fori_loop(0, 4, ends, 0)
-
-
-def sum_gradients(proj, small, out, gate, up, down):
-    bfloat = jnp.bfloat16
+
+def by_device(x):
+    return x.reshape(2, 16, x.shape[0] // 32, x.shape[1])
+
+
+def sum_gradients(proj, small, out, down):
     dma = pltpu.SemaphoreType.DMA
+    anywhere = pl.BlockSpec(memory_space=pl.ANY)
+    vmem = pl.BlockSpec(memory_space=pltpu.VMEM)
     rows = proj.shape[0] // 32
-    parts = [x.reshape(2, 16, rows, x.shape[1]) for x in (proj, small, out)]
-    width = sum(x.shape[3] for x in parts)
-    anywhere = pl.BlockSpec(memory_space=pl.ANY)
-    halves = [(x.shape[1] // 2, x.shape[2]) for x in (gate, up, down)]
+    width = proj.shape[1] + small.shape[1]
     return pl.pallas_call(
         sums_kernel,
         out_shape=(
             jax.ShapeDtypeStruct((rows, width), jnp.float32),
-            *(jax.ShapeDtypeStruct(shape, bfloat) for shape in halves),
+            jax.ShapeDtypeStruct((rows, out.shape[1]), jnp.float32),
+            jax.ShapeDtypeStruct((down.shape[1] // 2, down.shape[2]), down.dtype),
         ),
-        in_specs=[anywhere] * 6,
-        out_specs=(pl.BlockSpec(memory_space=pltpu.VMEM), anywhere, anywhere, anywhere),
+        in_specs=[anywhere] * 4,
+        out_specs=(vmem, vmem, anywhere),
         scratch_shapes=[
-            pltpu.VMEM((16, 2 * rows, width), bfloat),
-            pltpu.VMEM((8, 2 * rows, width), bfloat),
-            pltpu.VMEM((4, 2 * rows, width), bfloat),
-            pltpu.VMEM((5, 2 * rows, width), bfloat),
-            pltpu.VMEM((rows, width), bfloat),
             dma((6,)),
-            dma((6,)),
-            dma((6,)),
-            dma((8,)),
-            dma((8,)),
-            dma((4,)),
-            dma((4,)),
-            dma((4,)),
-            dma((5,)),
-            dma,
-            dma,
+            dma((1,)),
+            dma((1,)),
+            *ring_scratch_dp_early(rows, width),
+            *ring_scratch(rows, out.shape[1]),
         ],
         compiler_params=pltpu.CompilerParams(
-            collective_id=2, has_side_effects=True, vmem_limit_bytes=40 * 2**20
+            collective_id=2, has_side_effects=True, vmem_limit_bytes=56 * 2**20
         ),
         name="sum_gradients",
-    )(*parts, gate, up, down)
+    )(by_device(proj), by_device(small), by_device(out), down)
 
 
 def fill_bias(length_ref, bias, ctx):
@@ -669,10 +768,12 @@
 
 def attend_back_kernel(swap, *refs):
     query_ref, pairs_ref, grad_ref, length_ref, *refs = refs
-    sources, refs = refs[:swap], refs[swap:]
+    if swap:
+        gate_ref, up_ref, down_ref, *refs = refs
     query_out, pairs_out, *refs = refs
-    targets, refs = refs[:swap], refs[swap:]
-    parts, core_got, y_got, bias, swap_send, swap_recv, core_send, core_recv, y_send, y_recv = refs
+    if swap:
+        down_got, gate_got, up_got, *refs = refs
+    parts, core_got, y_got, bias, core_send, core_recv, y_send, y_recv, *refs = refs
     bfloat = jnp.bfloat16
     single = jnp.float32
     y, c, _, _, device, _ = place()
@@ -682,9 +783,17 @@
     for kind in kinds:
         pl.semaphore_signal(barrier, inc=1, device_id=device(kind), device_id_type=MESH_ID)
     pl.semaphore_wait(barrier, len(kinds))
-    swaps = swap_copies(sources, targets, 0, device, swap_send, swap_recv)
-    for copy in swaps:
-        copy.start()
+    swaps = []
+    if swap:
+        swap_send, swap_recv = refs
+        swaps = swap_copies(
+            ((down_ref, 0, down_got), (gate_ref, 1, gate_got), (up_ref, 1, up_got)),
+            device,
+            swap_send,
+            swap_recv,
+        )
+        for copy in swaps:
+            copy.start()
     fill_bias(length_ref, bias, mine)
     blocks = pairs_ref.shape[0]
     half = pairs_ref.shape[1] // 2
@@ -800,40 +909,48 @@
     dma = pltpu.SemaphoreType.DMA
     anywhere = pl.BlockSpec(memory_space=pl.ANY)
     vmem = pl.BlockSpec(memory_space=pltpu.VMEM)
-    swap = len(expert_grads)
+    swap = bool(expert_grads)
     blocks, rows, keys = pairs.shape
     turns = 2
     part = (turns, rows // turns, keys)
-    halves = [(x.shape[1] // 2, x.shape[2]) for x in expert_grads]
+    more_in, more_out, more_scratch, more_specs = [], [], [], []
+    if swap:
+        gate, up, down = expert_grads
+        more_in = [gate, up, down]
+        more_out = [
+            jax.ShapeDtypeStruct((x.shape[1] // 2, x.shape[2]), bfloat) for x in (down, gate, up)
+        ]
+        more_specs = [anywhere] * 3
+        more_scratch = [dma((3,)), dma((3,))]
     return pl.pallas_call(
         functools.partial(attend_back_kernel, swap),
         out_shape=(
             jax.ShapeDtypeStruct(query.shape, single),
             jax.ShapeDtypeStruct(part, single),
-            *(jax.ShapeDtypeStruct(shape, bfloat) for shape in halves),
+            *more_out,
         ),
-        in_specs=[vmem, vmem, vmem, pl.BlockSpec(memory_space=pltpu.SMEM)] + [anywhere] * swap,
-        out_specs=(vmem, vmem, *([anywhere] * swap)),
+        in_specs=[vmem, vmem, vmem, pl.BlockSpec(memory_space=pltpu.SMEM)] + [anywhere] * len(more_in),
+        out_specs=(vmem, vmem, *more_specs),
         scratch_shapes=[
             pltpu.VMEM((blocks, *part), bfloat),
             pltpu.VMEM((turns, 2, *part[1:]), bfloat),
             pltpu.VMEM(part, bfloat),
             pltpu.VMEM((blocks, keys, query.shape[1]), single),
-            dma((3,)),
-            dma((3,)),
             dma((turns, 2)),
             dma((turns, 2)),
             dma((turns,)),
             dma((turns,)),
+            *more_scratch,
         ],
         compiler_params=pltpu.CompilerParams(
             collective_id=4, has_side_effects=True, vmem_limit_bytes=48 * 2**20
         ),
         name="attend_back",
-    )(query, pairs, grad, lengths, *expert_grads)
+    )(query, pairs, grad, lengths, *more_in)
 
 
 def experts_kernel(
+    swap,
     hidden_ref,
     final_ref,
     routes_ref,
@@ -843,10 +960,51 @@
     down_hbm,
     back_ref,
     part_ref,
-    score_ref,
+    score_got,
     grad_gate_ref,
     grad_up_ref,
     grad_down_ref,
+    *refs,
+):
+    gate_got, up_got, *refs = refs if swap else (None, None, *refs)
+    experts_steps(
+        swap,
+        hidden_ref,
+        final_ref,
+        routes_ref,
+        router_ref,
+        gate_hbm,
+        up_hbm,
+        down_hbm,
+        back_ref,
+        part_ref,
+        score_got,
+        grad_gate_ref,
+        grad_up_ref,
+        grad_down_ref,
+        gate_got,
+        up_got,
+        *refs,
+    )
+
+
+def experts_steps(
+    swap,
+    hidden_ref,
+    final_ref,
+    routes_ref,
+    router_ref,
+    gate_hbm,
+    up_hbm,
+    down_hbm,
+    back_ref,
+    part_ref,
+    score_got,
+    grad_gate_ref,
+    grad_up_ref,
+    grad_down_ref,
+    gate_got,
+    up_got,
     held,
     w_gate,
     w_up,
@@ -871,6 +1029,11 @@
     y_recv,
     z_recv,
     ready,
+    score_ref,
+    score_send,
+    score_recv,
+    swap_send,
+    swap_recv,
 ):
     single = jnp.float32
     bfloat = jnp.bfloat16
@@ -882,34 +1045,7 @@
     capacity = picks.shape[1] // local_exp
     group_rows = 4 * capacity
     ctx = lax.axis_index("context")
-    z = lax.axis_index("expert")
-    y = ctx // 2
-    c = ctx % 2
-    inner = z + (z // 2) * (3 - 2 * z)
-
-    def device(kind):
-        if kind == UP:
-            return {"context": ctx, "expert": z + 1}
-        if kind == DOWN:
-            return {"context": ctx, "expert": z - 1}
-        if kind == ACROSS:
-            return {"context": (1 - y) * 2 + c, "expert": z}
-        return {"context": y * 2 + 1 - c, "expert": z}
-
-    def block_id(yy, cc, zz):
-        return (yy * 2 + cc) * 4 + zz
-
-    def per_side(action):
-        @pl.when(z < 3)
-        def _():
-            action(UP)
-
-        @pl.when(z > 0)
-        def _():
-            action(DOWN)
-
-        action(ACROSS)
-        action(CORE)
+    y, c, z, inner, device, per_side = place()
 
     weights = (
         pltpu.make_async_copy(gate_hbm, w_gate, load_sem.at[0]),
@@ -923,12 +1059,22 @@
         copy.start()
 
     barrier = pltpu.get_barrier_semaphore()
-    per_side(
-        lambda kind: pl.semaphore_signal(
-            barrier, inc=1, device_id=device(kind), device_id_type=MESH_ID
-        )
-    )
-    pl.semaphore_wait(barrier, 3 + inner)
+
+    def member_device(block):
+        return {"context": block // 4, "expert": block % 4}
+
+    @pl.loop(1, 16)
+    def _(shift):
+        pl.semaphore_signal(
+            barrier,
+            inc=1,
+            device_id=member_device((mine + shift) % 16),
+            device_id_type=MESH_ID,
+        )
+
+    if swap:
+        pl.semaphore_signal(barrier, inc=1, device_id=device(DP), device_id_type=MESH_ID)
+    pl.semaphore_wait(barrier, 16 if swap else 15)
     own.wait()
 
     def spread(kind, block):
@@ -1100,6 +1246,22 @@
 
     lax.fori_loop(0, 4, forward_group, 0)
 
+    def score_copy(block, source):
+        return pltpu.make_async_remote_copy(
+            src_ref=score_ref.at[block],
+            dst_ref=score_got.at[source],
+            send_sem=score_send.at[block],
+            recv_sem=score_recv.at[source],
+            device_id=member_device(block),
+            device_id_type=MESH_ID,
+        )
+
+    @pl.loop(1, 16)
+    def _(shift):
+        score_copy((mine + shift) % 16, mine).start()
+
+    score_got[mine] = score_ref[mine]
+
     @pl.loop(0, 4)
     def _(p):
         store_part(line_order(z, 3), p).wait()
@@ -1292,6 +1454,13 @@
             copy.start()
 
     weight_grads(0)
+    swaps = []
+    if swap:
+        swaps = swap_copies(
+            ((w_gate, 0, gate_got), (w_up, 0, up_got)), device, swap_send, swap_recv
+        )
+        for copy in swaps:
+            copy.start()
     line_sum(1)
     weight_grads(1)
     to_across(0, z).wait_recv()
@@ -1316,10 +1485,21 @@
         to_core(p, z).wait_send()
         to_across(p, z).wait_send()
     to_line(CORE, 1, z, False).wait_send()
+
+    @pl.loop(1, 16)
+    def _(shift):
+        other = (mine + shift) % 16
+        score_copy(other, mine).wait_send()
+        score_copy(other, other).wait_recv()
+
+    for copy in swaps:
+        copy.wait()
     result.wait()
 
 
-def experts_on_owner(hidden, final_all, routes_all, router_rows, w_gate, w_up, w_down, capacity):
+def experts_on_owner(
+    hidden, final_all, routes_all, router_rows, w_gate, w_up, w_down, capacity, swap
+):
     blocks = final_all.shape[0]
     tokens_block, width = hidden.shape
     local_exp, _, units = w_gate.shape
@@ -1330,7 +1510,7 @@
     vmem = pl.BlockSpec(memory_space=pltpu.VMEM)
     dma = pltpu.SemaphoreType.DMA
     return pl.pallas_call(
-        experts_kernel,
+        functools.partial(experts_kernel, swap),
         out_shape=(
             jax.ShapeDtypeStruct((tokens_block, width), bfloat),
             jax.ShapeDtypeStruct((blocks, tokens_block, width), bfloat),
@@ -1338,9 +1518,10 @@
             jax.ShapeDtypeStruct(w_gate.shape, bfloat),
             jax.ShapeDtypeStruct(w_up.shape, bfloat),
             jax.ShapeDtypeStruct(w_down.shape, bfloat),
+            *([jax.ShapeDtypeStruct((width // 2, units), bfloat)] * (2 if swap else 0)),
         ),
         in_specs=[anywhere, anywhere, vmem, vmem, anywhere, anywhere, anywhere],
-        out_specs=(anywhere, anywhere, vmem, anywhere, anywhere, anywhere),
+        out_specs=(anywhere, anywhere, vmem, *([anywhere] * (5 if swap else 3))),
         scratch_shapes=[
             pltpu.VMEM((blocks, tokens_block, width), bfloat),
             pltpu.VMEM(w_gate.shape, bfloat),
@@ -1366,6 +1547,11 @@
             dma((4,)),
             dma((5,)),
             pltpu.SemaphoreType.REGULAR((4,)),
+            pltpu.VMEM((blocks, 8, tokens_block), single),
+            dma((16,)),
+            dma((16,)),
+            dma((2,)),
+            dma((2,)),
         ],
         compiler_params=pltpu.CompilerParams(
             collective_id=1, has_side_effects=True, vmem_limit_bytes=63 * 2**20
@@ -1413,34 +1599,31 @@
         axis=1,
     )
     if pair:
-        packed = routes.reshape(-1, 64).astype(bfloat)
+        packed = routes[0].T.reshape(-1, 64).astype(bfloat)
         packed = jnp.pad(packed, ((0, own_rows - packed.shape[0]), (0, 0)))
-        early, late = gather_weights(
+        early, small_all, late = gather_weights(
             w_query, key_weight, value_weight, jnp.concatenate([small, packed], axis=1), w_out
         )
         routes_all = lax.dynamic_slice(
-            early,
-            (lax.axis_index("dp") * 16, 0, proj_width + 64),
-            (16, tokens_own * TOP // 64, 64),
-        )
-        routes_all = routes_all.astype(jnp.int32).reshape(16, tokens_own, TOP)
-        routes_all = routes_all.swapaxes(1, 2)
-        early = early.reshape(-1, early.shape[2])
+            small_all, (lax.axis_index("dp") * 16, 0, 64), (16, tokens_own * TOP // 64, 64)
+        )
+        routes_all = routes_all.astype(jnp.int32).reshape(16, TOP, tokens_own)
+        proj_w = early.reshape(-1, proj_width)
+        small_all = small_all.reshape(-1, small_all.shape[2])
         out_w = late.reshape(-1, late.shape[2])
     else:
-        early = jnp.concatenate([w_query, key_weight, value_weight, small], axis=1)
-        early = lax.all_gather(early, EVERY, axis=0, tiled=True)
+        proj_w = jnp.concatenate([w_query, key_weight, value_weight], axis=1)
+        proj_w = lax.all_gather(proj_w, EVERY, axis=0, tiled=True)
+        small_all = lax.all_gather(small, EVERY, axis=0, tiled=True)
         out_w = lax.all_gather(w_out, EVERY, axis=0, tiled=True)
         routes_all = lax.all_gather(routes[0].T, GROUP, axis=0, tiled=False)
     positions = lax.axis_index("context") * tokens_own + jnp.arange(tokens_own, dtype=jnp.int32)
     valid = (positions < lengths[0]).astype(single)[:, None]
     grad_final = cotangent[0].astype(single) * valid
-    final_low, early = lax.optimization_barrier((grad_final.astype(bfloat), early))
-    final_all = lax.all_gather(final_low, GROUP, axis=0, tiled=False)
-    proj_w = early[:, :proj_width]
-    router_w = early[:, proj_width : proj_width + experts]
-    gain_one = early[:, proj_width + experts].astype(single)
-    gain_two = early[:, proj_width + experts + 1].astype(single)
+    final_all = lax.all_gather(grad_final.astype(bfloat), GROUP, axis=0, tiled=False)
+    router_w = small_all[:, :experts]
+    gain_one = small_all[:, experts].astype(single)
+    gain_two = small_all[:, experts + 1].astype(single)
     cosine, sine = rotation_tables(positions)
 
     inputs = tokens[0].astype(single)
@@ -1459,11 +1642,12 @@
     normed_two = resid * inverse_two
     hidden_two = (normed_two * gain_two).astype(bfloat)
 
-    grad_hidden, combined, scores, grad_w_gate, grad_w_up, grad_w_down = experts_on_owner(
-        hidden_two, final_all, routes_all, router_w.T, w_gate, w_up, w_down, capacity
+    grad_hidden, combined, scores, *expert_grads = experts_on_owner(
+        hidden_two, final_all, routes_all, router_w.T, w_gate, w_up, w_down, capacity, pair
     )
+    expert_grads, got = expert_grads[:3], expert_grads[3:]
     combined = lax.psum_scatter(combined, GROUP, scatter_dimension=0, tiled=False)
-    scores = lax.all_to_all(scores[:, :local_exp], GROUP, split_axis=0, concat_axis=0, tiled=True)
+    scores = scores[:, :local_exp]
     grad_gates = scores.reshape(experts, tokens_own).T
 
     routed = jnp.any(routes[0][:, :, None] == jnp.arange(experts, dtype=jnp.int32), axis=1)
@@ -1482,9 +1666,13 @@
 
     grad_out_w = jnp.einsum("es,sd->ed", mixed, grad_attn, preferred_element_type=single)
     grad_mixed = jnp.einsum("ed,sd->es", out_w, grad_attn, preferred_element_type=single)
-    expert_grads = (grad_w_gate, grad_w_up, grad_w_down)
-    grad_query, grad_pairs, *first_got = attend_back(
-        query, pairs, grad_mixed.astype(bfloat), lengths, expert_grads if pair else ()
+    grad_out_w = grad_out_w.astype(bfloat)
+    grad_query, grad_pairs, *more = attend_back(
+        query,
+        pairs,
+        grad_mixed.astype(bfloat),
+        lengths,
+        expert_grads if pair else (),
     )
     grad_pairs = grad_pairs.reshape(2, 2, key_width // 2, tokens_own)
     grad_key = grad_pairs[:, 0].reshape(key_width, tokens_own)
@@ -1512,9 +1700,11 @@
         axis=1,
     ).astype(bfloat)
     grad_proj_w = grad_proj_w.astype(bfloat)
-    grad_out_w = grad_out_w.astype(bfloat)
     if pair:
-        summed, *last_got = sum_gradients(grad_proj_w, grad_small, grad_out_w, *expert_grads)
+        down_first, gate_last, up_last = more
+        summed, out_sum, down_last = sum_gradients(
+            grad_proj_w, grad_small, grad_out_w, expert_grads[2]
+        )
 
         def both(whole, *others):
             half = whole.shape[1] // 2
@@ -1522,7 +1712,10 @@
             return own.astype(single) + jnp.stack(others).astype(single)
 
         expert_sums = tuple(
-            both(whole, *others) for whole, *others in zip(expert_grads, first_got, last_got)
+            both(whole, *others)
+            for whole, *others in zip(
+                expert_grads, (*got, down_first), (gate_last, up_last, down_last)
+            )
         )
     else:
         summed = lax.psum_scatter(
@@ -1531,6 +1724,7 @@
             scatter_dimension=0,
             tiled=True,
         ).astype(single)
+        out_sum = summed[:, proj_width + 128 :]
         expert_sums = tuple(
             lax.psum_scatter(x, "dp", scatter_dimension=1, tiled=True).astype(single)
             for x in expert_grads
@@ -1544,7 +1738,7 @@
         summed[:, :query_width],
         summed[:, query_width : query_width + key_width],
         summed[:, query_width + key_width : proj_width],
-        summed[:, proj_width + 128 :],
+        out_sum,
         summed[:, proj_width + experts + 1],
         summed[:, proj_width : proj_width + experts],
         *expert_sums,

time: 612 us -> 577 us (0.943)
  waiting for transfers between devices: 45.3 us -> 0.04 us
  Pallas kernels: 445 us -> 477 us
  local copies, waits for them, and re-layouts: 37.7 us -> 16.7 us
    all_gather x1, waiting for transfers between devices: 38.8 us -> 0.01 us  [on_device(): lax.all_gather(grad_final.astype(bfloat), GROUP, axis=0, tiled=False)]
    pallas_call x2, Pallas kernels: 260 us -> 290 us  [the longest x1 194 us: experts_on_owner(): pl.pallas_call(functools.partial(experts_kernel, swap), out_shape=(jax.Sh...]
    optimization_barrier x1 -> x0, local copies, waits for them, and re-layouts: 11.9 us -> none  [on_device(): lax.optimization_barrier((grad_final.astype(bfloat), early))]
    all_to_all x1 -> x0, waiting for transfers between devices: 6.47 us -> none  [on_device(): lax.all_to_all(scores[:, :local_exp], GROUP, split_axis=0, concat_axis=0,...]
  transfers between devices with their start and end apart: 3 -> 2, of which waited for: 2 -> 0; matrix products, arithmetic and copies ran while one was open for 12% -> 11% of each run, Pallas kernels for 31% -> 50%
where the time goes in v4:
time: 577 us; the launch traced here: 567 us
  Pallas kernels  477 us (83%)
  matrix products  33.3 us (6%)
  other arithmetic  24.2 us (4%)
  local copies, waits for them, and re-layouts  16.7 us (3%)
  between operations  15.6 us (3%)
    pallas_call x1, Pallas kernels, experts_on_owner(): pl.pallas_call(functools.partial(experts_kernel, swap), out_shape=(jax.Sh...  194 us
    pallas_call x1, Pallas kernels, gather_weights(): pl.pallas_call(gather_kernel, out_shape=tuple((jax.ShapeDtypeStruct((32,...  95.9 us
    pallas_call x1, Pallas kernels, sum_gradients(): pl.pallas_call(sums_kernel, out_shape=(jax.ShapeDtypeStruct((rows, width)...  93.6 us
    pallas_call x1, Pallas kernels, attend_back(): pl.pallas_call(functools.partial(attend_back_kernel, swap), out_shape=(ja...  62.2 us
    pallas_call x1, Pallas kernels, attend(): pl.pallas_call(attend_kernel, out_shape=(jax.ShapeDtypeStruct(query.shape...  31.8 us
  transfers between devices with their start and end apart: 2, of which 0 were waited for; matrix products, arithmetic and copies ran while one was open for 11% of the time, Pallas kernels for 50%

profile of v4, /device:TPU:0, one launch (start us, length us, event | category | flops | bytes accessed | tf_op | source)
XLA Modules:
  0.0 567.4 jit_solution(170863348138770978)
XLA Ops:
  8.0 2.3 fusion.6
  10.8 0.7 concatenate.21.small_ref
  11.5 95.9 %gather_weights.1 = (bf16[32,48,2560]{2,1,0:T(8,128)(2,1)}, bf16[32,48,128]{2,1,0:T(8,128)(2,1)}, bf16[32,48,1536]{2,1,0:T(8,128)(2,1)}) custom-call(bf16[48,1536]{1,0:T(8,128)(2,1)} %query_ref.1, bf16[48,512]{1,0:T(8,128)(2,1)} %key_ref.1, bf16[48,512]{1,0:T(8,128)(2,1)} %value_ref.1, bf16[48,128]{1,0:T(8,128)(2,1)} %concatenate.21.small_ref, ...), custom_call_target="tpu_custom_call" | custom-call | tf_op jit(solution)/shard_map/gather_weights/pallas_call | solution.py:422
  107.3 1.7 convert_reduce_fusion
  109.0 0.2 fusion.16
  109.3 0.6 copy-done.34
  109.8 6.4 %fusion.23 = f32[2560,256]{1,0:T(8,128)S(1)} fusion(bf16[1536,2560]{1,0:T(8,128)(2,1)} %bitcast.133, bf16[1,256,1536]{2,1,0:T(8,128)(2,1)S(1)} %copy-done.9, f32[1536]{0:T(1024)S(1)} %get-tuple-element.125, f32[256]{0:T(256)S(1)} %add_rsqrt_fusion.1), kind=kOutput, calls=%fused_computation.47 | convolution fusion | flops 2014838784 | bytes 11279360 | tf_op jit(solution)/shard_map/de,sd->es/dot_general | solution.py:1633
  116.2 0.1 slice.96
  116.4 0.8 copy-done.15
  117.3 0.8 reshape.265.routes_ref
  118.1 0.8 copy.68
  118.9 0.8 fusion.38
  119.7 0.3 add_convert_fusion
  120.1 0.3 copy-done.28
  120.6 31.8 %attend.1 = (bf16[1536,256]{1,0:T(8,128)(2,1)S(1)}, bf16[4,1024,256]{2,1,0:T(8,128)(2,1)S(1)}) custom-call(bf16[1536,256]{1,0:T(8,128)(2,1)S(1)} %bitcast.97, bf16[1024,256]{1,0:T(8,128)(2,1)S(1)} %pad_maximum_fusion.4.own_ref, s32[1]{0:T(128)} %copy.70.length_ref.refs_3_), custom_call_target="tpu_custom_call" | custom-call | tf_op jit(solution)/shard_map/attend/pallas_call | solution.py:747
  152.4 1.5 multiply_reduce_fusion.2
  154.0 1.1 copy-done.3
  155.1 1.1 multiply_convert_fusion.1.hidden_ref
  156.2 194.0 %experts.1 = (bf16[256,1536]{1,0:T(8,128)(2,1)}, bf16[16,256,1536]{2,1,0:T(8,128)(2,1)}, f32[16,8,256]{2,1,0:T(8,128)}, bf16[2,1536,512]{2,1,0:T(8,128)(2,1)}, b...) custom-call(bf16[256,1536]{1,0:T(8,128)(2,1)} %multiply_convert_fusi, ...), custom_call_target="tpu_custom_call" | custom-call | tf_op jit(solution)/shard_map/experts/pallas_call | solution.py:1512
  350.3 0.6 copy-done.33
  350.9 0.4 copy-done.14
  351.3 1.4 fusion.45
  352.7 0.9 slice.82
  353.8 2.0 multiply_reduce_fusion
  355.8 0.5 fusion.8
  356.4 4.3 convolution_convert_fusion.2.refs_2_
  360.7 62.2 %attend_back.1 = (f32[1536,256]{1,0:T(8,128)}, f32[2,512,256]{2,1,0:T(8,128)S(1)}, bf16[256,1536]{1,0:T(8,128)(2,1)S(1)}, bf16[768,512]{1,0:T(8,128)(2,1)S(1)}, bf16[768,512]{1,0:T(8,128)(2,1)S(1)}) custom-call(bf16[1536,256]{1,0:T(8,128)(2,1)S(1)} %bitcast.98, bf16[4,1024,256]{2,1,0:T(8,128)(2,1)} %copy-done.2, ...), custom_call_target="tpu_custom_call" | custom-call | tf_op jit(solution)/shard_map/attend_back/pallas_call | solution.py:925
  423.0 0.7 slice.140
  423.7 0.8 slice.106
  424.5 1.5 concatenate.29
  426.0 1.1 subtract_convert_fusion.2
  427.2 1.7 subtract_convert_fusion.1
  429.0 7.3 %fusion.11 = (f32[256]{0:T(256)S(1)}, bf16[1536]{0:T(1024)(128)(2,1)S(1)}, f32[256,1536]{1,0:T(8,128)}) fusion(bf16[1,256,1536]{2,1,0:T(8,128)(2,1)S(1)} %copy-done.11, f32[1536]{0:T(1024)S(1)} %get-tuple-element.125, f32[256]{0:T(256)S(1)} %copy-done.35, bf16[1536,2560]{1,0:T(8,128)(2,1)} %bitcast.134, bf16[512,256]{1,0:T(8,128)(2,1)S(1)} %bitcast.120, ...), kind=kOutput, calls=%fused_computation.24 | convolution fusion | flops 2019948800 | bytes 11545600 | tf_op jit(solution)/shard_map/es,de->sd/dot_general | solution.py:1689
  436.3 1.5 concatenate.28
  437.8 1.4 convolution_convert_fusion.3
  439.2 0.9 copy.64
  440.1 2.5 maximum_maximum_fusion.small_ref
  442.7 3.5 convolution_convert_fusion.1
  446.2 5.5 convolution_convert_fusion
  451.7 93.6 %sum_gradients.1 = (f32[48,2688]{1,0:T(8,128)}, f32[48,1536]{1,0:T(8,128)}, bf16[256,1536]{1,0:T(8,128)(2,1)}) custom-call(bf16[2,16,48,2560]{3,2,1,0:T(8,128)(2,1)} %bitcast.104, bf16[2,16,48,128]{3,2,1,0:T(8,128)(2,1)} %maximum_maximum_fusion.small_ref, bf16[2,16,48,1536]{3,2,1,0:T(8,128)(2,1)} %bitcast.105, ...), custom_call_target="tpu_custom_call" | custom-call | tf_op jit(solution)/shard_map/sum_gradients/pallas_call | solution.py:634
  545.4 5.2 convert_add_fusion.1
  550.6 2.1 convert_add_fusion
  552.8 0.7 slice_reduce_fusion
  553.5 0.7 slice.90
  554.2 0.7 fusion.44
  554.9 0.7 copy.67
  555.6 4.0 fusion.15
  559.6 0.7 copy.71
  (116 shorter events, 1.4 us)
Async XLA Ops:
  7.2 3.1 copy-start.38
  7.2 3.2 copy-start.39
  7.2 3.3 copy-start.40
  7.2 3.4 copy-start.32
  7.2 148.9 %all-gather.2.cloned.1.call-start = ((), (), s32[]{:S(2)}) async-start(), calls=%async_computation.1 | async-start | bytes 13369344 | tf_op jit(solution)/shard_map/all_gather | solution.py:1623
  7.9 2.3 copy-start.36
  7.9 101.1 %copy-start.9 = (bf16[1,256,1536]{2,1,0:T(8,128)(2,1)S(1)}, bf16[1,256,1536]{2,1,0:T(8,128)(2,1)}, u32[]{:S(2)}) copy-start(bf16[1,256,1536]{2,1,0:T(8,128)(2,1)} %param.14) | copy-start | bytes 2359300
  10.3 542.5 %reduce-scatter.2.cloned.1.call-start = ((), (), s32[]{:S(2)}) async-start(), calls=%async_computation.2 | async-start | bytes 13369344 | tf_op jit(solution)/shard_map/reduce_scatter | solution.py:1649
  109.3 0.6 copy-start.34
  116.2 1.0 copy-start.15
  116.2 36.2 %slice-start = ((s8[4718592]{0:T(1024)(128)(4,1)}), s8[524288]{0:T(1024)(128)(4,1)S(1)}, s32[]{:S(2)}) async-start(s8[4718592]{0:T(1024)(128)(4,1)} %bitcast.107), calls=%async_computation.3 | async-start | bytes 1048576
  119.7 0.6 copy-start.28
  119.7 32.7 %slice-start.1 = ((s8[4718592]{0:T(1024)(128)(4,1)}), s8[4194304]{0:T(1024)(128)(4,1)S(1)}, s32[]{:S(2)}) async-start(s8[4718592]{0:T(1024)(128)(4,1)} %bitcast.107), calls=%async_computation.4 | async-start | bytes 8388608
  120.4 32.0 %copy-start.10 = (bf16[1,256,1536]{2,1,0:T(8,128)(2,1)S(1)}, bf16[1,256,1536]{2,1,0:T(8,128)(2,1)}, u32[]{:S(2)}) copy-start(bf16[1,256,1536]{2,1,0:T(8,128)(2,1)} %param.14) | copy-start | bytes 2359300
  120.5 33.4 %copy-start = (bf16[24,2,32,256]{3,2,1,0:T(8,128)(2,1)}, bf16[24,2,32,256]{3,2,1,0:T(8,128)(2,1)S(1)}, u32[]{:S(2)}) copy-start(bf16[24,2,32,256]{3,2,1,0:T(8,128)(2,1)S(1)} %fusion.20) | copy-start | bytes 2359300
  152.4 1.5 copy-start.2
  153.9 1.1 copy-start.3
  350.2 0.7 copy-start.33
  350.2 1.1 copy-start.14
  350.2 3.5 copy-start.4
  353.7 2.1 copy-start.19
  353.8 2.1 copy-start.37
  356.3 4.4 copy-start.7
  356.3 4.4 copy-start.1
  422.9 3.0 copy-start.29
  422.9 3.0 copy-start.30
  427.1 1.9 copy-start.22
  427.1 1.9 copy-start.11
  427.1 1.9 copy-start.20
  427.2 1.9 copy-start.35
  429.0 7.3 %copy-start.17 = (bf16[24,2,32,256]{3,2,1,0:T(8,128)(2,1)}, bf16[24,2,32,256]{3,2,1,0:T(8,128)(2,1)S(1)}, u32[]{:S(2)}) copy-start(bf16[24,2,32,256]{3,2,1,0:T(8,128)(2,1)S(1)} %pad_maximum_fusion.1) | copy-start | bytes 2359300
  440.1 2.5 copy-start.8
  442.6 3.6 copy-start.12
  442.6 3.6 copy-start.18
  442.6 3.6 copy-start.21
  442.6 3.6 copy-start.23
  451.7 93.6 %copy-start.16 = (bf16[2,1536,512]{2,1,0:T(8,128)(2,1)S(1)}, bf16[2,1536,512]{2,1,0:T(8,128)(2,1)}, u32[]{:S(2)}) copy-start(bf16[2,1536,512]{2,1,0:T(8,128)(2,1)} %get-tuple-element.43.refs_4_) | copy-start | bytes 9437188
  451.7 93.6 %copy-start.24 = (bf16[768,512]{1,0:T(8,128)(2,1)S(1)}, bf16[768,512]{1,0:T(8,128)(2,1)}, u32[]{:S(2)}) copy-start(bf16[768,512]{1,0:T(8,128)(2,1)} %get-tuple-element.52) | copy-start | bytes 2359300
  451.7 93.6 %copy-start.25 = (bf16[768,512]{1,0:T(8,128)(2,1)S(1)}, bf16[768,512]{1,0:T(8,128)(2,1)}, u32[]{:S(2)}) copy-start(bf16[768,512]{1,0:T(8,128)(2,1)} %get-tuple-element.54) | copy-start | bytes 2359300
  545.4 5.2 copy-start.6
  545.4 5.2 copy-start.26
  550.6 2.1 copy-start.27
  550.6 5.0 copy-start.5
  552.8 2.8 copy-start.13
  555.6 4.1 copy-start.31
Sparse Core Ops, SparseCore 0:
  10.9 116.3 all-gather.1
  350.3 165.4 reduce-scatter.1
